TPU v7x, 32 devices: a whole 2x2x4 slice. The times are simulated.
32 devices in a mesh: parts: 2 (over x), tm: 16 (over z, y, core).
Axes of the slice: x: 2, y: 2, z: 4, core: 2. Of those that a mesh axis runs over, the one named last changes fastest.
Arguments:
- initial: float32 [16, 6, 16, 2048], P('tm', 'parts'), parts along dimension 1, may hold values from -0.6 to 0.6
- velocity: float32 [128, 4, 16, 2048], P('tm', 'parts'), parts along dimension 1, may hold values from -3 to 3
- forcing: float32 [128, 32, 2048], P('tm', 'parts'), parts along dimension 1, may hold values from -0.3 to 0.3
- depth_table: float32 [16], replicated, may hold values from 0.3 to 1.2
- levels: int32 [32, 2048], P('parts'), parts along dimension 0, may hold values from 0 to 15
- wet_mask: int32 [32, 2048], P('parts'), parts along dimension 0, may hold values 0 or 1
Outputs:
- corrected: float32 [16, 6, 16, 2048], P('tm', 'parts'), parts along dimension 1
- gradient: float32 [32, 2048], P('parts'), parts along dimension 0
There are 2 independent parts, one for each index of `parts`. A program takes and returns all parts, laid end to end along the dimension named above; an argument that names none is the same for every part. Nothing has to cross between parts.
All inputs are finite; a program needn't handle non-finite values.
Results may differ from a plain program's by a relative error of at most 0.00002.
Values sent between devices are 32-bit elements; how exact they have to be, the bound alone decides.
No kernel may reach another device: no remote copies, remote signals or barrier semaphores. Data moves between devices by JAX's collectives and lax.ppermute only.
A program may use at most 128 MiB of HBM per device.

v0:
```python
import jax
import jax.numpy as jnp
from jax import lax
from jax.sharding import PartitionSpec as P

COURANT = 0.06


def from_behind(value, axis, steps):
    count = lax.axis_size(axis)
    leading, last = (max(0, -steps), min(count, count - steps))
    return lax.ppermute(value, axis, [(source, source + steps) for source in range(leading, last)])


def face_depths(depths):
    face_x = jnp.pad(0.5 * (depths[:, :-1] + depths[:, 1:]), ((0, 0), (0, 1)))
    face_y = jnp.pad(0.5 * (depths[:-1, :] + depths[1:, :]), ((0, 1), (0, 0)))
    return (face_x, face_y)


def divergence(flux_x, flux_y):
    west = jnp.pad(flux_x[:, :-1], ((0, 0), (1, 0)))
    south = jnp.pad(flux_y[:-1, :], ((1, 0), (0, 0)))
    return flux_x - west + flux_y - south


def forward_step(fields, face_x, face_y, courant):
    surface = fields[0]
    slope_x = jnp.pad(surface[:, 1:] - surface[:, :-1], ((0, 0), (0, 1)))
    slope_y = jnp.pad(surface[1:, :] - surface[:-1, :], ((0, 1), (0, 0)))
    east_flow = fields[1] - courant * slope_x
    north_flow = fields[2] - courant * slope_y
    surface_new = surface - courant * divergence(face_x * east_flow, face_y * north_flow)
    return jnp.stack([surface_new, east_flow, north_flow])


def adjoint_step(adjoint, face_x, face_y, courant):
    unused, pullback = jax.vjp(
        lambda fields: forward_step(fields, face_x, face_y, courant), adjoint
    )
    return pullback(adjoint)[0]


def depth_pull(cell_depth, flow_pair, surface_adjoint):

    def flux_term(depths):
        face_x, face_y = face_depths(depths)
        return -COURANT * divergence(face_x * flow_pair[0], face_y * flow_pair[1])

    unused, pullback = jax.vjp(flux_term, cell_depth)
    return pullback(surface_adjoint)[0]


def sweep(start, forcing, velocity, cell_depth, face_x, face_y, with_grad):
    adjoint = start
    partial_grad = jnp.zeros(cell_depth.shape, jnp.float32)
    for step_no in reversed(range(velocity.shape[0])):
        if with_grad:
            partial_grad = partial_grad + depth_pull(cell_depth, velocity[step_no], adjoint[0])
        adjoint = adjoint_step(adjoint, face_x, face_y, COURANT)
        adjoint = adjoint.at[0].add(forcing[step_no])
    return (adjoint, partial_grad)


def restrict(field):
    shaped = field.reshape(field.shape[:-2] + (field.shape[-2] // 2, 2, field.shape[-1] // 2, 2))
    return shaped.mean(axis=(-3, -1))


def prolong(field):
    return jnp.repeat(jnp.repeat(field, 2, axis=-2), 2, axis=-1)


def level_depth(depth_table, levels, wet_mask):
    selector = (levels[..., None] == jnp.arange(depth_table.shape[0], dtype=jnp.int32)).astype(
        jnp.float32
    )
    return wet_mask.astype(jnp.float32) * jnp.sum(selector * depth_table, axis=-1)


def shards(initial, velocity, forcing, depth_table, levels, wet_mask):
    cell_depth = level_depth(depth_table, levels, wet_mask)
    face_x, face_y = face_depths(cell_depth)
    coarse_x, coarse_y = face_depths(restrict(cell_depth))
    coarse_courant = velocity.shape[0] * COURANT / 2
    guessed = initial[0]
    following = from_behind(guessed, "tm", -1)
    relaxed, unused = sweep(following, forcing, velocity, cell_depth, face_x, face_y, False)
    coarse_residual = restrict(relaxed - guessed)

    def backward_turn(turn_no, carried_pair):
        arrived = from_behind(carried_pair[0], "tm", -1)
        return (
            coarse_residual + adjoint_step(arrived, coarse_x, coarse_y, coarse_courant),
            arrived,
        )

    correction, last_arrived = lax.fori_loop(
        0,
        lax.axis_size("tm") - 1,
        backward_turn,
        (coarse_residual, jnp.zeros_like(coarse_residual)),
    )
    corrected = guessed + prolong(correction)
    following = from_behind(corrected, "tm", -1)
    unused, partial_grad = sweep(following, forcing, velocity, cell_depth, face_x, face_y, True)
    masked = wet_mask.astype(jnp.float32) * partial_grad
    summed = lax.psum(masked, "tm")
    return (corrected[None], summed)


def solution(mesh):
    in_specs = (
        P("tm", "parts", None, None),
        P("tm", "parts", None, None),
        P("tm", "parts", None),
        P(),
        P("parts", None),
        P("parts", None),
    )
    out_specs = (P("tm", "parts", None, None), P("parts", None))
    return jax.shard_map(shards, mesh=mesh, in_specs=in_specs, out_specs=out_specs, check_vma=False)
```

profile of v0, /device:TPU:0, one launch (start us, length us, event | category | flops | bytes accessed | tf_op | source)
XLA Modules:
  0.0 303.5 jit_solution(1656526141534651188)
XLA Ops:
  7.2 1.3 collective-permute-start.1
  8.5 1.4 select_reduce_fusion
  10.0 0.9 convert_multiply_fusion
  10.9 10.6 %reshape.444 = f32[8,2,1024,2]{3,2,1,0:T(8,128)} reshape(f32[16,2048]{1,0:T(8,128)S(1)} %convert_multiply_fusion) | data formatting | bytes 262144 | tf_op jit(solution)/shard_map/reshape | solution.py:66
  21.5 4.5 %reduce_sum.29 = f32[8,1024]{1,0:T(8,128)S(1)} reduce(f32[8,2,1024,2]{3,2,1,0:T(8,128)} %reshape.444, f32[]{:T(128)} %constant.433.clone.1), dimensions={1,3}, to_apply=%region_2.3 | reduce | flops 24576 | bytes 163844 | tf_op jit(solution)/shard_map/reduce_sum | solution.py:67
  26.7 0.9 fusion.103
  28.0 0.9 fusion.104
  29.3 0.9 fusion.105
  30.6 0.9 fusion.106
  31.9 0.9 fusion.107
  33.2 0.9 fusion.108
  34.5 0.9 fusion.109
  35.9 0.9 fusion.60
  36.9 27.6 %reshape.443 = f32[3,8,2,1024,2]{4,3,2,1,0:T(8,128)} reshape(f32[3,16,2048]{2,1,0:T(8,128)S(1)} %bitcast_subtract_fusion) | data formatting | bytes 786432 | tf_op jit(solution)/shard_map/reshape | solution.py:66
  64.5 10.2 %reduce_sum.28 = f32[3,8,1024]{2,1,0:T(8,128)S(1)} reduce(f32[3,8,2,1024,2]{4,3,2,1,0:T(8,128)} %reshape.443, f32[]{:T(128)} %constant.433.clone.1), dimensions={2,4}, to_apply=%region_1.2 | reduce | flops 73728 | bytes 491524 | tf_op jit(solution)/shard_map/reduce_sum | solution.py:67
  74.7 99.7 %while.25 = (s32[]{:T(128)}, f32[3,8,1024]{2,1,0:T(8,128)S(1)}, f32[8,1024]{1,0:T(8,128)S(1)}, f32[8,1024]{1,0:T(8,128)S(1)}, f32[3,8,1024]{2,1,0:T(8,128)S(1)}, /*index=5*/s32[]{:T(128)}) while((s32[]{:T(128)}, f32[3,8,1024]{2,1,0:T(8,128)S(1)}, f32[8,1024]{1,0:T(8,128)S(1)}, f32[8,1024]{1,0:T(8,128)S(1)}, f32[3,8,1024]{2,1,0:T(8,128)S(1)}, ...), condition=%wide.region_4.5_spmd, body=%wide.region_3.4_spmd.sunk | while | flops 242666 | bytes 1539949 | solution.py:98
  74.7 1.3 collective-permute-start
  76.0 2.5 collective-permute-done
  78.8 1.3 collective-permute-start
  80.1 5.5 %collective-permute-done = f32[3,8,1024]{2,1,0:T(8,128)S(1)} collective-permute-done((f32[3,8,1024]{2,1,0:T(8,128)S(1)}, f32[3,8,1024]{2,1,0:T(8,128)S(1)}, u32[]{:S(2)}, u32[]{:S(2)}) %collective-permute-start) | collective-permute-done | bytes 98336 | tf_op jit(solution)/shard_map/while/body/eval_jaxpr/ppermute | solution.py:12
  85.8 1.3 collective-permute-start
  87.1 4.6 %collective-permute-done = f32[3,8,1024]{2,1,0:T(8,128)S(1)} collective-permute-done((f32[3,8,1024]{2,1,0:T(8,128)S(1)}, f32[3,8,1024]{2,1,0:T(8,128)S(1)}, u32[]{:S(2)}, u32[]{:S(2)}) %collective-permute-start) | collective-permute-done | bytes 98336 | tf_op jit(solution)/shard_map/while/body/eval_jaxpr/ppermute | solution.py:12
  92.0 1.3 collective-permute-start
  93.3 4.6 %collective-permute-done = f32[3,8,1024]{2,1,0:T(8,128)S(1)} collective-permute-done((f32[3,8,1024]{2,1,0:T(8,128)S(1)}, f32[3,8,1024]{2,1,0:T(8,128)S(1)}, u32[]{:S(2)}, u32[]{:S(2)}) %collective-permute-start) | collective-permute-done | bytes 98336 | tf_op jit(solution)/shard_map/while/body/eval_jaxpr/ppermute | solution.py:12
  98.2 1.3 collective-permute-start
  99.5 4.6 %collective-permute-done = f32[3,8,1024]{2,1,0:T(8,128)S(1)} collective-permute-done((f32[3,8,1024]{2,1,0:T(8,128)S(1)}, f32[3,8,1024]{2,1,0:T(8,128)S(1)}, u32[]{:S(2)}, u32[]{:S(2)}) %collective-permute-start) | collective-permute-done | bytes 98336 | tf_op jit(solution)/shard_map/while/body/eval_jaxpr/ppermute | solution.py:12
  104.4 1.3 collective-permute-start
  105.7 4.6 %collective-permute-done = f32[3,8,1024]{2,1,0:T(8,128)S(1)} collective-permute-done((f32[3,8,1024]{2,1,0:T(8,128)S(1)}, f32[3,8,1024]{2,1,0:T(8,128)S(1)}, u32[]{:S(2)}, u32[]{:S(2)}) %collective-permute-start) | collective-permute-done | bytes 98336 | tf_op jit(solution)/shard_map/while/body/eval_jaxpr/ppermute | solution.py:12
  110.6 1.3 collective-permute-start
  111.9 5.5 %collective-permute-done = f32[3,8,1024]{2,1,0:T(8,128)S(1)} collective-permute-done((f32[3,8,1024]{2,1,0:T(8,128)S(1)}, f32[3,8,1024]{2,1,0:T(8,128)S(1)}, u32[]{:S(2)}, u32[]{:S(2)}) %collective-permute-start) | collective-permute-done | bytes 98336 | tf_op jit(solution)/shard_map/while/body/eval_jaxpr/ppermute | solution.py:12
  117.6 1.3 collective-permute-start
  118.9 5.5 %collective-permute-done = f32[3,8,1024]{2,1,0:T(8,128)S(1)} collective-permute-done((f32[3,8,1024]{2,1,0:T(8,128)S(1)}, f32[3,8,1024]{2,1,0:T(8,128)S(1)}, u32[]{:S(2)}, u32[]{:S(2)}) %collective-permute-start) | collective-permute-done | bytes 98336 | tf_op jit(solution)/shard_map/while/body/eval_jaxpr/ppermute | solution.py:12
  124.7 1.3 collective-permute-start
  126.0 5.5 %collective-permute-done = f32[3,8,1024]{2,1,0:T(8,128)S(1)} collective-permute-done((f32[3,8,1024]{2,1,0:T(8,128)S(1)}, f32[3,8,1024]{2,1,0:T(8,128)S(1)}, u32[]{:S(2)}, u32[]{:S(2)}) %collective-permute-start) | collective-permute-done | bytes 98336 | tf_op jit(solution)/shard_map/while/body/eval_jaxpr/ppermute | solution.py:12
  131.8 1.3 collective-permute-start
  133.1 5.5 %collective-permute-done = f32[3,8,1024]{2,1,0:T(8,128)S(1)} collective-permute-done((f32[3,8,1024]{2,1,0:T(8,128)S(1)}, f32[3,8,1024]{2,1,0:T(8,128)S(1)}, u32[]{:S(2)}, u32[]{:S(2)}) %collective-permute-start) | collective-permute-done | bytes 98336 | tf_op jit(solution)/shard_map/while/body/eval_jaxpr/ppermute | solution.py:12
  138.9 1.3 collective-permute-start
  140.2 5.5 %collective-permute-done = f32[3,8,1024]{2,1,0:T(8,128)S(1)} collective-permute-done((f32[3,8,1024]{2,1,0:T(8,128)S(1)}, f32[3,8,1024]{2,1,0:T(8,128)S(1)}, u32[]{:S(2)}, u32[]{:S(2)}) %collective-permute-start) | collective-permute-done | bytes 98336 | tf_op jit(solution)/shard_map/while/body/eval_jaxpr/ppermute | solution.py:12
  146.0 1.3 collective-permute-start
  147.3 5.5 %collective-permute-done = f32[3,8,1024]{2,1,0:T(8,128)S(1)} collective-permute-done((f32[3,8,1024]{2,1,0:T(8,128)S(1)}, f32[3,8,1024]{2,1,0:T(8,128)S(1)}, u32[]{:S(2)}, u32[]{:S(2)}) %collective-permute-start) | collective-permute-done | bytes 98336 | tf_op jit(solution)/shard_map/while/body/eval_jaxpr/ppermute | solution.py:12
  153.1 1.3 collective-permute-start
  154.4 5.5 %collective-permute-done = f32[3,8,1024]{2,1,0:T(8,128)S(1)} collective-permute-done((f32[3,8,1024]{2,1,0:T(8,128)S(1)}, f32[3,8,1024]{2,1,0:T(8,128)S(1)}, u32[]{:S(2)}, u32[]{:S(2)}) %collective-permute-start) | collective-permute-done | bytes 98336 | tf_op jit(solution)/shard_map/while/body/eval_jaxpr/ppermute | solution.py:12
  160.2 1.3 collective-permute-start
  161.5 5.5 %collective-permute-done = f32[3,8,1024]{2,1,0:T(8,128)S(1)} collective-permute-done((f32[3,8,1024]{2,1,0:T(8,128)S(1)}, f32[3,8,1024]{2,1,0:T(8,128)S(1)}, u32[]{:S(2)}, u32[]{:S(2)}) %collective-permute-start) | collective-permute-done | bytes 98336 | tf_op jit(solution)/shard_map/while/body/eval_jaxpr/ppermute | solution.py:12
  167.3 1.3 collective-permute-start
  168.6 5.5 %collective-permute-done = f32[3,8,1024]{2,1,0:T(8,128)S(1)} collective-permute-done((f32[3,8,1024]{2,1,0:T(8,128)S(1)}, f32[3,8,1024]{2,1,0:T(8,128)S(1)}, u32[]{:S(2)}, u32[]{:S(2)}) %collective-permute-start) | collective-permute-done | bytes 98336 | tf_op jit(solution)/shard_map/while/body/eval_jaxpr/ppermute | solution.py:12
  174.5 0.1 reshape.445
  174.6 1.7 copy.112
  176.3 2.5 broadcast_in_dim.179
  178.8 1.8 copy.114
  180.6 1.2 bitcast_add_fusion
  181.7 1.5 collective-permute-start.2
  183.2 1.7 slice_bitcast_fusion.50
  184.9 4.0 %collective-permute-done.2 = f32[3,16,2048]{2,1,0:T(8,128)S(1)} collective-permute-done((f32[3,16,2048]{2,1,0:T(8,128)S(1)}, f32[3,16,2048]{2,1,0:T(8,128)S(1)}, u32[]{:S(2)}, u32[]{:S(2)}) %collective-permute-start.2) | collective-permute-done | bytes 393248 | tf_op jit(solution)/shard_map/ppermute | solution.py:12
  189.3 0.1 add_bitcast_fusion.7
  189.4 0.8 copy-done
  193.5 0.1 add_bitcast_fusion.1
  194.4 0.7 copy-done.2
  195.1 1.0 add_multiply_fusion
  196.1 3.0 %copy.113 = f32[1,3,16,2048]{2,3,1,0:T(8,128)} copy(f32[1,3,16,2048]{3,2,1,0:T(8,128)} %param.38) | data formatting | bytes 786432 | tf_op args[0]
  199.1 3.8 %add.556 = f32[1,3,16,2048]{2,3,1,0:T(8,128)} add(f32[1,3,16,2048]{2,3,1,0:T(8,128)} %copy.113, f32[1,3,16,2048]{2,3,1,0:T(8,128)S(1)} %bitcast.326) | non-fusion elementwise | flops 98304 | bytes 1179648 | tf_op jit(solution)/shard_map/add | solution.py:104
  203.0 3.0 copy.115
  206.0 89.1 %all-reduce.198.cloned.1.call-done = f32[16,2048]{1,0:T(8,128)} async-done(((f32[16,2048]{1,0:T(8,128)}), f32[16,2048]{1,0:T(8,128)}) %all-reduce.198.cloned.1.call-update) | async-done | bytes 131088 | tf_op jit(solution)/shard_map/psum | solution.py:108
  295.1 1.6 copy.126
  (279 shorter events, 10.1 us)
Async XLA Ops:
  7.2 287.9 %all-reduce.198.cloned.1.call-start = ((), (), s32[]{:S(2)}) async-start(), calls=%async_computation | async-start | bytes 262144 | tf_op jit(solution)/shard_map/psum | solution.py:108
  7.2 19.0 %collective-permute-start.1 = (f32[3,16,2048]{2,1,0:T(8,128)}, f32[3,16,2048]{2,1,0:T(8,128)S(1)}, u32[]{:S(2)}, u32[]{:S(2)}) collective-permute-start(f32[3,16,2048]{2,1,0:T(8,128)} %bitcast.329), channel_id=1, source_target_pairs={{1,0},{2,1},{3,2},{4,3},{5,4},{6,5},{7,6},{8,7},{9,8},{10,9},{11,1... | collective-permute-start | bytes 1179656 | tf_op jit(solution)/shard_map/ppermute | solution.py:12
  35.5 1.3 copy-start.1
  74.7 3.8 %collective-permute-start = (f32[3,8,1024]{2,1,0:T(8,128)S(1)}, f32[3,8,1024]{2,1,0:T(8,128)S(1)}, u32[]{:S(2)}, u32[]{:S(2)}) collective-permute-start(f32[3,8,1024]{2,1,0:T(8,128)S(1)} %get-tuple-element.443), channel_id=1, source_target_pairs={{1,0},{2,1},{3,2},{4,3},{5,4},{6,5},{7,6},{8,7},{9,8},{10,9},{11,1... | collective-permute-start | bytes 294920 | tf_op jit(solution)/shard_map/while/body/eval_jaxpr/ppermute | solution.py:12
  78.8 6.8 %collective-permute-start = (f32[3,8,1024]{2,1,0:T(8,128)S(1)}, f32[3,8,1024]{2,1,0:T(8,128)S(1)}, u32[]{:S(2)}, u32[]{:S(2)}) collective-permute-start(f32[3,8,1024]{2,1,0:T(8,128)S(1)} %get-tuple-element.443), channel_id=1, source_target_pairs={{1,0},{2,1},{3,2},{4,3},{5,4},{6,5},{7,6},{8,7},{9,8},{10,9},{11,1... | collective-permute-start | bytes 294920 | tf_op jit(solution)/shard_map/while/body/eval_jaxpr/ppermute | solution.py:12
  85.8 5.9 %collective-permute-start = (f32[3,8,1024]{2,1,0:T(8,128)S(1)}, f32[3,8,1024]{2,1,0:T(8,128)S(1)}, u32[]{:S(2)}, u32[]{:S(2)}) collective-permute-start(f32[3,8,1024]{2,1,0:T(8,128)S(1)} %get-tuple-element.443), channel_id=1, source_target_pairs={{1,0},{2,1},{3,2},{4,3},{5,4},{6,5},{7,6},{8,7},{9,8},{10,9},{11,1... | collective-permute-start | bytes 294920 | tf_op jit(solution)/shard_map/while/body/eval_jaxpr/ppermute | solution.py:12
  92.0 5.9 %collective-permute-start = (f32[3,8,1024]{2,1,0:T(8,128)S(1)}, f32[3,8,1024]{2,1,0:T(8,128)S(1)}, u32[]{:S(2)}, u32[]{:S(2)}) collective-permute-start(f32[3,8,1024]{2,1,0:T(8,128)S(1)} %get-tuple-element.443), channel_id=1, source_target_pairs={{1,0},{2,1},{3,2},{4,3},{5,4},{6,5},{7,6},{8,7},{9,8},{10,9},{11,1... | collective-permute-start | bytes 294920 | tf_op jit(solution)/shard_map/while/body/eval_jaxpr/ppermute | solution.py:12
  98.2 5.9 %collective-permute-start = (f32[3,8,1024]{2,1,0:T(8,128)S(1)}, f32[3,8,1024]{2,1,0:T(8,128)S(1)}, u32[]{:S(2)}, u32[]{:S(2)}) collective-permute-start(f32[3,8,1024]{2,1,0:T(8,128)S(1)} %get-tuple-element.443), channel_id=1, source_target_pairs={{1,0},{2,1},{3,2},{4,3},{5,4},{6,5},{7,6},{8,7},{9,8},{10,9},{11,1... | collective-permute-start | bytes 294920 | tf_op jit(solution)/shard_map/while/body/eval_jaxpr/ppermute | solution.py:12
  104.4 5.9 %collective-permute-start = (f32[3,8,1024]{2,1,0:T(8,128)S(1)}, f32[3,8,1024]{2,1,0:T(8,128)S(1)}, u32[]{:S(2)}, u32[]{:S(2)}) collective-permute-start(f32[3,8,1024]{2,1,0:T(8,128)S(1)} %get-tuple-element.443), channel_id=1, source_target_pairs={{1,0},{2,1},{3,2},{4,3},{5,4},{6,5},{7,6},{8,7},{9,8},{10,9},{11,1... | collective-permute-start | bytes 294920 | tf_op jit(solution)/shard_map/while/body/eval_jaxpr/ppermute | solution.py:12
  110.6 6.8 %collective-permute-start = (f32[3,8,1024]{2,1,0:T(8,128)S(1)}, f32[3,8,1024]{2,1,0:T(8,128)S(1)}, u32[]{:S(2)}, u32[]{:S(2)}) collective-permute-start(f32[3,8,1024]{2,1,0:T(8,128)S(1)} %get-tuple-element.443), channel_id=1, source_target_pairs={{1,0},{2,1},{3,2},{4,3},{5,4},{6,5},{7,6},{8,7},{9,8},{10,9},{11,1... | collective-permute-start | bytes 294920 | tf_op jit(solution)/shard_map/while/body/eval_jaxpr/ppermute | solution.py:12
  117.6 6.8 %collective-permute-start = (f32[3,8,1024]{2,1,0:T(8,128)S(1)}, f32[3,8,1024]{2,1,0:T(8,128)S(1)}, u32[]{:S(2)}, u32[]{:S(2)}) collective-permute-start(f32[3,8,1024]{2,1,0:T(8,128)S(1)} %get-tuple-element.443), channel_id=1, source_target_pairs={{1,0},{2,1},{3,2},{4,3},{5,4},{6,5},{7,6},{8,7},{9,8},{10,9},{11,1... | collective-permute-start | bytes 294920 | tf_op jit(solution)/shard_map/while/body/eval_jaxpr/ppermute | solution.py:12
  124.7 6.8 %collective-permute-start = (f32[3,8,1024]{2,1,0:T(8,128)S(1)}, f32[3,8,1024]{2,1,0:T(8,128)S(1)}, u32[]{:S(2)}, u32[]{:S(2)}) collective-permute-start(f32[3,8,1024]{2,1,0:T(8,128)S(1)} %get-tuple-element.443), channel_id=1, source_target_pairs={{1,0},{2,1},{3,2},{4,3},{5,4},{6,5},{7,6},{8,7},{9,8},{10,9},{11,1... | collective-permute-start | bytes 294920 | tf_op jit(solution)/shard_map/while/body/eval_jaxpr/ppermute | solution.py:12
  131.8 6.8 %collective-permute-start = (f32[3,8,1024]{2,1,0:T(8,128)S(1)}, f32[3,8,1024]{2,1,0:T(8,128)S(1)}, u32[]{:S(2)}, u32[]{:S(2)}) collective-permute-start(f32[3,8,1024]{2,1,0:T(8,128)S(1)} %get-tuple-element.443), channel_id=1, source_target_pairs={{1,0},{2,1},{3,2},{4,3},{5,4},{6,5},{7,6},{8,7},{9,8},{10,9},{11,1... | collective-permute-start | bytes 294920 | tf_op jit(solution)/shard_map/while/body/eval_jaxpr/ppermute | solution.py:12
  138.9 6.8 %collective-permute-start = (f32[3,8,1024]{2,1,0:T(8,128)S(1)}, f32[3,8,1024]{2,1,0:T(8,128)S(1)}, u32[]{:S(2)}, u32[]{:S(2)}) collective-permute-start(f32[3,8,1024]{2,1,0:T(8,128)S(1)} %get-tuple-element.443), channel_id=1, source_target_pairs={{1,0},{2,1},{3,2},{4,3},{5,4},{6,5},{7,6},{8,7},{9,8},{10,9},{11,1... | collective-permute-start | bytes 294920 | tf_op jit(solution)/shard_map/while/body/eval_jaxpr/ppermute | solution.py:12
  146.0 6.8 %collective-permute-start = (f32[3,8,1024]{2,1,0:T(8,128)S(1)}, f32[3,8,1024]{2,1,0:T(8,128)S(1)}, u32[]{:S(2)}, u32[]{:S(2)}) collective-permute-start(f32[3,8,1024]{2,1,0:T(8,128)S(1)} %get-tuple-element.443), channel_id=1, source_target_pairs={{1,0},{2,1},{3,2},{4,3},{5,4},{6,5},{7,6},{8,7},{9,8},{10,9},{11,1... | collective-permute-start | bytes 294920 | tf_op jit(solution)/shard_map/while/body/eval_jaxpr/ppermute | solution.py:12
  153.1 6.8 %collective-permute-start = (f32[3,8,1024]{2,1,0:T(8,128)S(1)}, f32[3,8,1024]{2,1,0:T(8,128)S(1)}, u32[]{:S(2)}, u32[]{:S(2)}) collective-permute-start(f32[3,8,1024]{2,1,0:T(8,128)S(1)} %get-tuple-element.443), channel_id=1, source_target_pairs={{1,0},{2,1},{3,2},{4,3},{5,4},{6,5},{7,6},{8,7},{9,8},{10,9},{11,1... | collective-permute-start | bytes 294920 | tf_op jit(solution)/shard_map/while/body/eval_jaxpr/ppermute | solution.py:12
  160.2 6.8 %collective-permute-start = (f32[3,8,1024]{2,1,0:T(8,128)S(1)}, f32[3,8,1024]{2,1,0:T(8,128)S(1)}, u32[]{:S(2)}, u32[]{:S(2)}) collective-permute-start(f32[3,8,1024]{2,1,0:T(8,128)S(1)} %get-tuple-element.443), channel_id=1, source_target_pairs={{1,0},{2,1},{3,2},{4,3},{5,4},{6,5},{7,6},{8,7},{9,8},{10,9},{11,1... | collective-permute-start | bytes 294920 | tf_op jit(solution)/shard_map/while/body/eval_jaxpr/ppermute | solution.py:12
  167.3 6.8 %collective-permute-start = (f32[3,8,1024]{2,1,0:T(8,128)S(1)}, f32[3,8,1024]{2,1,0:T(8,128)S(1)}, u32[]{:S(2)}, u32[]{:S(2)}) collective-permute-start(f32[3,8,1024]{2,1,0:T(8,128)S(1)} %get-tuple-element.443), channel_id=1, source_target_pairs={{1,0},{2,1},{3,2},{4,3},{5,4},{6,5},{7,6},{8,7},{9,8},{10,9},{11,1... | collective-permute-start | bytes 294920 | tf_op jit(solution)/shard_map/while/body/eval_jaxpr/ppermute | solution.py:12
  181.7 7.3 %collective-permute-start.2 = (f32[3,16,2048]{2,1,0:T(8,128)S(1)}, f32[3,16,2048]{2,1,0:T(8,128)S(1)}, u32[]{:S(2)}, u32[]{:S(2)}) collective-permute-start(f32[3,16,2048]{2,1,0:T(8,128)S(1)} %bitcast_add_fusion), channel_id=1, source_target_pairs={{1,0},{2,1},{3,2},{4,3},{5,4},{6,5},{7,6},{8,7},{9,8},{10,9},{11,1... | collective-permute-start | bytes 1179656 | tf_op jit(solution)/shard_map/ppermute | solution.py:12
  189.0 1.2 copy-start
  194.2 0.9 copy-start.2
Sparse Core Ops, SparseCore 0:
  196.2 98.7 all-reduce.197
where the time goes:
time: 306 us; the launch traced here: 303 us
  waiting for transfers between devices  169 us (55%)
  local copies, waits for them, and re-layouts  58.8 us (19%)
  other arithmetic  37.1 us (12%)
  starting transfers between devices  22.2 us (7%)
  between operations  15.2 us (5%)
    psum x1, waiting for transfers between devices, shards(): summed = lax.psum(masked, 'tm')  89.1 us
    ppermute x17, waiting for transfers between devices, from_behind(): lax.ppermute(value, axis, [(source, source + steps) for source in range(l...  80.3 us
    reshape x2, local copies, waits for them, and re-layouts, restrict(): field.reshape(field.shape[:-2] + (field.shape[-2] // 2, 2, field.shape[-1...  38.2 us
    ppermute x17, starting transfers between devices, from_behind(): lax.ppermute(value, axis, [(source, source + steps) for source in range(l...  22.1 us
    reduce_sum x2, other arithmetic, restrict(): return shaped.mean(axis=(-3, -1))  14.7 us
    unnamed x10, local copies, waits for them, and re-layouts  9.1 us
    neg x30, other arithmetic, divergence(): return flux_x - west + flux_y - south  6.69 us
  transfers between devices with their start and end apart: 18, of which 17 were waited for; matrix products, arithmetic and copies ran while one was open for 10% of the time, Pallas kernels for 0%

commit v1 on v0

v1 whole, which is shorter than its diff:
```python
import functools

import jax
import jax.numpy as jnp
from jax import lax
from jax.experimental import pallas as pl
from jax.experimental.pallas import tpu as pltpu
from jax.sharding import PartitionSpec as P

COURANT = 0.06
LANES = 128
VMEM = pl.BlockSpec(memory_space=pltpu.VMEM)
SMEM = pl.BlockSpec(memory_space=pltpu.SMEM)
EXACT = lax.Precision.HIGHEST


def roll(value, steps, axis):
    return pltpu.roll(value, steps % value.shape[axis], axis)


def index_of(shape, axis):
    return lax.broadcasted_iota(jnp.int32, shape, axis)


def faces(depth, scale):
    rows, cols = depth.shape
    half = 0.5 * scale
    east = half * (depth + roll(depth, -1, 1))
    north = half * (depth + roll(depth, -1, 0))
    east = jnp.where(index_of(depth.shape, 1) < cols - 1, east, 0.0)
    north = jnp.where(index_of(depth.shape, 0) < rows - 1, north, 0.0)
    return east, north


def fine_step(s, e, n, face_x, face_y):
    slope_x = roll(s, -1, 1) - s
    slope_y = roll(s, -1, 0) - s
    e = e + face_x * slope_x
    n = n + face_y * slope_y
    s = s + ((e - roll(e, 1, 1)) + (n - roll(n, 1, 0)))
    return s, e, n, slope_x, slope_y


def coarse_step(fields, face_x, face_y):
    s, e, n = fields
    rows, cols = s.shape
    e = e + face_x * (roll(s, -1, 1) - s)
    n = n + face_y * (roll(s, -1, 0) - s)
    e_in = jnp.where(index_of(s.shape, 1) < cols - 1, e, 0.0)
    n_in = jnp.where(index_of(s.shape, 0) < rows - 1, n, 0.0)
    s = s + ((e_in - roll(e_in, 1, 1)) + (n_in - roll(n_in, 1, 0)))
    return s, e, n


def power(fields, count, face_x, face_y):
    if count <= 4:
        for _ in range(count):
            fields = coarse_step(fields, face_x, face_y)
        return fields
    return lax.fori_loop(0, count, lambda _, f: coarse_step(f, face_x, face_y), fields)


def add(a, b):
    return tuple(x + y for x, y in zip(a, b))


def scaled(a, factor):
    return tuple(x * factor for x in a)


def pick(first, a, b):
    return tuple(jnp.where(first, x, y) for x, y in zip(a, b))


def read(ref, at=0):
    return tuple(ref[at + i] for i in range(3))


def write(ref, fields, at=0):
    for i, field in enumerate(fields):
        ref[at + i] = field


def pair_matrix(shape, wide_axis, weight):
    wide = index_of(shape, wide_axis) // 2
    return jnp.where(wide == index_of(shape, 1 - wide_axis), weight, 0.0)


def product(a, b):
    return jnp.dot(a, b, precision=EXACT, preferred_element_type=jnp.float32)


def restrict_all(fields):
    rows, cols = fields[0].shape
    half = rows // 2
    stacked = jnp.concatenate(fields, axis=0)
    gather = pair_matrix((2 * LANES, LANES), 0, 0.25)
    merged = jnp.concatenate(
        [product(stacked[:, c : c + 2 * LANES], gather) for c in range(0, cols, 2 * LANES)], axis=1
    )
    merged = product(pair_matrix((stacked.shape[0] // 2, stacked.shape[0]), 1, 1.0), merged)
    return [merged[i * half : (i + 1) * half] for i in range(len(fields))]


def prolong_all(fields):
    half, cols = fields[0].shape
    stacked = jnp.concatenate(fields, axis=0)
    stacked = product(pair_matrix((2 * stacked.shape[0], stacked.shape[0]), 0, 1.0), stacked)
    spread = pair_matrix((LANES, 2 * LANES), 1, 1.0)
    merged = jnp.concatenate(
        [product(stacked[:, c : c + LANES], spread) for c in range(0, cols, LANES)], axis=1
    )
    return [merged[2 * i * half : 2 * (i + 1) * half] for i in range(len(fields))]


def prepare(table, levels, wet, initial, forcing, own, sent, fine_faces, coarse_faces):
    rows, cols = levels.shape
    steps = forcing.shape[0]
    width = own.shape[2]
    coarse_cols = cols // 2
    level = levels[...]
    depth = jnp.zeros((rows, cols), jnp.float32)
    for i in range(table.shape[0]):
        depth = jnp.where(level == i, table[i], depth)
    depth = depth * wet[...].astype(jnp.float32)
    face_x, face_y = faces(depth, COURANT * COURANT)
    fine_faces[0] = face_x
    fine_faces[1] = face_y
    inner_x = index_of((rows, cols), 1) < cols - 1
    inner_y = index_of((rows, cols), 0) < rows - 1

    s0, e0, n0 = initial[0, 0], initial[0, 1] * COURANT, initial[0, 2] * COURANT
    s, e, n = s0, jnp.where(inner_x, e0, 0.0), jnp.where(inner_y, n0, 0.0)
    for _ in range(steps):
        s, e, n, _, _ = fine_step(s, e, n, face_x, face_y)
    relaxed = [s, jnp.where(inner_x, e, e0), jnp.where(inner_y, n, n0)]

    s = forcing[steps - 1]
    e = jnp.zeros_like(s)
    n = jnp.zeros_like(s)
    for step in reversed(range(steps - 1)):
        s, e, n, _, _ = fine_step(s, e, n, face_x, face_y)
        s = s + forcing[step]
    relaxed += [s - s0, e - e0, n - n0, depth]
    su, eu, nu, sw, ew, nw, coarse_depth = restrict_all(relaxed)
    ratio = steps / 2
    coarse_courant = COURANT * ratio
    cx, cy = faces(coarse_depth, coarse_courant * coarse_courant)
    w = (sw, ew * ratio, nw * ratio)
    g = add((su, eu * ratio, nu * ratio), coarse_step(w, cx, cy))

    core = lax.rem(lax.axis_index("tm"), 2)
    right = coarse_cols - width

    def store(mine, other):
        for ref, at in ((own, mine), (sent, other)):
            for i in range(3):
                ref[i] = g[i][:, at : at + width]
                ref[3 + i] = w[i][:, at : at + width]
        coarse_faces[0] = cx[:, mine : mine + width]
        coarse_faces[1] = cy[:, mine : mine + width]

    @pl.when(core == 0)
    def _():
        store(0, right)

    @pl.when(core == 1)
    def _():
        store(right, 0)


def chip_pair(own, got, coarse_faces, out):
    cx, cy = coarse_faces[0], coarse_faces[1]
    first = lax.rem(lax.axis_index("tm"), 2) == 0
    g_own, g_got = read(own), read(got)
    g_low, g_high = pick(first, g_own, g_got), pick(first, g_got, g_own)
    w_low = pick(first, read(own, 3), read(got, 3))
    write(out, add(g_low, coarse_step(g_high, cx, cy)))
    write(out, add(w_low, g_high), 3)


def row_pair(own, got, coarse_faces, out, out_t):
    cx, cy = coarse_faces[0], coarse_faces[1]
    first = lax.rem(lax.axis_index("tm") // 2, 2) == 0
    t_own, t_got = read(own), read(got)
    t_low, t_high = pick(first, t_own, t_got), pick(first, t_got, t_own)
    q_low = pick(first, read(own, 3), read(got, 3))
    moved = coarse_step(t_high, cx, cy)
    total = add(t_low, coarse_step(moved, cx, cy))
    write(out, total)
    write(out_t, total)
    write(out, add(q_low, moved), 3)


def widen(stride, own, got, coarse_faces, out, *, per_row, rows_in_all):
    row = lax.axis_index("tm") // per_row
    there = jnp.where(row + stride < rows_in_all, 1.0, 0.0)
    moved = power(scaled(read(got), there), per_row * stride, coarse_faces[0], coarse_faces[1])
    write(out, add(read(own), moved))


def finish(near, far, farther, own, got, chip, partner, coarse_faces, kept, sent, *, per_row, rows_in_all):
    cx, cy = coarse_faces[0], coarse_faces[1]
    width = coarse_faces.shape[2]
    half = kept.shape[2]
    device = lax.axis_index("tm")
    row = device // per_row

    def there(stride):
        return jnp.where(row + stride < rows_in_all, 1.0, 0.0)

    rest = scaled(read(far), there(2))
    if farther is not None:
        rest = add(rest, power(scaled(read(farther), there(3)), per_row, cx, cy))
    rest = power(rest, per_row - 1, cx, cy)
    after = add(scaled(read(near, 3), there(1)), rest)
    end = add(scaled(read(near), there(1)), coarse_step(rest, cx, cy))
    if partner is not None:
        low = lax.rem(device // 2, 2) == 0
        moved = coarse_step(end, cx, cy)
        after = pick(low, add(read(partner, 3), moved), after)
        end = pick(low, add(read(partner), coarse_step(moved, cx, cy)), end)
    first = lax.rem(device, 2) == 0
    w_high = pick(first, read(got, 3), read(own, 3))
    q = read(chip, 3)
    c_low = add(q, coarse_step(end, cx, cy))
    c_high = add(w_high, end)

    @pl.when(first)
    def _():
        for i in range(3):
            kept[i] = c_low[i][:, :half]
            kept[3 + i] = c_high[i][:, :half]
            sent[i] = c_high[i][:, :half]
            sent[3 + i] = after[i][:, :half]

    @pl.when(jnp.logical_not(first))
    def _():
        for i in range(3):
            kept[i] = c_high[i][:, width - half :]
            kept[3 + i] = after[i][:, width - half :]
            sent[i] = c_low[i][:, width - half :]
            sent[3 + i] = c_high[i][:, width - half :]


def descend(kept, got, initial, following, forcing, velocity, fine_faces, wet, corrected, mine, other):
    steps = forcing.shape[0]
    rows, cols = wet.shape
    device = lax.axis_index("tm")
    first = lax.rem(device, 2) == 0
    unscale = 1.0 / (COURANT * (steps / 2))
    fields = []
    for i in range(6):
        left = jnp.where(first, kept[i], got[i])
        right = jnp.where(first, got[i], kept[i])
        field = jnp.concatenate([left, right], axis=1)
        fields.append(field if i % 3 == 0 else field * unscale)
    fields = prolong_all(fields)
    for i in range(3):
        corrected[0, i] = initial[0, i] + fields[i]

    there = jnp.where(device + 1 < lax.axis_size("tm"), 1.0, 0.0)
    inner_x = index_of((rows, cols), 1) < cols - 1
    inner_y = index_of((rows, cols), 0) < rows - 1
    s = (following[0, 0] * there) + fields[3]
    e = jnp.where(inner_x, (following[0, 1] * there + fields[4]) * COURANT, 0.0)
    n = jnp.where(inner_y, (following[0, 2] * there + fields[5]) * COURANT, 0.0)
    face_x, face_y = fine_faces[0], fine_faces[1]
    grad_x = jnp.zeros_like(s)
    grad_y = jnp.zeros_like(s)
    for step in reversed(range(steps)):
        s, e, n, slope_x, slope_y = fine_step(s, e, n, face_x, face_y)
        grad_x = grad_x + slope_x * velocity[step, 0]
        grad_y = grad_y + slope_y * velocity[step, 1]
        s = s + forcing[step]
    grad_x = jnp.where(inner_x, grad_x, 0.0)
    grad_y = jnp.where(inner_y, grad_y, 0.0)
    grad = (grad_x + roll(grad_x, 1, 1)) + (grad_y + roll(grad_y, 1, 0))
    grad = (0.5 * COURANT) * grad * wet[...].astype(jnp.float32)
    half = cols // 2

    @pl.when(first)
    def _():
        mine[...] = grad[:, :half]
        other[...] = grad[:, half:]

    @pl.when(jnp.logical_not(first))
    def _():
        mine[...] = grad[:, half:]
        other[...] = grad[:, :half]


def call(body, shapes, operands, specs=None):
    return pl.pallas_call(
        body,
        out_shape=[jax.ShapeDtypeStruct(shape, jnp.float32) for shape in shapes],
        in_specs=specs or [VMEM] * len(operands),
        out_specs=[VMEM] * len(shapes),
        compiler_params=pltpu.CompilerParams(vmem_limit_bytes=32 * 1024 * 1024),
    )(*operands)


def shards(initial, velocity, forcing, depth_table, levels, wet_mask):
    count = lax.axis_size("tm")
    rows, cols = levels.shape
    half_rows, half = rows // 2, cols // 4
    halo = -(-count // LANES) * LANES
    width = half + halo
    block = (half_rows, width)

    def paired(value, stride):
        return lax.ppermute(value, "tm", [(s, s ^ stride) for s in range(count)])

    def back(value, stride):
        return lax.ppermute(value, "tm", [(s, (s - stride) % count) for s in range(count)])

    following = lax.ppermute(initial, "tm", [(s, s - 1) for s in range(1, count)])
    own, sent, fine_faces, coarse_faces = call(
        prepare,
        [(6, *block), (6, *block), (2, rows, cols), (2, *block)],
        [depth_table, levels, wet_mask, initial, forcing],
        specs=[SMEM] + [VMEM] * 4,
    )
    got = paired(sent, 1)
    (chip,) = call(chip_pair, [(6, *block)], [own, got, coarse_faces])
    per_row = 4 if count <= 16 else 2
    rows_in_all = count // per_row
    if per_row == 4:
        partner = paired(chip, 2)
        row, row_t = call(row_pair, [(6, *block), (3, *block)], [chip, partner, coarse_faces])
    else:
        partner = None
        row, row_t = chip, chip[:3]
    near = back(row, per_row)
    if rows_in_all <= 4:
        far, farther = back(row_t, 2 * per_row), back(row_t, 3 * per_row)
    else:
        stride = 1
        while stride < rows_in_all - 2:
            (row_t,) = call(
                functools.partial(widen, stride, per_row=per_row, rows_in_all=rows_in_all),
                [(3, *block)],
                [row_t, back(row_t, stride * per_row), coarse_faces],
            )
            stride *= 2
        far, farther = back(row_t, 2 * per_row), None

    operands = {
        "near": near,
        "far": far,
        "farther": farther,
        "own": own,
        "got": got,
        "chip": chip,
        "partner": partner,
        "coarse_faces": coarse_faces,
    }
    names = [name for name, value in operands.items() if value is not None]

    def finish_body(*refs):
        given = dict.fromkeys(operands)
        given.update(zip(names, refs))
        kept, sent = refs[len(names) :]
        finish(**given, kept=kept, sent=sent, per_row=per_row, rows_in_all=rows_in_all)

    kept, sent = call(finish_body, [(6, half_rows, half)] * 2, [operands[name] for name in names])
    got = paired(sent, 1)
    corrected, mine, other = call(
        descend,
        [initial.shape, (rows, cols // 2), (rows, cols // 2)],
        [kept, got, initial, following, forcing, velocity, fine_faces, wet_mask],
    )
    mine = mine + paired(other, 1)
    if per_row == 4:
        mine = mine + paired(mine, 2)
    if rows_in_all == 4:
        mine = mine + paired(mine, 4) + paired(mine, 8) + paired(mine, 12)
    else:
        stride = per_row
        while stride < count:
            mine = mine + paired(mine, stride)
            stride *= 2
    other = paired(mine, 1)
    first = lax.rem(lax.axis_index("tm"), 2) == 0
    left, right = jnp.where(first, mine, other), jnp.where(first, other, mine)
    return corrected, jnp.concatenate([left, right], axis=1)


def solution(mesh):
    in_specs = (
        P("tm", "parts", None, None),
        P("tm", "parts", None, None),
        P("tm", "parts", None),
        P(),
        P("parts", None),
        P("parts", None),
    )
    out_specs = (P("tm", "parts", None, None), P("parts", None))
    return jax.shard_map(shards, mesh=mesh, in_specs=in_specs, out_specs=out_specs, check_vma=False)
```

time: 306 us -> 56.2 us (0.18)
  waiting for transfers between devices: 169 us -> 24.4 us
  local copies, waits for them, and re-layouts: 58.8 us -> 4.59 us
  other arithmetic: 37.1 us -> 0.71 us
  between operations: 15.2 us -> 0.73 us
  Pallas kernels: 0 us -> 10.8 us
  starting transfers between devices: 22.2 us -> 14.7 us
    psum x1 -> x0, waiting for transfers between devices: 89.1 us -> none  [shards(): summed = lax.psum(masked, 'tm')]
    ppermute x17 -> x13, waiting for transfers between devices: 80.3 us -> 24.4 us  [the longest x9 19.4 us: paired(): return lax.ppermute(value, 'tm', [(s, s ^ stride) for s in range(count)])]
    reshape x5 -> x0, local copies, waits for them, and re-layouts: 41.8 us -> none  [the longest x2 38.2 us: restrict(): field.reshape(field.shape[:-2] + (field.shape[-2] // 2, 2, field.shape[-1...]
    reduce_sum x3 -> x0, other arithmetic: 16.2 us -> none  [the longest x2 14.7 us: restrict(): return shaped.mean(axis=(-3, -1))]
    pallas_call x0 -> x5, Pallas kernels: none -> 10.8 us  [call(): pl.pallas_call(body, out_shape=[jax.ShapeDtypeStruct(shape, jnp.float32)...]
    neg x90 -> x0, other arithmetic: 7.64 us -> none  [the longest x30 6.69 us: divergence(): return flux_x - west + flux_y - south]
    ppermute x17 -> x13, starting transfers between devices: 22.1 us -> 14.7 us  [the longest x9 8.59 us: paired(): return lax.ppermute(value, 'tm', [(s, s ^ stride) for s in range(count)])]
    add x17 -> x3, other arithmetic: 5.19 us -> 0.03 us  [the longest x1 0.02 us: shards(): mine = mine + paired(mine, 4) + paired(mine, 8) + paired(mine, 12)]
  transfers between devices with their start and end apart: 18 -> 13, of which waited for: 17 -> 10; matrix products, arithmetic and copies ran while one was open for 10% -> 0% of each run, Pallas kernels for 0% -> 4%
where the time goes in v1:
time: 56.2 us; the launch traced here: 56 us
  waiting for transfers between devices  24.4 us (43%)
  starting transfers between devices  14.7 us (26%)
  Pallas kernels  10.8 us (19%)
  local copies, waits for them, and re-layouts  4.59 us (8%)
  between operations  0.73 us (1%)
  other arithmetic  0.71 us (1%)
    ppermute x9, waiting for transfers between devices, paired(): return lax.ppermute(value, 'tm', [(s, s ^ stride) for s in range(count)])  19.4 us
    pallas_call x5, Pallas kernels, call(): pl.pallas_call(body, out_shape=[jax.ShapeDtypeStruct(shape, jnp.float32)...  10.8 us
    ppermute x9, starting transfers between devices, paired(): return lax.ppermute(value, 'tm', [(s, s ^ stride) for s in range(count)])  8.59 us
    ppermute x3, waiting for transfers between devices, back(): lax.ppermute(value, 'tm', [(s, (s - stride) % count) for s in range(count)])  5.01 us
    ppermute x3, starting transfers between devices, back(): lax.ppermute(value, 'tm', [(s, (s - stride) % count) for s in range(count)])  4.87 us
    unnamed x14, local copies, waits for them, and re-layouts  4.59 us
    ppermute x1, starting transfers between devices, shards(): lax.ppermute(initial, 'tm', [(s, s - 1) for s in range(1, count)])  1.28 us
  transfers between devices with their start and end apart: 13, of which 10 were waited for; matrix products, arithmetic and copies ran while one was open for 0% of the time, Pallas kernels for 4%

profile of v1, /device:TPU:0, one launch (start us, length us, event | category | flops | bytes accessed | tf_op | source)
XLA Modules:
  0.0 56.0 jit_solution(11626379345432435465)
XLA Ops:
  0.6 0.0 copy-start
  0.6 1.2 %copy-done = f32[8,16,2048]{2,1,0:T(8,128)S(1)} copy-done((f32[8,16,2048]{2,1,0:T(8,128)S(1)}, f32[8,16,2048]{2,1,0:T(8,128)}, u32[]{:S(2)}) %copy-start) | copy-done | bytes 1048600
  1.9 0.0 copy-start.3
  1.9 0.9 %copy-done.3 = s32[16,2048]{1,0:T(8,128)S(1)} copy-done((s32[16,2048]{1,0:T(8,128)S(1)}, s32[16,2048]{1,0:T(8,128)}, u32[]{:S(2)}) %copy-start.3) | copy-done | bytes 131096
  2.8 0.0 copy-start.5
  2.8 0.9 %copy-done.5 = s32[16,2048]{1,0:T(8,128)S(1)} copy-done((s32[16,2048]{1,0:T(8,128)S(1)}, s32[16,2048]{1,0:T(8,128)}, u32[]{:S(2)}) %copy-start.5) | copy-done | bytes 131096
  3.7 0.0 copy-start.6
  3.7 0.7 %copy-done.6 = f32[16]{0:T(128)S(1)} copy-done((f32[16]{0:T(128)S(1)}, f32[16]{0:T(128)}, u32[]{:S(2)}) %copy-start.6) | copy-done | bytes 88
  4.3 0.0 copy-start.1
  4.3 0.0 copy-start.2
  4.3 4.5 %shard_map.77 = (f32[6,8,640]{2,1,0:T(8,128)S(1)}, f32[6,8,640]{2,1,0:T(8,128)S(1)}, f32[2,16,2048]{2,1,0:T(8,128)S(1)}, f32[2,8,640]{2,1,0:T(8,128)S(1)}) custom-call(f32[16]{0:T(128)S(1)} %copy-done.6, s32[16,2048]{1,0:T(8,128)S(1)} %copy-done.5, s32[16,2048]{1,0:T(8,128)S(1)} %copy-done.3, f32[1,3,16,2048]{3,2,1,0:T(8,128)} %initial.3, ...), custom_call_target="tpu_custom_call" | custom-call | tf_op jit(solution)/shard_map/pallas_call | solution.py:294
  8.9 0.5 collective-permute-start
  9.4 1.3 %collective-permute-start.6 = (f32[1,3,16,2048]{3,2,1,0:T(8,128)}, f32[1,3,16,2048]{3,2,1,0:T(8,128)S(1)}, u32[]{:S(2)}, u32[]{:S(2)}) collective-permute-start(f32[1,3,16,2048]{3,2,1,0:T(8,128)} %initial.3), channel_id=1, source_target_pairs={{1,0},{2,1},{3,2},{4,3},{5,4},{6,5},{7,6},{8,7},{9,8},{10,9},{11,1... | collective-permute-start | bytes 1179656 | tf_op jit(solution)/shard_map/ppermute | solution.py:317
  10.7 0.0 collective-permute-done.got.refs_4_
  10.7 0.2 shard_map.78.own.refs_5_
  10.8 3.2 %collective-permute-start.1 = (f32[6,8,640]{2,1,0:T(8,128)S(1)}, f32[6,8,640]{2,1,0:T(8,128)S(1)}, u32[]{:S(2)}, u32[]{:S(2)}) collective-permute-start(f32[6,8,640]{2,1,0:T(8,128)S(1)} %shard_map.78.own.refs_5_), channel_id=1, source_target_pairs={{0,2},{1,3},{2,0},{3,1},{4,6},{5,7},{6,4},{7,5},{8,10},{9,11},{10,... | collective-permute-start | bytes 368648 | tf_op jit(solution)/shard_map/ppermute | solution.py:312
  14.0 8.2 %collective-permute-done.1.got.refs_6_ = f32[6,8,640]{2,1,0:T(8,128)S(1)} collective-permute-done((f32[6,8,640]{2,1,0:T(8,128)S(1)}, f32[6,8,640]{2,1,0:T(8,128)S(1)}, u32[]{:S(2)}, u32[]{:S(2)}) %collective-permute-start.1) | collective-permute-done | bytes 122912 | tf_op jit(solution)/shard_map/ppermute | solution.py:312
  22.2 0.3 shard_map.79
  22.5 3.9 %collective-permute-start.2 = (f32[6,8,640]{2,1,0:T(8,128)S(1)}, f32[6,8,640]{2,1,0:T(8,128)S(1)}, u32[]{:S(2)}, u32[]{:S(2)}) collective-permute-start(f32[6,8,640]{2,1,0:T(8,128)S(1)} %get-tuple-element.16), channel_id=1, source_target_pairs={{0,12},{1,13},{2,14},{3,15},{4,0},{5,1},{6,2},{7,3},{8,4},{9,5},{1... | collective-permute-start | bytes 368648 | tf_op jit(solution)/shard_map/ppermute | solution.py:315
  26.4 0.0 collective-permute-start.3
  26.4 1.0 %collective-permute-start.4 = (f32[3,8,640]{2,1,0:T(8,128)S(1)}, f32[3,8,640]{2,1,0:T(8,128)S(1)}, u32[]{:S(2)}, u32[]{:S(2)}) collective-permute-start(f32[3,8,640]{2,1,0:T(8,128)S(1)} %get-tuple-element.17), channel_id=1, source_target_pairs={{0,4},{1,5},{2,6},{3,7},{4,8},{5,9},{6,10},{7,11},{8,12},{9,13},{1... | collective-permute-start | bytes 184328 | tf_op jit(solution)/shard_map/ppermute | solution.py:315
  27.4 4.1 %collective-permute-done.3.refs_1_ = f32[3,8,640]{2,1,0:T(8,128)S(1)} collective-permute-done((f32[3,8,640]{2,1,0:T(8,128)S(1)}, f32[3,8,640]{2,1,0:T(8,128)S(1)}, u32[]{:S(2)}, u32[]{:S(2)}) %collective-permute-start.3) | collective-permute-done | bytes 61472 | tf_op jit(solution)/shard_map/ppermute | solution.py:315
  31.5 0.9 %collective-permute-done.4.refs_2_ = f32[3,8,640]{2,1,0:T(8,128)S(1)} collective-permute-done((f32[3,8,640]{2,1,0:T(8,128)S(1)}, f32[3,8,640]{2,1,0:T(8,128)S(1)}, u32[]{:S(2)}, u32[]{:S(2)}) %collective-permute-start.4) | collective-permute-done | bytes 61472 | tf_op jit(solution)/shard_map/ppermute | solution.py:315
  32.4 0.0 collective-permute-done.2.refs_0_
  32.4 1.6 %shard_map.80 = (f32[6,8,512]{2,1,0:T(8,128)S(1)}, f32[6,8,512]{2,1,0:T(8,128)S(1)}) custom-call(f32[6,8,640]{2,1,0:T(8,128)S(1)} %collective-permute-done.2.refs_0_, f32[3,8,640]{2,1,0:T(8,128)S(1)} %collective-permute-done.3.refs_1_, f32[3,8,640]{2,1,0:T(8,128)S(1)} %collective-permute-done.4.refs_2_, f32[6,8,640]{2,1,0:T(8,128)S(1)} %get-tuple-element.13.own.refs_3_, ...), custom_call_target="tpu_custom_call" | custom-call | tf_op jit(solution)/shard_map/pallas_call | solution.py:294
  34.1 0.1 collective-permute-start.5
  34.1 0.0 collective-permute-done.6.following
  34.1 1.3 %collective-permute-done.5.got = f32[6,8,512]{2,1,0:T(8,128)S(1)} collective-permute-done((f32[6,8,512]{2,1,0:T(8,128)S(1)}, f32[6,8,512]{2,1,0:T(8,128)S(1)}, u32[]{:S(2)}, u32[]{:S(2)}) %collective-permute-start.5) | collective-permute-done | bytes 98336 | tf_op jit(solution)/shard_map/ppermute | solution.py:312
  35.4 0.0 copy-done.1
  35.4 0.0 copy-done.2
  35.4 0.0 copy-start.4
  35.4 0.9 %copy-done.4 = s32[16,2048]{1,0:T(8,128)S(1)} copy-done((s32[16,2048]{1,0:T(8,128)S(1)}, s32[16,2048]{1,0:T(8,128)}, u32[]{:S(2)}) %copy-start.4) | copy-done | bytes 131096
  36.3 4.2 %shard_map.81 = (f32[1,3,16,2048]{3,2,1,0:T(8,128)}, f32[16,1024]{1,0:T(8,128)S(1)}, f32[16,1024]{1,0:T(8,128)S(1)}) custom-call(f32[6,8,512]{2,1,0:T(8,128)S(1)} %get-tuple-element.18.kept, f32[6,8,512]{2,1,0:T(8,128)S(1)} %collective-permute-done.5.got, f32[1,3,16,2048]{3,2,1,0:T(8,128)} %initial.3, ...), custom_call_target="tpu_custom_call" | custom-call | tf_op jit(solution)/shard_map/pallas_call | solution.py:294
  40.5 0.2 collective-permute-start.7
  40.7 1.1 %collective-permute-done.7 = f32[16,1024]{1,0:T(8,128)S(1)} collective-permute-done((f32[16,1024]{1,0:T(8,128)S(1)}, f32[16,1024]{1,0:T(8,128)S(1)}, u32[]{:S(2)}, u32[]{:S(2)}) %collective-permute-start.7) | collective-permute-done | bytes 65568 | tf_op jit(solution)/shard_map/ppermute | solution.py:312
  41.8 1.0 %collective-permute-start.8 = (f32[16,1024]{1,0:T(8,128)S(1)}, f32[16,1024]{1,0:T(8,128)S(1)}, u32[]{:S(2)}, u32[]{:S(2)}) collective-permute-start(f32[16,1024]{1,0:T(8,128)S(1)} %add.15), channel_id=1, source_target_pairs={{0,2},{1,3},{2,0},{3,1},{4,6},{5,7},{6,4},{7,5},{8,10},{9,11},{10,... | collective-permute-start | bytes 196616 | tf_op jit(solution)/shard_map/ppermute | solution.py:312
  42.8 3.3 %collective-permute-done.8 = f32[16,1024]{1,0:T(8,128)S(1)} collective-permute-done((f32[16,1024]{1,0:T(8,128)S(1)}, f32[16,1024]{1,0:T(8,128)S(1)}, u32[]{:S(2)}, u32[]{:S(2)}) %collective-permute-start.8) | collective-permute-done | bytes 65568 | tf_op jit(solution)/shard_map/ppermute | solution.py:312
  46.1 1.4 %collective-permute-start.10 = (f32[16,1024]{1,0:T(8,128)S(1)}, f32[16,1024]{1,0:T(8,128)S(1)}, u32[]{:S(2)}, u32[]{:S(2)}) collective-permute-start(f32[16,1024]{1,0:T(8,128)S(1)} %add.16), channel_id=1, source_target_pairs={{0,8},{1,9},{2,10},{3,11},{4,12},{5,13},{6,14},{7,15},{8,0},{9,1},... | collective-permute-start | bytes 196616 | tf_op jit(solution)/shard_map/ppermute | solution.py:312
  47.5 1.3 %collective-permute-start.11 = (f32[16,1024]{1,0:T(8,128)S(1)}, f32[16,1024]{1,0:T(8,128)S(1)}, u32[]{:S(2)}, u32[]{:S(2)}) collective-permute-start(f32[16,1024]{1,0:T(8,128)S(1)} %add.16), channel_id=1, source_target_pairs={{0,12},{1,13},{2,14},{3,15},{4,8},{5,9},{6,10},{7,11},{8,4},{9,5},... | collective-permute-start | bytes 196616 | tf_op jit(solution)/shard_map/ppermute | solution.py:312
  48.8 0.9 %collective-permute-start.9 = (f32[16,1024]{1,0:T(8,128)S(1)}, f32[16,1024]{1,0:T(8,128)S(1)}, u32[]{:S(2)}, u32[]{:S(2)}) collective-permute-start(f32[16,1024]{1,0:T(8,128)S(1)} %add.16), channel_id=1, source_target_pairs={{0,4},{1,5},{2,6},{3,7},{4,0},{5,1},{6,2},{7,3},{8,12},{9,13},{10,... | collective-permute-start | bytes 196616 | tf_op jit(solution)/shard_map/ppermute | solution.py:312
  49.7 2.9 %collective-permute-done.10 = f32[16,1024]{1,0:T(8,128)S(1)} collective-permute-done((f32[16,1024]{1,0:T(8,128)S(1)}, f32[16,1024]{1,0:T(8,128)S(1)}, u32[]{:S(2)}, u32[]{:S(2)}) %collective-permute-start.10) | collective-permute-done | bytes 65568 | tf_op jit(solution)/shard_map/ppermute | solution.py:312
  52.6 1.1 %collective-permute-done.11 = f32[16,1024]{1,0:T(8,128)S(1)} collective-permute-done((f32[16,1024]{1,0:T(8,128)S(1)}, f32[16,1024]{1,0:T(8,128)S(1)}, u32[]{:S(2)}, u32[]{:S(2)}) %collective-permute-start.11) | collective-permute-done | bytes 65568 | tf_op jit(solution)/shard_map/ppermute | solution.py:312
  53.7 0.3 collective-permute-done.9
  54.0 0.1 collective-permute-start.12
  54.1 1.2 %collective-permute-done.12 = f32[16,1024]{1,0:T(8,128)S(1)} collective-permute-done((f32[16,1024]{1,0:T(8,128)S(1)}, f32[16,1024]{1,0:T(8,128)S(1)}, u32[]{:S(2)}, u32[]{:S(2)}) %collective-permute-start.12) | collective-permute-done | bytes 65568 | tf_op jit(solution)/shard_map/ppermute | solution.py:312
  55.3 0.7 %pad_maximum_fusion = f32[16,2048]{1,0:T(8,128)} fusion(f32[16,1024]{1,0:T(8,128)S(1)} %get-tuple-element.25, f32[16,1024]{1,0:T(8,128)S(1)} %get-tuple-element.24), kind=kLoop, calls=%fused_computation | loop fusion | flops 32768 | bytes 262144 | tf_op jit(solution)/shard_map/concatenate | solution.py:386
  (4 shorter events, 0.0 us)
Async XLA Ops:
  0.6 1.2 %copy-start = (f32[8,16,2048]{2,1,0:T(8,128)S(1)}, f32[8,16,2048]{2,1,0:T(8,128)}, u32[]{:S(2)}) copy-start(f32[8,16,2048]{2,1,0:T(8,128)} %forcing.3) | copy-start | bytes 3145732
  1.9 0.9 %copy-start.3 = (s32[16,2048]{1,0:T(8,128)S(1)}, s32[16,2048]{1,0:T(8,128)}, u32[]{:S(2)}) copy-start(s32[16,2048]{1,0:T(8,128)} %wet.3) | copy-start | bytes 393220
  2.8 0.9 %copy-start.5 = (s32[16,2048]{1,0:T(8,128)S(1)}, s32[16,2048]{1,0:T(8,128)}, u32[]{:S(2)}) copy-start(s32[16,2048]{1,0:T(8,128)} %levels.1) | copy-start | bytes 393220
  3.7 0.7 %copy-start.6 = (f32[16]{0:T(128)S(1)}, f32[16]{0:T(128)}, u32[]{:S(2)}) copy-start(f32[16]{0:T(128)} %table.1) | copy-start | bytes 196
  4.3 31.1 %copy-start.1 = (f32[8,16,2048]{2,1,0:T(8,128)S(1)}, f32[8,16,2048]{2,1,0:T(8,128)}, u32[]{:S(2)}) copy-start(f32[8,16,2048]{2,1,0:T(8,128)} %forcing.3) | copy-start | bytes 3145732
  4.3 31.1 %copy-start.2 = (f32[8,2,16,2048]{3,2,1,0:T(8,128)S(1)}, f32[8,2,16,2048]{3,2,1,0:T(8,128)}, u32[]{:S(2)}) copy-start(f32[8,2,16,2048]{3,2,1,0:T(8,128)} %velocity.1) | copy-start | bytes 6291460
  8.9 1.8 %collective-permute-start = (f32[6,8,640]{2,1,0:T(8,128)S(1)}, f32[6,8,640]{2,1,0:T(8,128)S(1)}, u32[]{:S(2)}, u32[]{:S(2)}) collective-permute-start(f32[6,8,640]{2,1,0:T(8,128)S(1)} %get-tuple-element.14), channel_id=1, source_target_pairs={{0,1},{1,0},{2,3},{3,2},{4,5},{5,4},{6,7},{7,6},{8,9},{9,8},{10,11... | collective-permute-start | bytes 368648 | tf_op jit(solution)/shard_map/ppermute | solution.py:312
  9.4 24.8 %collective-permute-start.6 = (f32[1,3,16,2048]{3,2,1,0:T(8,128)}, f32[1,3,16,2048]{3,2,1,0:T(8,128)S(1)}, u32[]{:S(2)}, u32[]{:S(2)}) collective-permute-start(f32[1,3,16,2048]{3,2,1,0:T(8,128)} %initial.3), channel_id=1, source_target_pairs={{1,0},{2,1},{3,2},{4,3},{5,4},{6,5},{7,6},{8,7},{9,8},{10,9},{11,1... | collective-permute-start | bytes 1179656 | tf_op jit(solution)/shard_map/ppermute | solution.py:317
  10.8 11.4 %collective-permute-start.1 = (f32[6,8,640]{2,1,0:T(8,128)S(1)}, f32[6,8,640]{2,1,0:T(8,128)S(1)}, u32[]{:S(2)}, u32[]{:S(2)}) collective-permute-start(f32[6,8,640]{2,1,0:T(8,128)S(1)} %shard_map.78.own.refs_5_), channel_id=1, source_target_pairs={{0,2},{1,3},{2,0},{3,1},{4,6},{5,7},{6,4},{7,5},{8,10},{9,11},{10,... | collective-permute-start | bytes 368648 | tf_op jit(solution)/shard_map/ppermute | solution.py:312
  22.5 9.9 %collective-permute-start.2 = (f32[6,8,640]{2,1,0:T(8,128)S(1)}, f32[6,8,640]{2,1,0:T(8,128)S(1)}, u32[]{:S(2)}, u32[]{:S(2)}) collective-permute-start(f32[6,8,640]{2,1,0:T(8,128)S(1)} %get-tuple-element.16), channel_id=1, source_target_pairs={{0,12},{1,13},{2,14},{3,15},{4,0},{5,1},{6,2},{7,3},{8,4},{9,5},{1... | collective-permute-start | bytes 368648 | tf_op jit(solution)/shard_map/ppermute | solution.py:315
  26.4 5.1 %collective-permute-start.3 = (f32[3,8,640]{2,1,0:T(8,128)S(1)}, f32[3,8,640]{2,1,0:T(8,128)S(1)}, u32[]{:S(2)}, u32[]{:S(2)}) collective-permute-start(f32[3,8,640]{2,1,0:T(8,128)S(1)} %get-tuple-element.17), channel_id=1, source_target_pairs={{0,8},{1,9},{2,10},{3,11},{4,12},{5,13},{6,14},{7,15},{8,0},{9,1},... | collective-permute-start | bytes 184328 | tf_op jit(solution)/shard_map/ppermute | solution.py:315
  26.4 6.0 %collective-permute-start.4 = (f32[3,8,640]{2,1,0:T(8,128)S(1)}, f32[3,8,640]{2,1,0:T(8,128)S(1)}, u32[]{:S(2)}, u32[]{:S(2)}) collective-permute-start(f32[3,8,640]{2,1,0:T(8,128)S(1)} %get-tuple-element.17), channel_id=1, source_target_pairs={{0,4},{1,5},{2,6},{3,7},{4,8},{5,9},{6,10},{7,11},{8,12},{9,13},{1... | collective-permute-start | bytes 184328 | tf_op jit(solution)/shard_map/ppermute | solution.py:315
  34.1 1.4 %collective-permute-start.5 = (f32[6,8,512]{2,1,0:T(8,128)S(1)}, f32[6,8,512]{2,1,0:T(8,128)S(1)}, u32[]{:S(2)}, u32[]{:S(2)}) collective-permute-start(f32[6,8,512]{2,1,0:T(8,128)S(1)} %get-tuple-element.19), channel_id=1, source_target_pairs={{0,1},{1,0},{2,3},{3,2},{4,5},{5,4},{6,7},{7,6},{8,9},{9,8},{10,11... | collective-permute-start | bytes 294920 | tf_op jit(solution)/shard_map/ppermute | solution.py:312
  35.4 0.9 %copy-start.4 = (s32[16,2048]{1,0:T(8,128)S(1)}, s32[16,2048]{1,0:T(8,128)}, u32[]{:S(2)}) copy-start(s32[16,2048]{1,0:T(8,128)} %wet.3) | copy-start | bytes 393220
  40.5 1.3 %collective-permute-start.7 = (f32[16,1024]{1,0:T(8,128)S(1)}, f32[16,1024]{1,0:T(8,128)S(1)}, u32[]{:S(2)}, u32[]{:S(2)}) collective-permute-start(f32[16,1024]{1,0:T(8,128)S(1)} %get-tuple-element.23), channel_id=1, source_target_pairs={{0,1},{1,0},{2,3},{3,2},{4,5},{5,4},{6,7},{7,6},{8,9},{9,8},{10,11... | collective-permute-start | bytes 196616 | tf_op jit(solution)/shard_map/ppermute | solution.py:312
  41.8 4.3 %collective-permute-start.8 = (f32[16,1024]{1,0:T(8,128)S(1)}, f32[16,1024]{1,0:T(8,128)S(1)}, u32[]{:S(2)}, u32[]{:S(2)}) collective-permute-start(f32[16,1024]{1,0:T(8,128)S(1)} %add.15), channel_id=1, source_target_pairs={{0,2},{1,3},{2,0},{3,1},{4,6},{5,7},{6,4},{7,5},{8,10},{9,11},{10,... | collective-permute-start | bytes 196616 | tf_op jit(solution)/shard_map/ppermute | solution.py:312
  46.1 6.5 %collective-permute-start.10 = (f32[16,1024]{1,0:T(8,128)S(1)}, f32[16,1024]{1,0:T(8,128)S(1)}, u32[]{:S(2)}, u32[]{:S(2)}) collective-permute-start(f32[16,1024]{1,0:T(8,128)S(1)} %add.16), channel_id=1, source_target_pairs={{0,8},{1,9},{2,10},{3,11},{4,12},{5,13},{6,14},{7,15},{8,0},{9,1},... | collective-permute-start | bytes 196616 | tf_op jit(solution)/shard_map/ppermute | solution.py:312
  47.5 6.2 %collective-permute-start.11 = (f32[16,1024]{1,0:T(8,128)S(1)}, f32[16,1024]{1,0:T(8,128)S(1)}, u32[]{:S(2)}, u32[]{:S(2)}) collective-permute-start(f32[16,1024]{1,0:T(8,128)S(1)} %add.16), channel_id=1, source_target_pairs={{0,12},{1,13},{2,14},{3,15},{4,8},{5,9},{6,10},{7,11},{8,4},{9,5},... | collective-permute-start | bytes 196616 | tf_op jit(solution)/shard_map/ppermute | solution.py:312
  48.8 5.2 %collective-permute-start.9 = (f32[16,1024]{1,0:T(8,128)S(1)}, f32[16,1024]{1,0:T(8,128)S(1)}, u32[]{:S(2)}, u32[]{:S(2)}) collective-permute-start(f32[16,1024]{1,0:T(8,128)S(1)} %add.16), channel_id=1, source_target_pairs={{0,4},{1,5},{2,6},{3,7},{4,0},{5,1},{6,2},{7,3},{8,12},{9,13},{10,... | collective-permute-start | bytes 196616 | tf_op jit(solution)/shard_map/ppermute | solution.py:312
  54.0 1.3 %collective-permute-start.12 = (f32[16,1024]{1,0:T(8,128)S(1)}, f32[16,1024]{1,0:T(8,128)S(1)}, u32[]{:S(2)}, u32[]{:S(2)}) collective-permute-start(f32[16,1024]{1,0:T(8,128)S(1)} %add_add_fusion), channel_id=1, source_target_pairs={{0,1},{1,0},{2,3},{3,2},{4,5},{5,4},{6,7},{7,6},{8,9},{9,8},{10,11... | collective-permute-start | bytes 196616 | tf_op jit(solution)/shard_map/ppermute | solution.py:312

commit v2 on v1

--- a/solution.py
+++ b/solution.py
@@ -10,7 +10,11 @@
 COURANT = 0.06
 LANES = 128
 VMEM = pl.BlockSpec(memory_space=pltpu.VMEM)
-SMEM = pl.BlockSpec(memory_space=pltpu.SMEM)
+HBM = pl.BlockSpec(memory_space=pltpu.HBM)
+ANY = pl.BlockSpec(memory_space=pl.ANY)
+PREPARE_COST = 40_000_000
+BASE_COST = 8_000_000
+CORRECT_COST = 4_000_000
 EXACT = lax.Precision.HIGHEST
 
 
@@ -33,31 +37,123 @@
 
 
 def fine_step(s, e, n, face_x, face_y):
-    slope_x = roll(s, -1, 1) - s
-    slope_y = roll(s, -1, 0) - s
-    e = e + face_x * slope_x
-    n = n + face_y * slope_y
-    s = s + ((e - roll(e, 1, 1)) + (n - roll(n, 1, 0)))
+    slope_x = [roll(v, -1, 1) - v for v in s]
+    slope_y = [s[1] - s[0], roll(s[0], -1, 0) - s[1]]
+    e = [v + f * d for v, f, d in zip(e, face_x, slope_x)]
+    n = [v + f * d for v, f, d in zip(n, face_y, slope_y)]
+    flow_y = [n[0] - roll(n[1], 1, 0), n[1] - n[0]]
+    s = [v + ((x - roll(x, 1, 1)) + y) for v, x, y in zip(s, e, flow_y)]
     return s, e, n, slope_x, slope_y
 
 
+def inside_x(pair):
+    cols = pair[0].shape[1]
+    keep = index_of(pair[0].shape, 1) < cols - 1
+    return [jnp.where(keep, v, 0.0) for v in pair]
+
+
+def inside_y(pair):
+    rows = pair[1].shape[0]
+    return [pair[0], jnp.where(index_of(pair[1].shape, 0) < rows - 1, pair[1], 0.0)]
+
+
+def rows_of(ref, *at):
+    half = ref.shape[-2] // 2
+    return [
+        jnp.concatenate(
+            [ref[(v, *at, pl.ds(parity, half, stride=2), slice(None))] for v in range(ref.shape[0])], axis=1
+        )
+        for parity in range(2)
+    ]
+
+
+def spread_copies(source, stage, sem):
+    lead = (slice(None),) * (len(source.shape) - 1)
+    return [
+        pltpu.make_async_copy(source.at[(*lead, pl.ds(v * LANES, LANES))], stage.at[v], sem)
+        for v in range(stage.shape[0])
+    ]
+
+
+def wait_all(stage, sem):
+    pltpu.make_async_copy(stage, stage, sem).wait()
+
+
+def thirds(value):
+    high = value.astype(jnp.bfloat16)
+    rest = value - high.astype(jnp.float32)
+    mid = rest.astype(jnp.bfloat16)
+    low = (rest - mid.astype(jnp.float32)).astype(jnp.bfloat16)
+    return jnp.concatenate([high, mid, low], axis=1)
+
+
+def stacked(fields):
+    rows = sum(field.shape[0] for field in fields)
+    pad = -rows % 16
+    if pad:
+        fields = list(fields) + [jnp.zeros((pad, fields[0].shape[1]), jnp.float32)]
+    return jnp.concatenate(fields, axis=0)
+
+
+def restrict_pairs(pairs):
+    half, cols = pairs[0][0].shape
+    sums = stacked([even + odd for even, odd in pairs])
+    gather = pair_matrix((2 * LANES, LANES), 0, 0.25).astype(jnp.bfloat16)
+    gather = jnp.concatenate([gather] * 3, axis=0)
+    merged = jnp.concatenate(
+        [
+            jnp.dot(thirds(sums[:, c : c + 2 * LANES]), gather, preferred_element_type=jnp.float32)
+            for c in range(0, cols, 2 * LANES)
+        ],
+        axis=1,
+    )
+    return [merged[i * half : (i + 1) * half] for i in range(len(pairs))]
+
+
+def prolong_columns(fields):
+    half, cols = fields[0].shape
+    rows = stacked(fields)
+    spread = pair_matrix((LANES, 2 * LANES), 1, 1.0).astype(jnp.bfloat16)
+    spread = jnp.concatenate([spread] * 3, axis=0)
+    merged = jnp.concatenate(
+        [
+            jnp.dot(thirds(rows[:, c : c + LANES]), spread, preferred_element_type=jnp.float32)
+            for c in range(0, cols, LANES)
+        ],
+        axis=1,
+    )
+    return [merged[i * half : (i + 1) * half] for i in range(len(fields))]
+
+
 def coarse_step(fields, face_x, face_y):
+    return power(fields, 1, face_x, face_y)
+
+
+def power(fields, count, face_x, face_y):
+    if count == 0:
+        return fields
     s, e, n = fields
     rows, cols = s.shape
-    e = e + face_x * (roll(s, -1, 1) - s)
-    n = n + face_y * (roll(s, -1, 0) - s)
-    e_in = jnp.where(index_of(s.shape, 1) < cols - 1, e, 0.0)
-    n_in = jnp.where(index_of(s.shape, 0) < rows - 1, n, 0.0)
-    s = s + ((e_in - roll(e_in, 1, 1)) + (n_in - roll(n_in, 1, 0)))
-    return s, e, n
-
-
-def power(fields, count, face_x, face_y):
+    inner_x = index_of(s.shape, 1) < cols - 1
+    inner_y = index_of(s.shape, 0) < rows - 1
+    e_in, n_in = jnp.where(inner_x, e, 0.0), jnp.where(inner_y, n, 0.0)
+    e_edge, n_edge = e - e_in, n - n_in
+    face_x = jnp.where(inner_x, face_x, 0.0)
+
+    def body(_, carried):
+        s, e, n = carried
+        e = e + face_x * (roll(s, -1, 1) - s)
+        n = n + face_y * (roll(s, -1, 0) - s)
+        return s + ((e - roll(e, 1, 1)) + (n - roll(n, 1, 0))), e, n
+
+    carried = (s, e_in, n_in)
     if count <= 4:
-        for _ in range(count):
-            fields = coarse_step(fields, face_x, face_y)
-        return fields
-    return lax.fori_loop(0, count, lambda _, f: coarse_step(f, face_x, face_y), fields)
+        for step in range(count):
+            carried = body(step, carried)
+    else:
+        carried = lax.fori_loop(0, count, body, carried)
+    s, e, n = carried
+    return s, e + e_edge, n + n_edge
 
 
 def add(a, b):
@@ -88,18 +184,6 @@
 
 def product(a, b):
     return jnp.dot(a, b, precision=EXACT, preferred_element_type=jnp.float32)
-
-
-def restrict_all(fields):
-    rows, cols = fields[0].shape
-    half = rows // 2
-    stacked = jnp.concatenate(fields, axis=0)
-    gather = pair_matrix((2 * LANES, LANES), 0, 0.25)
-    merged = jnp.concatenate(
-        [product(stacked[:, c : c + 2 * LANES], gather) for c in range(0, cols, 2 * LANES)], axis=1
-    )
-    merged = product(pair_matrix((stacked.shape[0] // 2, stacked.shape[0]), 1, 1.0), merged)
-    return [merged[i * half : (i + 1) * half] for i in range(len(fields))]
 
 
 def prolong_all(fields):
@@ -113,36 +197,69 @@
     return [merged[2 * i * half : 2 * (i + 1) * half] for i in range(len(fields))]
 
 
-def prepare(table, levels, wet, initial, forcing, own, sent, fine_faces, coarse_faces):
-    rows, cols = levels.shape
+def prepare(
+    table_in,
+    levels,
+    wet,
+    initial,
+    forcing,
+    own,
+    sent,
+    planes,
+    coarse_faces,
+    table,
+    stage_l,
+    stage_w,
+    stage_i,
+    stage_f,
+    sems,
+):
+    load_table = pltpu.make_async_copy(table_in, table, sems.at[4])
+    load_table.start()
+    sources = ((levels, stage_l), (wet, stage_w), (initial.at[0], stage_i), (forcing, stage_f))
+    for i, (source, stage) in enumerate(sources):
+        for copy in spread_copies(source, stage, sems.at[i]):
+            copy.start()
     steps = forcing.shape[0]
     width = own.shape[2]
-    coarse_cols = cols // 2
-    level = levels[...]
-    depth = jnp.zeros((rows, cols), jnp.float32)
+    coarse_cols = levels.shape[1] // 2
+    load_table.wait()
+    wait_all(stage_l, sems.at[0])
+    level = rows_of(stage_l)
+    depth = [jnp.zeros(v.shape, jnp.float32) for v in level]
     for i in range(table.shape[0]):
-        depth = jnp.where(level == i, table[i], depth)
-    depth = depth * wet[...].astype(jnp.float32)
-    face_x, face_y = faces(depth, COURANT * COURANT)
-    fine_faces[0] = face_x
-    fine_faces[1] = face_y
-    inner_x = index_of((rows, cols), 1) < cols - 1
-    inner_y = index_of((rows, cols), 0) < rows - 1
-
-    s0, e0, n0 = initial[0, 0], initial[0, 1] * COURANT, initial[0, 2] * COURANT
-    s, e, n = s0, jnp.where(inner_x, e0, 0.0), jnp.where(inner_y, n0, 0.0)
+        depth = [jnp.where(v == i, table[i], d) for v, d in zip(level, depth)]
+    wait_all(stage_w, sems.at[1])
+    dry = [v.astype(jnp.float32) for v in rows_of(stage_w)]
+    depth = [d * v for d, v in zip(depth, dry)]
+    half = 0.5 * COURANT * COURANT
+    face_x = inside_x([half * (d + roll(d, -1, 1)) for d in depth])
+    face_y = inside_y([half * (depth[0] + depth[1]), half * (depth[1] + roll(depth[0], -1, 0))])
+    for i, plane in enumerate(face_x + face_y + dry):
+        planes[i] = plane
+
+    wait_all(stage_i, sems.at[2])
+    s0 = rows_of(stage_i, 0)
+    e0 = [v * COURANT for v in rows_of(stage_i, 1)]
+    n0 = [v * COURANT for v in rows_of(stage_i, 2)]
+    e_in, n_in = inside_x(e0), inside_y(n0)
+    s, e, n = s0, e_in, n_in
     for _ in range(steps):
         s, e, n, _, _ = fine_step(s, e, n, face_x, face_y)
-    relaxed = [s, jnp.where(inner_x, e, e0), jnp.where(inner_y, n, n0)]
-
-    s = forcing[steps - 1]
-    e = jnp.zeros_like(s)
-    n = jnp.zeros_like(s)
+    e = [v + (x - y) for v, x, y in zip(e, e0, e_in)]
+    n = [v + (x - y) for v, x, y in zip(n, n0, n_in)]
+    relaxed = [s, e, n]
+
+    wait_all(stage_f, sems.at[3])
+    s = rows_of(stage_f, steps - 1)
+    e = [jnp.zeros_like(v) for v in s]
+    n = e
     for step in reversed(range(steps - 1)):
         s, e, n, _, _ = fine_step(s, e, n, face_x, face_y)
-        s = s + forcing[step]
-    relaxed += [s - s0, e - e0, n - n0, depth]
-    su, eu, nu, sw, ew, nw, coarse_depth = restrict_all(relaxed)
+        s = [v + f for v, f in zip(s, rows_of(stage_f, step))]
+    for pair, start in zip((s, e, n), (s0, e0, n0)):
+        relaxed.append([v - x for v, x in zip(pair, start)])
+    su, eu, nu, sw, ew, nw, coarse_depth = restrict_pairs(relaxed + [depth])
     ratio = steps / 2
     coarse_courant = COURANT * ratio
     cx, cy = faces(coarse_depth, coarse_courant * coarse_courant)
@@ -243,59 +360,118 @@
             sent[3 + i] = c_high[i][:, width - half :]
 
 
-def descend(kept, got, initial, following, forcing, velocity, fine_faces, wet, corrected, mine, other):
-    steps = forcing.shape[0]
-    rows, cols = wet.shape
-    device = lax.axis_index("tm")
-    first = lax.rem(device, 2) == 0
-    unscale = 1.0 / (COURANT * (steps / 2))
+def joined(kept, got, at):
+    first = lax.rem(lax.axis_index("tm"), 2) == 0
     fields = []
-    for i in range(6):
+    for i in range(at, at + 3):
         left = jnp.where(first, kept[i], got[i])
         right = jnp.where(first, got[i], kept[i])
-        field = jnp.concatenate([left, right], axis=1)
-        fields.append(field if i % 3 == 0 else field * unscale)
-    fields = prolong_all(fields)
-    for i in range(3):
-        corrected[0, i] = initial[0, i] + fields[i]
-
+        fields.append(jnp.concatenate([left, right], axis=1))
+    return fields
+
+
+def correct(kept, got, initial_in, corrected, done, initial, sem, *, steps):
+    load = pltpu.make_async_copy(initial_in, initial, sem)
+    load.start()
+    done[...] = jnp.zeros_like(done)
+    unscale = 1.0 / (COURANT * (steps / 2))
+    s, e, n = joined(kept, got, 0)
+    fields = prolong_all([s, e * unscale, n * unscale])
+    load.wait()
+    for i, field in enumerate(fields):
+        corrected[0, i] = initial[0, i] + field
+
+
+def pulled(slopes, dry):
+    grad_x, grad_y = inside_x(slopes[0]), inside_y(slopes[1])
+    across = [grad_y[0] + roll(grad_y[1], 1, 0), grad_y[1] + grad_y[0]]
+    return [
+        (0.5 * COURANT) * ((x + roll(x, 1, 1)) + y) * keep for x, y, keep in zip(grad_x, across, dry)
+    ]
+
+
+def base(order, following, forcing, velocity, planes, flow, grad, stage_i, stage_f, sems):
+    sources = ((following.at[0], stage_i), (forcing, stage_f), (velocity, flow))
+    for i, (source, stage) in enumerate(sources):
+        for copy in spread_copies(source, stage, sems.at[i]):
+            copy.start()
+    steps = forcing.shape[0]
+    device = lax.axis_index("tm")
     there = jnp.where(device + 1 < lax.axis_size("tm"), 1.0, 0.0)
-    inner_x = index_of((rows, cols), 1) < cols - 1
-    inner_y = index_of((rows, cols), 0) < rows - 1
-    s = (following[0, 0] * there) + fields[3]
-    e = jnp.where(inner_x, (following[0, 1] * there + fields[4]) * COURANT, 0.0)
-    n = jnp.where(inner_y, (following[0, 2] * there + fields[5]) * COURANT, 0.0)
-    face_x, face_y = fine_faces[0], fine_faces[1]
-    grad_x = jnp.zeros_like(s)
-    grad_y = jnp.zeros_like(s)
+    face_x, face_y = [planes[0], planes[1]], [planes[2], planes[3]]
+    wait_all(stage_i, sems.at[0])
+    s = [v * there for v in rows_of(stage_i, 0)]
+    e = inside_x([v * (there * COURANT) for v in rows_of(stage_i, 1)])
+    n = inside_y([v * (there * COURANT) for v in rows_of(stage_i, 2)])
+    wait_all(stage_f, sems.at[1])
+    wait_all(flow, sems.at[2])
+    sums = [[jnp.zeros_like(v) for v in s] for _ in range(2)]
     for step in reversed(range(steps)):
-        s, e, n, slope_x, slope_y = fine_step(s, e, n, face_x, face_y)
-        grad_x = grad_x + slope_x * velocity[step, 0]
-        grad_y = grad_y + slope_y * velocity[step, 1]
-        s = s + forcing[step]
-    grad_x = jnp.where(inner_x, grad_x, 0.0)
-    grad_y = jnp.where(inner_y, grad_y, 0.0)
-    grad = (grad_x + roll(grad_x, 1, 1)) + (grad_y + roll(grad_y, 1, 0))
-    grad = (0.5 * COURANT) * grad * wet[...].astype(jnp.float32)
-    half = cols // 2
+        s, e, n, *slopes = fine_step(s, e, n, face_x, face_y)
+        for k in range(2):
+            sums[k] = [a + d * v for a, d, v in zip(sums[k], slopes[k], rows_of(flow, step, k))]
+        if step:
+            s = [v + f for v, f in zip(s, rows_of(stage_f, step))]
+    for i, value in enumerate(pulled(sums, [planes[4], planes[5]])):
+        grad[i] = value
+
+
+def descend(kept, got, flow, planes, grad, mine, other):
+    steps = flow.shape[1]
+    half = mine.shape[2]
+    first = lax.rem(lax.axis_index("tm"), 2) == 0
+    inverse = 1.0 / (steps / 2)
+    s, e, n = prolong_columns(joined(kept, got, 3))
+    e, n = e * inverse, n * inverse
+    s, e, n = [s, s], inside_x([e, e]), inside_y([n, n])
+    face_x, face_y = [planes[0], planes[1]], [planes[2], planes[3]]
+    sums = [[jnp.zeros_like(v) for v in s] for _ in range(2)]
+    for step in reversed(range(steps)):
+        s, e, n, *slopes = fine_step(s, e, n, face_x, face_y)
+        for k in range(2):
+            sums[k] = [a + d * v for a, d, v in zip(sums[k], slopes[k], rows_of(flow, step, k))]
+    total = [grad[i] + v for i, v in enumerate(pulled(sums, [planes[4], planes[5]]))]
 
     @pl.when(first)
     def _():
-        mine[...] = grad[:, :half]
-        other[...] = grad[:, half:]
+        for i in range(2):
+            mine[i] = total[i][:, :half]
+            other[i] = total[i][:, half:]
 
     @pl.when(jnp.logical_not(first))
     def _():
-        mine[...] = grad[:, half:]
-        other[...] = grad[:, :half]
-
-
-def call(body, shapes, operands, specs=None):
+        for i in range(2):
+            mine[i] = total[i][:, half:]
+            other[i] = total[i][:, :half]
+
+
+def plus(a, b, order, out):
+    out[...] = a[...] + b[...]
+
+
+def weave(mine, other, out, stage, sem):
+    first = lax.rem(lax.axis_index("tm"), 2) == 0
+    half = stage.shape[1] // 2
+    blocks = stage.shape[0] // 2
+    for i in range(2):
+        left, right = jnp.where(first, mine[i], other[i]), jnp.where(first, other[i], mine[i])
+        for v in range(blocks):
+            at = slice(v * LANES, (v + 1) * LANES)
+            stage[v, pl.ds(i, half, stride=2), :] = left[:, at]
+            stage[blocks + v, pl.ds(i, half, stride=2), :] = right[:, at]
+    for v in range(2 * blocks):
+        pltpu.make_async_copy(stage.at[v], out.at[:, pl.ds(v * LANES, LANES)], sem).start()
+    wait_all(stage, sem)
+
+
+def call(body, shapes, operands, *, specs=None, outs=None, scratch=(), cost=1000):
     return pl.pallas_call(
         body,
         out_shape=[jax.ShapeDtypeStruct(shape, jnp.float32) for shape in shapes],
         in_specs=specs or [VMEM] * len(operands),
-        out_specs=[VMEM] * len(shapes),
+        out_specs=outs or [VMEM] * len(shapes),
+        scratch_shapes=scratch,
+        cost_estimate=pl.CostEstimate(flops=cost, bytes_accessed=cost, transcendentals=0),
         compiler_params=pltpu.CompilerParams(vmem_limit_bytes=32 * 1024 * 1024),
     )(*operands)
 
@@ -303,10 +479,13 @@
 def shards(initial, velocity, forcing, depth_table, levels, wet_mask):
     count = lax.axis_size("tm")
     rows, cols = levels.shape
+    steps = forcing.shape[0]
     half_rows, half = rows // 2, cols // 4
     halo = -(-count // LANES) * LANES
     width = half + halo
     block = (half_rows, width)
+    blocks = cols // LANES
+    plane = (half_rows, cols)
 
     def paired(value, stride):
         return lax.ppermute(value, "tm", [(s, s ^ stride) for s in range(count)])
@@ -314,12 +493,28 @@
     def back(value, stride):
         return lax.ppermute(value, "tm", [(s, (s - stride) % count) for s in range(count)])
 
+    def stage(*lead, kind=jnp.float32):
+        return pltpu.VMEM((blocks, *lead, rows, LANES), kind)
+
+    initial, velocity, forcing, depth_table, levels, wet_mask = (
+        pltpu.with_memory_space_constraint(value, pltpu.HBM)
+        for value in (initial, velocity, forcing, depth_table, levels, wet_mask)
+    )
     following = lax.ppermute(initial, "tm", [(s, s - 1) for s in range(1, count)])
-    own, sent, fine_faces, coarse_faces = call(
+    own, sent, planes, coarse_faces = call(
         prepare,
-        [(6, *block), (6, *block), (2, rows, cols), (2, *block)],
+        [(6, *block), (6, *block), (6, *plane), (2, *block)],
         [depth_table, levels, wet_mask, initial, forcing],
-        specs=[SMEM] + [VMEM] * 4,
+        specs=[HBM] * 5,
+        scratch=[
+            pltpu.SMEM(depth_table.shape, jnp.float32),
+            stage(kind=jnp.int32),
+            stage(kind=jnp.int32),
+            stage(3),
+            stage(steps),
+            pltpu.SemaphoreType.DMA((5,)),
+        ],
+        cost=PREPARE_COST,
     )
     got = paired(sent, 1)
     (chip,) = call(chip_pair, [(6, *block)], [own, got, coarse_faces])
@@ -345,6 +540,15 @@
             stride *= 2
         far, farther = back(row_t, 2 * per_row), None
 
+    flow, grad = call(
+        base,
+        [(blocks, steps, 2, rows, LANES), (2, *plane)],
+        [row_t, following, forcing, velocity, planes],
+        specs=[ANY, ANY, HBM, HBM, VMEM],
+        scratch=[stage(3), stage(steps), pltpu.SemaphoreType.DMA((3,))],
+        cost=BASE_COST,
+    )
+
     operands = {
         "near": near,
         "far": far,
@@ -360,19 +564,30 @@
     def finish_body(*refs):
         given = dict.fromkeys(operands)
         given.update(zip(names, refs))
-        kept, sent = refs[len(names) :]
+        kept, sent = refs[len(names) + 1 :]
         finish(**given, kept=kept, sent=sent, per_row=per_row, rows_in_all=rows_in_all)
 
-    kept, sent = call(finish_body, [(6, half_rows, half)] * 2, [operands[name] for name in names])
+    kept, sent = call(
+        finish_body,
+        [(6, half_rows, half)] * 2,
+        [operands[name] for name in names] + [grad],
+        specs=[VMEM] * len(names) + [ANY],
+    )
     got = paired(sent, 1)
-    corrected, mine, other = call(
-        descend,
-        [initial.shape, (rows, cols // 2), (rows, cols // 2)],
-        [kept, got, initial, following, forcing, velocity, fine_faces, wet_mask],
+    mine, other = call(
+        descend, [(2, half_rows, cols // 2)] * 2, [kept, got, flow, planes, grad], cost=BASE_COST
     )
     mine = mine + paired(other, 1)
+    corrected, done = call(
+        functools.partial(correct, steps=steps),
+        [initial.shape, (8, LANES)],
+        [kept, got, initial],
+        specs=[VMEM, VMEM, HBM],
+        scratch=[pltpu.VMEM(initial.shape, jnp.float32), pltpu.SemaphoreType.DMA],
+        cost=CORRECT_COST,
+    )
     if per_row == 4:
-        mine = mine + paired(mine, 2)
+        (mine,) = call(plus, [mine.shape], [mine, paired(mine, 2), done], specs=[VMEM, VMEM, ANY])
     if rows_in_all == 4:
         mine = mine + paired(mine, 4) + paired(mine, 8) + paired(mine, 12)
     else:
@@ -380,10 +595,14 @@
         while stride < count:
             mine = mine + paired(mine, stride)
             stride *= 2
-    other = paired(mine, 1)
-    first = lax.rem(lax.axis_index("tm"), 2) == 0
-    left, right = jnp.where(first, mine, other), jnp.where(first, other, mine)
-    return corrected, jnp.concatenate([left, right], axis=1)
+    (gradient,) = call(
+        weave,
+        [(rows, cols)],
+        [mine, paired(mine, 1)],
+        outs=[HBM],
+        scratch=[stage(), pltpu.SemaphoreType.DMA],
+    )
+    return corrected, gradient
 
 
 def solution(mesh):

time: 56.2 us -> 47.8 us (0.85)
  waiting for transfers between devices: 24.4 us -> 15.2 us
  local copies, waits for them, and re-layouts: 4.59 us -> 0.75 us
  Pallas kernels: 10.8 us -> 14.5 us
  starting transfers between devices: 14.7 us -> 16.4 us
  other arithmetic: 0.71 us -> 0.03 us
    ppermute x9, waiting for transfers between devices: 19.4 us -> 14.1 us  [paired(): return lax.ppermute(value, 'tm', [(s, s ^ stride) for s in range(count)])]
    ppermute x3, waiting for transfers between devices: 5.01 us -> 1.09 us  [back(): lax.ppermute(value, 'tm', [(s, (s - stride) % count) for s in range(count)])]
    unnamed x14 -> x2, local copies, waits for them, and re-layouts: 4.59 us -> 0.75 us
    pallas_call x5 -> x9, Pallas kernels: 10.8 us -> 14.5 us  [call(): pl.pallas_call(body, out_shape=[jax.ShapeDtypeStruct(shape, jnp.float32)...]
    ppermute x9, starting transfers between devices: 8.59 us -> 9.75 us  [paired(): return lax.ppermute(value, 'tm', [(s, s ^ stride) for s in range(count)])]
    concatenate x1 -> x0, other arithmetic: 0.67 us -> none  [shards(): return (corrected, jnp.concatenate([left, right], axis=1))]
  transfers between devices with their start and end apart: 13 -> 13, of which waited for: 10 -> 10; matrix products, arithmetic and copies ran while one was open for 0% -> 0% of each run, Pallas kernels for 4% -> 22%
where the time goes in v2:
time: 47.8 us; the launch traced here: 47.6 us
  starting transfers between devices  16.4 us (34%)
  waiting for transfers between devices  15.2 us (32%)
  Pallas kernels  14.5 us (30%)
  local copies, waits for them, and re-layouts  0.75 us (2%)
  between operations  0.71 us (1%)
    pallas_call x9, Pallas kernels, call(): pl.pallas_call(body, out_shape=[jax.ShapeDtypeStruct(shape, jnp.float32)...  14.5 us
    ppermute x9, waiting for transfers between devices, paired(): return lax.ppermute(value, 'tm', [(s, s ^ stride) for s in range(count)])  14.1 us
    ppermute x9, starting transfers between devices, paired(): return lax.ppermute(value, 'tm', [(s, s ^ stride) for s in range(count)])  9.75 us
    ppermute x3, starting transfers between devices, back(): lax.ppermute(value, 'tm', [(s, (s - stride) % count) for s in range(count)])  5.36 us
    ppermute x1, starting transfers between devices, shards(): lax.ppermute(initial, 'tm', [(s, s - 1) for s in range(1, count)])  1.29 us
    ppermute x3, waiting for transfers between devices, back(): lax.ppermute(value, 'tm', [(s, (s - stride) % count) for s in range(count)])  1.09 us
  transfers between devices with their start and end apart: 13, of which 10 were waited for; matrix products, arithmetic and copies ran while one was open for 0% of the time, Pallas kernels for 22%

profile of v2, /device:TPU:0, one launch (start us, length us, event | category | flops | bytes accessed | tf_op | source)
XLA Modules:
  0.0 47.6 jit_solution(8865086519227928162)
XLA Ops:
  0.6 1.3 %collective-permute-start.5 = (f32[1,3,16,2048]{3,2,1,0:T(8,128)}, f32[1,3,16,2048]{3,2,1,0:T(8,128)S(1)}, u32[]{:S(2)}, u32[]{:S(2)}) collective-permute-start(f32[1,3,16,2048]{3,2,1,0:T(8,128)} %initial_in.1), channel_id=1, source_target_pairs={{1,0},{2,1},{3,2},{4,3},{5,4},{6,5},{7,6},{8,7},{9,8},{10,9},{11,1... | collective-permute-start | bytes 1179656 | tf_op jit(solution)/shard_map/ppermute | solution.py:503
  1.9 4.3 %shard_map.77 = (f32[6,8,640]{2,1,0:T(8,128)S(1)}, f32[6,8,640]{2,1,0:T(8,128)S(1)}, f32[6,8,2048]{2,1,0:T(8,128)S(1)}, f32[2,8,640]{2,1,0:T(8,128)S(1)}) custom-call(f32[16]{0:T(128)} %table_in.1, s32[16,2048]{1,0:T(8,128)} %levels.1, s32[16,2048]{1,0:T(8,128)} %wet.1, f32[1,3,16,2048]{3,2,1,0:T(8,128)} %initial_in.1, f32[8,16,2048]{2,1,0:T(8,128)} %forcing.3), custom_call_target="tpu_custom_call" | custom-call | flops 40000000 | bytes 40000000 | tf_op jit(solution)/shard_map/pallas_call | solution.py:468
  6.3 1.2 %collective-permute-start = (f32[6,8,640]{2,1,0:T(8,128)S(1)}, f32[6,8,640]{2,1,0:T(8,128)S(1)}, u32[]{:S(2)}, u32[]{:S(2)}) collective-permute-start(f32[6,8,640]{2,1,0:T(8,128)S(1)} %get-tuple-element.17), channel_id=1, source_target_pairs={{0,1},{1,0},{2,3},{3,2},{4,5},{5,4},{6,7},{7,6},{8,9},{9,8},{10,11... | collective-permute-start | bytes 368648 | tf_op jit(solution)/shard_map/ppermute | solution.py:491
  7.5 1.0 %collective-permute-done.got.refs_4_ = f32[6,8,640]{2,1,0:T(8,128)S(1)} collective-permute-done((f32[6,8,640]{2,1,0:T(8,128)S(1)}, f32[6,8,640]{2,1,0:T(8,128)S(1)}, u32[]{:S(2)}, u32[]{:S(2)}) %collective-permute-start) | collective-permute-done | bytes 122912 | tf_op jit(solution)/shard_map/ppermute | solution.py:491
  8.5 0.2 shard_map.78.own.refs_5_
  8.6 3.0 %collective-permute-start.1 = (f32[6,8,640]{2,1,0:T(8,128)S(1)}, f32[6,8,640]{2,1,0:T(8,128)S(1)}, u32[]{:S(2)}, u32[]{:S(2)}) collective-permute-start(f32[6,8,640]{2,1,0:T(8,128)S(1)} %shard_map.78.own.refs_5_), channel_id=1, source_target_pairs={{0,2},{1,3},{2,0},{3,1},{4,6},{5,7},{6,4},{7,5},{8,10},{9,11},{10,... | collective-permute-start | bytes 368648 | tf_op jit(solution)/shard_map/ppermute | solution.py:491
  11.6 3.8 %collective-permute-done.1.got.refs_6_ = f32[6,8,640]{2,1,0:T(8,128)S(1)} collective-permute-done((f32[6,8,640]{2,1,0:T(8,128)S(1)}, f32[6,8,640]{2,1,0:T(8,128)S(1)}, u32[]{:S(2)}, u32[]{:S(2)}) %collective-permute-start.1) | collective-permute-done | bytes 122912 | tf_op jit(solution)/shard_map/ppermute | solution.py:491
  15.4 0.3 shard_map.79
  15.8 4.3 %collective-permute-start.2 = (f32[6,8,640]{2,1,0:T(8,128)S(1)}, f32[6,8,640]{2,1,0:T(8,128)S(1)}, u32[]{:S(2)}, u32[]{:S(2)}) collective-permute-start(f32[6,8,640]{2,1,0:T(8,128)S(1)} %get-tuple-element.19), channel_id=1, source_target_pairs={{0,12},{1,13},{2,14},{3,15},{4,0},{5,1},{6,2},{7,3},{8,4},{9,5},{1... | collective-permute-start | bytes 368648 | tf_op jit(solution)/shard_map/ppermute | solution.py:494
  20.1 0.0 collective-permute-start.3
  20.1 1.0 %collective-permute-start.4 = (f32[3,8,640]{2,1,0:T(8,128)S(1)}, f32[3,8,640]{2,1,0:T(8,128)S(1)}, u32[]{:S(2)}, u32[]{:S(2)}) collective-permute-start(f32[3,8,640]{2,1,0:T(8,128)S(1)} %get-tuple-element.20.order), channel_id=1, source_target_pairs={{0,4},{1,5},{2,6},{3,7},{4,8},{5,9},{6,10},{7,11},{8,12},{9,13},{1... | collective-permute-start | bytes 184328 | tf_op jit(solution)/shard_map/ppermute | solution.py:494
  21.1 0.0 collective-permute-done.5.following
  21.1 0.0 copy-start
  21.1 0.7 %copy-done = f32[1,3,16,2048]{3,2,1,0:T(8,128)} copy-done((f32[1,3,16,2048]{3,2,1,0:T(8,128)}, f32[1,3,16,2048]{3,2,1,0:T(8,128)S(1)}, u32[]{:S(2)}) %copy-start) | copy-done | bytes 393240
  21.9 3.4 %shard_map.80 = (f32[16,8,2,16,128]{4,3,2,1,0:T(8,128)S(1)}, f32[2,8,2048]{2,1,0:T(8,128)S(1)}) custom-call(f32[3,8,640]{2,1,0:T(8,128)S(1)} %get-tuple-element.20.order, f32[1,3,16,2048]{3,2,1,0:T(8,128)} %copy-done, f32[8,16,2048]{2,1,0:T(8,128)} %forcing.3, f32[8,2,16,2048]{3,2,1,0:T(8,128)} %velocity.1, f32[6,8,2048]{2,1,0:T(8,128)S(1)} %get-tuple-element.21.planes), custom_call_target="tpu_custom_call" | custom-call | flops 8000000 | bytes 8000000 | tf_op jit(solution)/shard_map/pallas_call | solution.py:468
  25.3 1.1 %collective-permute-done.3.refs_1_ = f32[3,8,640]{2,1,0:T(8,128)S(1)} collective-permute-done((f32[3,8,640]{2,1,0:T(8,128)S(1)}, f32[3,8,640]{2,1,0:T(8,128)S(1)}, u32[]{:S(2)}, u32[]{:S(2)}) %collective-permute-start.3) | collective-permute-done | bytes 61472 | tf_op jit(solution)/shard_map/ppermute | solution.py:494
  26.4 0.0 collective-permute-done.4.refs_2_
  26.4 0.0 collective-permute-done.2.refs_0_
  26.4 1.6 %shard_map.81 = (f32[6,8,512]{2,1,0:T(8,128)S(1)}, f32[6,8,512]{2,1,0:T(8,128)S(1)}) custom-call(f32[6,8,640]{2,1,0:T(8,128)S(1)} %collective-permute-done.2.refs_0_, f32[3,8,640]{2,1,0:T(8,128)S(1)} %collective-permute-done.3.refs_1_, f32[3,8,640]{2,1,0:T(8,128)S(1)} %collective-permute-done.4.refs_2_, f32[6,8,640]{2,1,0:T(8,128)S(1)} %get-tuple-element.16.own.refs_3_, ...), custom_call_target="tpu_custom_call" | custom-call | flops 1000 | bytes 1000 | tf_op jit(solution)/shard_map/pallas_call | solution.py:468
  28.0 0.1 collective-permute-start.6
  28.1 1.3 %collective-permute-done.6.got = f32[6,8,512]{2,1,0:T(8,128)S(1)} collective-permute-done((f32[6,8,512]{2,1,0:T(8,128)S(1)}, f32[6,8,512]{2,1,0:T(8,128)S(1)}, u32[]{:S(2)}, u32[]{:S(2)}) %collective-permute-start.6) | collective-permute-done | bytes 98336 | tf_op jit(solution)/shard_map/ppermute | solution.py:491
  29.4 1.7 %shard_map.83 = (f32[2,8,1024]{2,1,0:T(8,128)S(1)}, f32[2,8,1024]{2,1,0:T(8,128)S(1)}) custom-call(f32[6,8,512]{2,1,0:T(8,128)S(1)} %get-tuple-element.23.kept, f32[6,8,512]{2,1,0:T(8,128)S(1)} %collective-permute-done.6.got, f32[16,8,2,16,128]{4,3,2,1,0:T(8,128)S(1)} %get-tuple-element.26.flow, f32[6,8,2048]{2,1,0:T(8,128)S(1)} %get-tuple-element.21.planes, ...), custom_call_target="tpu_custom_call" | custom-call | flops 8000000 | bytes 8000000 | tf_op jit(solution)/shard_map/pallas_call | solution.py:468
  31.1 0.2 collective-permute-start.7
  31.3 1.1 %collective-permute-done.7 = f32[2,8,1024]{2,1,0:T(8,128)S(1)} collective-permute-done((f32[2,8,1024]{2,1,0:T(8,128)S(1)}, f32[2,8,1024]{2,1,0:T(8,128)S(1)}, u32[]{:S(2)}, u32[]{:S(2)}) %collective-permute-start.7) | collective-permute-done | bytes 65568 | tf_op jit(solution)/shard_map/ppermute | solution.py:491
  32.4 1.3 %collective-permute-start.8 = (f32[2,8,1024]{2,1,0:T(8,128)S(1)}, f32[2,8,1024]{2,1,0:T(8,128)S(1)}, u32[]{:S(2)}, u32[]{:S(2)}) collective-permute-start(f32[2,8,1024]{2,1,0:T(8,128)S(1)} %add.12.a), channel_id=1, source_target_pairs={{0,2},{1,3},{2,0},{3,1},{4,6},{5,7},{6,4},{7,5},{8,10},{9,11},{10,... | collective-permute-start | bytes 196616 | tf_op jit(solution)/shard_map/ppermute | solution.py:491
  33.8 2.3 %shard_map.82 = (f32[1,3,16,2048]{3,2,1,0:T(8,128)}, f32[8,128]{1,0:T(8,128)S(1)}) custom-call(f32[6,8,512]{2,1,0:T(8,128)S(1)} %get-tuple-element.23.kept, f32[6,8,512]{2,1,0:T(8,128)S(1)} %collective-permute-done.6.got, f32[1,3,16,2048]{3,2,1,0:T(8,128)} %initial_in.1), custom_call_target="tpu_custom_call" | custom-call | flops 4000000 | bytes 4000000 | tf_op jit(solution)/shard_map/pallas_call | solution.py:468
  36.1 0.7 %collective-permute-done.8.b = f32[2,8,1024]{2,1,0:T(8,128)S(1)} collective-permute-done((f32[2,8,1024]{2,1,0:T(8,128)S(1)}, f32[2,8,1024]{2,1,0:T(8,128)S(1)}, u32[]{:S(2)}, u32[]{:S(2)}) %collective-permute-start.8) | collective-permute-done | bytes 65568 | tf_op jit(solution)/shard_map/ppermute | solution.py:491
  36.8 2.5 %collective-permute-start.10 = (f32[2,8,1024]{2,1,0:T(8,128)S(1)}, f32[2,8,1024]{2,1,0:T(8,128)S(1)}, u32[]{:S(2)}, u32[]{:S(2)}) collective-permute-start(f32[2,8,1024]{2,1,0:T(8,128)S(1)} %shard_map.84), channel_id=1, source_target_pairs={{0,8},{1,9},{2,10},{3,11},{4,12},{5,13},{6,14},{7,15},{8,0},{9,1},... | collective-permute-start | bytes 196616 | tf_op jit(solution)/shard_map/ppermute | solution.py:491
  39.3 1.3 %collective-permute-start.11 = (f32[2,8,1024]{2,1,0:T(8,128)S(1)}, f32[2,8,1024]{2,1,0:T(8,128)S(1)}, u32[]{:S(2)}, u32[]{:S(2)}) collective-permute-start(f32[2,8,1024]{2,1,0:T(8,128)S(1)} %shard_map.84), channel_id=1, source_target_pairs={{0,12},{1,13},{2,14},{3,15},{4,8},{5,9},{6,10},{7,11},{8,4},{9,5},... | collective-permute-start | bytes 196616 | tf_op jit(solution)/shard_map/ppermute | solution.py:491
  40.6 0.0 collective-permute-start.9
  40.6 3.2 %collective-permute-done.10 = f32[2,8,1024]{2,1,0:T(8,128)S(1)} collective-permute-done((f32[2,8,1024]{2,1,0:T(8,128)S(1)}, f32[2,8,1024]{2,1,0:T(8,128)S(1)}, u32[]{:S(2)}, u32[]{:S(2)}) %collective-permute-start.10) | collective-permute-done | bytes 65568 | tf_op jit(solution)/shard_map/ppermute | solution.py:491
  43.8 1.6 %collective-permute-done.11 = f32[2,8,1024]{2,1,0:T(8,128)S(1)} collective-permute-done((f32[2,8,1024]{2,1,0:T(8,128)S(1)}, f32[2,8,1024]{2,1,0:T(8,128)S(1)}, u32[]{:S(2)}, u32[]{:S(2)}) %collective-permute-start.11) | collective-permute-done | bytes 65568 | tf_op jit(solution)/shard_map/ppermute | solution.py:491
  45.5 0.1 collective-permute-done.9
  45.6 0.1 collective-permute-start.12
  45.7 1.2 %collective-permute-done.12.other = f32[2,8,1024]{2,1,0:T(8,128)S(1)} collective-permute-done((f32[2,8,1024]{2,1,0:T(8,128)S(1)}, f32[2,8,1024]{2,1,0:T(8,128)S(1)}, u32[]{:S(2)}, u32[]{:S(2)}) %collective-permute-start.12) | collective-permute-done | bytes 65568 | tf_op jit(solution)/shard_map/ppermute | solution.py:491
  46.9 0.7 %shard_map.85 = f32[16,2048]{1,0:T(8,128)} custom-call(f32[2,8,1024]{2,1,0:T(8,128)S(1)} %add_add_fusion.mine, f32[2,8,1024]{2,1,0:T(8,128)S(1)} %collective-permute-done.12.other), custom_call_target="tpu_custom_call" | custom-call | flops 1000 | bytes 1000 | tf_op jit(solution)/shard_map/pallas_call | solution.py:468
  (3 shorter events, 0.0 us)
Async XLA Ops:
  0.6 20.5 %collective-permute-start.5 = (f32[1,3,16,2048]{3,2,1,0:T(8,128)}, f32[1,3,16,2048]{3,2,1,0:T(8,128)S(1)}, u32[]{:S(2)}, u32[]{:S(2)}) collective-permute-start(f32[1,3,16,2048]{3,2,1,0:T(8,128)} %initial_in.1), channel_id=1, source_target_pairs={{1,0},{2,1},{3,2},{4,3},{5,4},{6,5},{7,6},{8,7},{9,8},{10,9},{11,1... | collective-permute-start | bytes 1179656 | tf_op jit(solution)/shard_map/ppermute | solution.py:503
  6.3 2.2 %collective-permute-start = (f32[6,8,640]{2,1,0:T(8,128)S(1)}, f32[6,8,640]{2,1,0:T(8,128)S(1)}, u32[]{:S(2)}, u32[]{:S(2)}) collective-permute-start(f32[6,8,640]{2,1,0:T(8,128)S(1)} %get-tuple-element.17), channel_id=1, source_target_pairs={{0,1},{1,0},{2,3},{3,2},{4,5},{5,4},{6,7},{7,6},{8,9},{9,8},{10,11... | collective-permute-start | bytes 368648 | tf_op jit(solution)/shard_map/ppermute | solution.py:491
  8.6 6.8 %collective-permute-start.1 = (f32[6,8,640]{2,1,0:T(8,128)S(1)}, f32[6,8,640]{2,1,0:T(8,128)S(1)}, u32[]{:S(2)}, u32[]{:S(2)}) collective-permute-start(f32[6,8,640]{2,1,0:T(8,128)S(1)} %shard_map.78.own.refs_5_), channel_id=1, source_target_pairs={{0,2},{1,3},{2,0},{3,1},{4,6},{5,7},{6,4},{7,5},{8,10},{9,11},{10,... | collective-permute-start | bytes 368648 | tf_op jit(solution)/shard_map/ppermute | solution.py:491
  15.8 10.6 %collective-permute-start.2 = (f32[6,8,640]{2,1,0:T(8,128)S(1)}, f32[6,8,640]{2,1,0:T(8,128)S(1)}, u32[]{:S(2)}, u32[]{:S(2)}) collective-permute-start(f32[6,8,640]{2,1,0:T(8,128)S(1)} %get-tuple-element.19), channel_id=1, source_target_pairs={{0,12},{1,13},{2,14},{3,15},{4,0},{5,1},{6,2},{7,3},{8,4},{9,5},{1... | collective-permute-start | bytes 368648 | tf_op jit(solution)/shard_map/ppermute | solution.py:494
  20.1 6.3 %collective-permute-start.3 = (f32[3,8,640]{2,1,0:T(8,128)S(1)}, f32[3,8,640]{2,1,0:T(8,128)S(1)}, u32[]{:S(2)}, u32[]{:S(2)}) collective-permute-start(f32[3,8,640]{2,1,0:T(8,128)S(1)} %get-tuple-element.20.order), channel_id=1, source_target_pairs={{0,8},{1,9},{2,10},{3,11},{4,12},{5,13},{6,14},{7,15},{8,0},{9,1},... | collective-permute-start | bytes 184328 | tf_op jit(solution)/shard_map/ppermute | solution.py:494
  20.1 6.3 %collective-permute-start.4 = (f32[3,8,640]{2,1,0:T(8,128)S(1)}, f32[3,8,640]{2,1,0:T(8,128)S(1)}, u32[]{:S(2)}, u32[]{:S(2)}) collective-permute-start(f32[3,8,640]{2,1,0:T(8,128)S(1)} %get-tuple-element.20.order), channel_id=1, source_target_pairs={{0,4},{1,5},{2,6},{3,7},{4,8},{5,9},{6,10},{7,11},{8,12},{9,13},{1... | collective-permute-start | bytes 184328 | tf_op jit(solution)/shard_map/ppermute | solution.py:494
  21.1 0.7 %copy-start = (f32[1,3,16,2048]{3,2,1,0:T(8,128)}, f32[1,3,16,2048]{3,2,1,0:T(8,128)S(1)}, u32[]{:S(2)}) copy-start(f32[1,3,16,2048]{3,2,1,0:T(8,128)S(1)} %collective-permute-done.5.following) | copy-start | bytes 1179652
  28.0 1.4 %collective-permute-start.6 = (f32[6,8,512]{2,1,0:T(8,128)S(1)}, f32[6,8,512]{2,1,0:T(8,128)S(1)}, u32[]{:S(2)}, u32[]{:S(2)}) collective-permute-start(f32[6,8,512]{2,1,0:T(8,128)S(1)} %get-tuple-element.24), channel_id=1, source_target_pairs={{0,1},{1,0},{2,3},{3,2},{4,5},{5,4},{6,7},{7,6},{8,9},{9,8},{10,11... | collective-permute-start | bytes 294920 | tf_op jit(solution)/shard_map/ppermute | solution.py:491
  31.1 1.3 %collective-permute-start.7 = (f32[2,8,1024]{2,1,0:T(8,128)S(1)}, f32[2,8,1024]{2,1,0:T(8,128)S(1)}, u32[]{:S(2)}, u32[]{:S(2)}) collective-permute-start(f32[2,8,1024]{2,1,0:T(8,128)S(1)} %get-tuple-element.28), channel_id=1, source_target_pairs={{0,1},{1,0},{2,3},{3,2},{4,5},{5,4},{6,7},{7,6},{8,9},{9,8},{10,11... | collective-permute-start | bytes 196616 | tf_op jit(solution)/shard_map/ppermute | solution.py:491
  32.4 4.3 %collective-permute-start.8 = (f32[2,8,1024]{2,1,0:T(8,128)S(1)}, f32[2,8,1024]{2,1,0:T(8,128)S(1)}, u32[]{:S(2)}, u32[]{:S(2)}) collective-permute-start(f32[2,8,1024]{2,1,0:T(8,128)S(1)} %add.12.a), channel_id=1, source_target_pairs={{0,2},{1,3},{2,0},{3,1},{4,6},{5,7},{6,4},{7,5},{8,10},{9,11},{10,... | collective-permute-start | bytes 196616 | tf_op jit(solution)/shard_map/ppermute | solution.py:491
  36.8 7.1 %collective-permute-start.10 = (f32[2,8,1024]{2,1,0:T(8,128)S(1)}, f32[2,8,1024]{2,1,0:T(8,128)S(1)}, u32[]{:S(2)}, u32[]{:S(2)}) collective-permute-start(f32[2,8,1024]{2,1,0:T(8,128)S(1)} %shard_map.84), channel_id=1, source_target_pairs={{0,8},{1,9},{2,10},{3,11},{4,12},{5,13},{6,14},{7,15},{8,0},{9,1},... | collective-permute-start | bytes 196616 | tf_op jit(solution)/shard_map/ppermute | solution.py:491
  39.3 6.2 %collective-permute-start.11 = (f32[2,8,1024]{2,1,0:T(8,128)S(1)}, f32[2,8,1024]{2,1,0:T(8,128)S(1)}, u32[]{:S(2)}, u32[]{:S(2)}) collective-permute-start(f32[2,8,1024]{2,1,0:T(8,128)S(1)} %shard_map.84), channel_id=1, source_target_pairs={{0,12},{1,13},{2,14},{3,15},{4,8},{5,9},{6,10},{7,11},{8,4},{9,5},... | collective-permute-start | bytes 196616 | tf_op jit(solution)/shard_map/ppermute | solution.py:491
  40.6 5.0 %collective-permute-start.9 = (f32[2,8,1024]{2,1,0:T(8,128)S(1)}, f32[2,8,1024]{2,1,0:T(8,128)S(1)}, u32[]{:S(2)}, u32[]{:S(2)}) collective-permute-start(f32[2,8,1024]{2,1,0:T(8,128)S(1)} %shard_map.84), channel_id=1, source_target_pairs={{0,4},{1,5},{2,6},{3,7},{4,0},{5,1},{6,2},{7,3},{8,12},{9,13},{10,... | collective-permute-start | bytes 196616 | tf_op jit(solution)/shard_map/ppermute | solution.py:491
  45.6 1.3 %collective-permute-start.12 = (f32[2,8,1024]{2,1,0:T(8,128)S(1)}, f32[2,8,1024]{2,1,0:T(8,128)S(1)}, u32[]{:S(2)}, u32[]{:S(2)}) collective-permute-start(f32[2,8,1024]{2,1,0:T(8,128)S(1)} %add_add_fusion.mine), channel_id=1, source_target_pairs={{0,1},{1,0},{2,3},{3,2},{4,5},{5,4},{6,7},{7,6},{8,9},{9,8},{10,11... | collective-permute-start | bytes 196616 | tf_op jit(solution)/shard_map/ppermute | solution.py:491

commit v3 on v2

--- a/solution.py
+++ b/solution.py
@@ -9,6 +9,7 @@
 
 COURANT = 0.06
 LANES = 128
+SUBLANES = 8
 VMEM = pl.BlockSpec(memory_space=pltpu.VMEM)
 HBM = pl.BlockSpec(memory_space=pltpu.HBM)
 ANY = pl.BlockSpec(memory_space=pl.ANY)
@@ -61,18 +62,26 @@
     half = ref.shape[-2] // 2
     return [
         jnp.concatenate(
-            [ref[(v, *at, pl.ds(parity, half, stride=2), slice(None))] for v in range(ref.shape[0])], axis=1
+            [ref[(*at, v, pl.ds(parity, half, stride=2), slice(None))] for v in range(ref.shape[-3])], axis=1
         )
         for parity in range(2)
     ]
 
 
 def spread_copies(source, stage, sem):
-    lead = (slice(None),) * (len(source.shape) - 1)
+    lead = (slice(None),) * (len(source.shape) - 4)
     return [
-        pltpu.make_async_copy(source.at[(*lead, pl.ds(v * LANES, LANES))], stage.at[v], sem)
-        for v in range(stage.shape[0])
+        pltpu.make_async_copy(
+            source.at[(*lead, tile)], stage.at[(*lead, slice(None), pl.ds(tile * SUBLANES, SUBLANES))], sem
+        )
+        for tile in range(source.shape[-4])
     ]
+
+
+def tiled(value):
+    *lead, rows, cols = value.shape
+    value = value.reshape(*lead, rows // SUBLANES, SUBLANES, cols // LANES, LANES)
+    return jnp.swapaxes(value, -2, -3)
 
 
 def wait_all(stage, sem):
@@ -139,20 +148,23 @@
     e_in, n_in = jnp.where(inner_x, e, 0.0), jnp.where(inner_y, n, 0.0)
     e_edge, n_edge = e - e_in, n - n_in
     face_x = jnp.where(inner_x, face_x, 0.0)
+    face_w, face_s = roll(face_x, 1, 1), roll(face_y, 1, 0)
 
     def body(_, carried):
-        s, e, n = carried
+        s, e, n, west, south = carried
         e = e + face_x * (roll(s, -1, 1) - s)
         n = n + face_y * (roll(s, -1, 0) - s)
-        return s + ((e - roll(e, 1, 1)) + (n - roll(n, 1, 0))), e, n
-
-    carried = (s, e_in, n_in)
+        west = west + face_w * (s - roll(s, 1, 1))
+        south = south + face_s * (s - roll(s, 1, 0))
+        return s + ((e - west) + (n - south)), e, n, west, south
+
+    carried = (s, e_in, n_in, roll(e_in, 1, 1), roll(n_in, 1, 0))
     if count <= 4:
         for step in range(count):
             carried = body(step, carried)
     else:
         carried = lax.fori_loop(0, count, body, carried)
-    s, e, n = carried
+    s, e, n, _, _ = carried
     return s, e + e_edge, n + n_edge
 
 
@@ -222,7 +234,7 @@
             copy.start()
     steps = forcing.shape[0]
     width = own.shape[2]
-    coarse_cols = levels.shape[1] // 2
+    coarse_cols = stage_l.shape[0] * LANES // 2
     load_table.wait()
     wait_all(stage_l, sems.at[0])
     level = rows_of(stage_l)
@@ -417,7 +429,7 @@
 
 
 def descend(kept, got, flow, planes, grad, mine, other):
-    steps = flow.shape[1]
+    steps = flow.shape[0]
     half = mine.shape[2]
     first = lax.rem(lax.axis_index("tm"), 2) == 0
     inverse = 1.0 / (steps / 2)
@@ -459,8 +471,9 @@
             at = slice(v * LANES, (v + 1) * LANES)
             stage[v, pl.ds(i, half, stride=2), :] = left[:, at]
             stage[blocks + v, pl.ds(i, half, stride=2), :] = right[:, at]
-    for v in range(2 * blocks):
-        pltpu.make_async_copy(stage.at[v], out.at[:, pl.ds(v * LANES, LANES)], sem).start()
+    for tile in range(out.shape[0]):
+        rows = pl.ds(tile * SUBLANES, SUBLANES)
+        pltpu.make_async_copy(stage.at[:, rows], out.at[tile], sem).start()
     wait_all(stage, sem)
 
 
@@ -476,6 +489,10 @@
     )(*operands)
 
 
+def in_hbm(value):
+    return pltpu.with_memory_space_constraint(value, pltpu.HBM)
+
+
 def shards(initial, velocity, forcing, depth_table, levels, wet_mask):
     count = lax.axis_size("tm")
     rows, cols = levels.shape
@@ -494,17 +511,16 @@
         return lax.ppermute(value, "tm", [(s, (s - stride) % count) for s in range(count)])
 
     def stage(*lead, kind=jnp.float32):
-        return pltpu.VMEM((blocks, *lead, rows, LANES), kind)
-
-    initial, velocity, forcing, depth_table, levels, wet_mask = (
-        pltpu.with_memory_space_constraint(value, pltpu.HBM)
-        for value in (initial, velocity, forcing, depth_table, levels, wet_mask)
-    )
+        return pltpu.VMEM((*lead, blocks, rows, LANES), kind)
+
+    tiled_in = dict(levels=levels, wet=wet_mask, initial=initial, forcing=forcing, velocity=velocity)
+    tiled_in = {name: in_hbm(tiled(value)) for name, value in tiled_in.items()}
+    pinned = in_hbm(initial)
     following = lax.ppermute(initial, "tm", [(s, s - 1) for s in range(1, count)])
     own, sent, planes, coarse_faces = call(
         prepare,
         [(6, *block), (6, *block), (6, *plane), (2, *block)],
-        [depth_table, levels, wet_mask, initial, forcing],
+        [in_hbm(depth_table), *(tiled_in[name] for name in ("levels", "wet", "initial", "forcing"))],
         specs=[HBM] * 5,
         scratch=[
             pltpu.SMEM(depth_table.shape, jnp.float32),
@@ -542,9 +558,9 @@
 
     flow, grad = call(
         base,
-        [(blocks, steps, 2, rows, LANES), (2, *plane)],
-        [row_t, following, forcing, velocity, planes],
-        specs=[ANY, ANY, HBM, HBM, VMEM],
+        [(steps, 2, blocks, rows, LANES), (2, *plane)],
+        [row_t, tiled(following), tiled_in["forcing"], tiled_in["velocity"], planes],
+        specs=[ANY, VMEM, HBM, HBM, VMEM],
         scratch=[stage(3), stage(steps), pltpu.SemaphoreType.DMA((3,))],
         cost=BASE_COST,
     )
@@ -581,7 +597,7 @@
     corrected, done = call(
         functools.partial(correct, steps=steps),
         [initial.shape, (8, LANES)],
-        [kept, got, initial],
+        [kept, got, pinned],
         specs=[VMEM, VMEM, HBM],
         scratch=[pltpu.VMEM(initial.shape, jnp.float32), pltpu.SemaphoreType.DMA],
         cost=CORRECT_COST,
@@ -597,12 +613,12 @@
             stride *= 2
     (gradient,) = call(
         weave,
-        [(rows, cols)],
+        [(rows // SUBLANES, blocks, SUBLANES, LANES)],
         [mine, paired(mine, 1)],
         outs=[HBM],
         scratch=[stage(), pltpu.SemaphoreType.DMA],
     )
-    return corrected, gradient
+    return corrected, jnp.swapaxes(gradient, 1, 2).reshape(rows, cols)
 
 
 def solution(mesh):

time: 47.8 us -> 46.8 us (0.979)
  Pallas kernels: 14.5 us -> 13.5 us
  waiting for transfers between devices: 15.2 us -> 16.2 us
  local copies, waits for them, and re-layouts: 0.75 us -> 0 us
    pallas_call x9, Pallas kernels: 14.5 us -> 13.5 us  [call(): pl.pallas_call(body, out_shape=[jax.ShapeDtypeStruct(shape, jnp.float32)...]
    ppermute x3, waiting for transfers between devices: 1.09 us -> 1.99 us  [back(): lax.ppermute(value, 'tm', [(s, (s - stride) % count) for s in range(count)])]
    unnamed x2 -> x0, local copies, waits for them, and re-layouts: 0.75 us -> none
  transfers between devices with their start and end apart: 13 -> 13, of which waited for: 10 -> 9; matrix products, arithmetic and copies ran while one was open for 0% -> 0% of each run, Pallas kernels for 22% -> 22%
where the time goes in v3:
time: 46.8 us; the launch traced here: 46.6 us
  starting transfers between devices  16.2 us (35%)
  waiting for transfers between devices  16.2 us (35%)
  Pallas kernels  13.5 us (29%)
  between operations  0.73 us (2%)
    ppermute x9, waiting for transfers between devices, paired(): return lax.ppermute(value, 'tm', [(s, s ^ stride) for s in range(count)])  14.2 us
    pallas_call x9, Pallas kernels, call(): pl.pallas_call(body, out_shape=[jax.ShapeDtypeStruct(shape, jnp.float32)...  13.5 us
    ppermute x9, starting transfers between devices, paired(): return lax.ppermute(value, 'tm', [(s, s ^ stride) for s in range(count)])  9.5 us
    ppermute x3, starting transfers between devices, back(): lax.ppermute(value, 'tm', [(s, (s - stride) % count) for s in range(count)])  5.36 us
    ppermute x3, waiting for transfers between devices, back(): lax.ppermute(value, 'tm', [(s, (s - stride) % count) for s in range(count)])  1.99 us
    ppermute x1, starting transfers between devices, shards(): lax.ppermute(initial, 'tm', [(s, s - 1) for s in range(1, count)])  1.29 us
  transfers between devices with their start and end apart: 13, of which 9 were waited for; matrix products, arithmetic and copies ran while one was open for 0% of the time, Pallas kernels for 22%

profile of v3, /device:TPU:0, one launch (start us, length us, event | category | flops | bytes accessed | tf_op | source)
XLA Modules:
  0.0 46.6 jit_solution(18190100916161775499)
XLA Ops:
  0.6 1.3 %collective-permute-start.5 = (f32[1,3,16,2048]{3,2,1,0:T(8,128)}, f32[1,3,16,2048]{3,2,1,0:T(8,128)S(1)}, u32[]{:S(2)}, u32[]{:S(2)}) collective-permute-start(f32[1,3,16,2048]{3,2,1,0:T(8,128)} %initial_in.1), channel_id=1, source_target_pairs={{1,0},{2,1},{3,2},{4,3},{5,4},{6,5},{7,6},{8,7},{9,8},{10,9},{11,1... | collective-permute-start | bytes 1179656 | tf_op jit(solution)/shard_map/ppermute | solution.py:519
  1.9 4.4 %shard_map.77 = (f32[6,8,640]{2,1,0:T(8,128)S(1)}, f32[6,8,640]{2,1,0:T(8,128)S(1)}, f32[6,8,2048]{2,1,0:T(8,128)S(1)}, f32[2,8,640]{2,1,0:T(8,128)S(1)}) custom-call(f32[16]{0:T(128)} %table_in.1, s32[2,16,8,128]{3,2,1,0:T(8,128)} %bitcast.26, s32[2,16,8,128]{3,2,1,0:T(8,128)} %bitcast.27, f32[1,3,2,16,8,128]{5,4,3,2,1,0:T(8,128)} %bitcast.25, ...), custom_call_target="tpu_custom_call" | custom-call | flops 40000000 | bytes 40000000 | tf_op jit(solution)/shard_map/pallas_call | solution.py:481
  6.3 1.2 %collective-permute-start = (f32[6,8,640]{2,1,0:T(8,128)S(1)}, f32[6,8,640]{2,1,0:T(8,128)S(1)}, u32[]{:S(2)}, u32[]{:S(2)}) collective-permute-start(f32[6,8,640]{2,1,0:T(8,128)S(1)} %get-tuple-element.17), channel_id=1, source_target_pairs={{0,1},{1,0},{2,3},{3,2},{4,5},{5,4},{6,7},{7,6},{8,9},{9,8},{10,11... | collective-permute-start | bytes 368648 | tf_op jit(solution)/shard_map/ppermute | solution.py:508
  7.5 1.0 %collective-permute-done.got.refs_4_ = f32[6,8,640]{2,1,0:T(8,128)S(1)} collective-permute-done((f32[6,8,640]{2,1,0:T(8,128)S(1)}, f32[6,8,640]{2,1,0:T(8,128)S(1)}, u32[]{:S(2)}, u32[]{:S(2)}) %collective-permute-start) | collective-permute-done | bytes 122912 | tf_op jit(solution)/shard_map/ppermute | solution.py:508
  8.5 0.1 shard_map.78.own.refs_5_
  8.6 3.0 %collective-permute-start.1 = (f32[6,8,640]{2,1,0:T(8,128)S(1)}, f32[6,8,640]{2,1,0:T(8,128)S(1)}, u32[]{:S(2)}, u32[]{:S(2)}) collective-permute-start(f32[6,8,640]{2,1,0:T(8,128)S(1)} %shard_map.78.own.refs_5_), channel_id=1, source_target_pairs={{0,2},{1,3},{2,0},{3,1},{4,6},{5,7},{6,4},{7,5},{8,10},{9,11},{10,... | collective-permute-start | bytes 368648 | tf_op jit(solution)/shard_map/ppermute | solution.py:508
  11.6 3.8 %collective-permute-done.1.got.refs_6_ = f32[6,8,640]{2,1,0:T(8,128)S(1)} collective-permute-done((f32[6,8,640]{2,1,0:T(8,128)S(1)}, f32[6,8,640]{2,1,0:T(8,128)S(1)}, u32[]{:S(2)}, u32[]{:S(2)}) %collective-permute-start.1) | collective-permute-done | bytes 122912 | tf_op jit(solution)/shard_map/ppermute | solution.py:508
  15.5 0.2 shard_map.79
  15.7 4.3 %collective-permute-start.2 = (f32[6,8,640]{2,1,0:T(8,128)S(1)}, f32[6,8,640]{2,1,0:T(8,128)S(1)}, u32[]{:S(2)}, u32[]{:S(2)}) collective-permute-start(f32[6,8,640]{2,1,0:T(8,128)S(1)} %get-tuple-element.19), channel_id=1, source_target_pairs={{0,12},{1,13},{2,14},{3,15},{4,0},{5,1},{6,2},{7,3},{8,4},{9,5},{1... | collective-permute-start | bytes 368648 | tf_op jit(solution)/shard_map/ppermute | solution.py:511
  20.0 0.0 collective-permute-start.3
  20.0 1.0 %collective-permute-start.4 = (f32[3,8,640]{2,1,0:T(8,128)S(1)}, f32[3,8,640]{2,1,0:T(8,128)S(1)}, u32[]{:S(2)}, u32[]{:S(2)}) collective-permute-start(f32[3,8,640]{2,1,0:T(8,128)S(1)} %get-tuple-element.20.order), channel_id=1, source_target_pairs={{0,4},{1,5},{2,6},{3,7},{4,8},{5,9},{6,10},{7,11},{8,12},{9,13},{1... | collective-permute-start | bytes 184328 | tf_op jit(solution)/shard_map/ppermute | solution.py:511
  21.0 0.0 collective-permute-done.5
  21.0 3.2 %shard_map.80 = (f32[8,2,16,16,128]{4,3,2,1,0:T(8,128)S(1)}, f32[2,8,2048]{2,1,0:T(8,128)S(1)}) custom-call(f32[3,8,640]{2,1,0:T(8,128)S(1)} %get-tuple-element.20.order, f32[1,3,2,16,8,128]{5,4,3,2,1,0:T(8,128)S(1)} %bitcast.21, f32[8,2,16,8,128]{4,3,2,1,0:T(8,128)} %bitcast.23, f32[8,2,2,16,8,128]{5,4,3,2,1,0:T(8,128)} %bitcast.24, ...), custom_call_target="tpu_custom_call" | custom-call | flops 8000000 | bytes 8000000 | tf_op jit(solution)/shard_map/pallas_call | solution.py:481
  24.3 2.0 %collective-permute-done.3.refs_1_ = f32[3,8,640]{2,1,0:T(8,128)S(1)} collective-permute-done((f32[3,8,640]{2,1,0:T(8,128)S(1)}, f32[3,8,640]{2,1,0:T(8,128)S(1)}, u32[]{:S(2)}, u32[]{:S(2)}) %collective-permute-start.3) | collective-permute-done | bytes 61472 | tf_op jit(solution)/shard_map/ppermute | solution.py:511
  26.3 0.0 collective-permute-done.4.refs_2_
  26.3 0.0 collective-permute-done.2.refs_0_
  26.3 0.9 %shard_map.81 = (f32[6,8,512]{2,1,0:T(8,128)S(1)}, f32[6,8,512]{2,1,0:T(8,128)S(1)}) custom-call(f32[6,8,640]{2,1,0:T(8,128)S(1)} %collective-permute-done.2.refs_0_, f32[3,8,640]{2,1,0:T(8,128)S(1)} %collective-permute-done.3.refs_1_, f32[3,8,640]{2,1,0:T(8,128)S(1)} %collective-permute-done.4.refs_2_, f32[6,8,640]{2,1,0:T(8,128)S(1)} %get-tuple-element.16.own.refs_3_, ...), custom_call_target="tpu_custom_call" | custom-call | flops 1000 | bytes 1000 | tf_op jit(solution)/shard_map/pallas_call | solution.py:481
  27.2 0.1 collective-permute-start.6
  27.3 1.3 %collective-permute-done.6.got = f32[6,8,512]{2,1,0:T(8,128)S(1)} collective-permute-done((f32[6,8,512]{2,1,0:T(8,128)S(1)}, f32[6,8,512]{2,1,0:T(8,128)S(1)}, u32[]{:S(2)}, u32[]{:S(2)}) %collective-permute-start.6) | collective-permute-done | bytes 98336 | tf_op jit(solution)/shard_map/ppermute | solution.py:508
  28.6 1.7 %shard_map.83 = (f32[2,8,1024]{2,1,0:T(8,128)S(1)}, f32[2,8,1024]{2,1,0:T(8,128)S(1)}) custom-call(f32[6,8,512]{2,1,0:T(8,128)S(1)} %get-tuple-element.23.kept, f32[6,8,512]{2,1,0:T(8,128)S(1)} %collective-permute-done.6.got, f32[8,2,16,16,128]{4,3,2,1,0:T(8,128)S(1)} %get-tuple-element.26.flow, f32[6,8,2048]{2,1,0:T(8,128)S(1)} %get-tuple-element.21.planes, ...), custom_call_target="tpu_custom_call" | custom-call | flops 8000000 | bytes 8000000 | tf_op jit(solution)/shard_map/pallas_call | solution.py:481
  30.3 0.2 collective-permute-start.7
  30.6 1.1 %collective-permute-done.7 = f32[2,8,1024]{2,1,0:T(8,128)S(1)} collective-permute-done((f32[2,8,1024]{2,1,0:T(8,128)S(1)}, f32[2,8,1024]{2,1,0:T(8,128)S(1)}, u32[]{:S(2)}, u32[]{:S(2)}) %collective-permute-start.7) | collective-permute-done | bytes 65568 | tf_op jit(solution)/shard_map/ppermute | solution.py:508
  31.7 1.3 %collective-permute-start.8 = (f32[2,8,1024]{2,1,0:T(8,128)S(1)}, f32[2,8,1024]{2,1,0:T(8,128)S(1)}, u32[]{:S(2)}, u32[]{:S(2)}) collective-permute-start(f32[2,8,1024]{2,1,0:T(8,128)S(1)} %add.12.a), channel_id=1, source_target_pairs={{0,2},{1,3},{2,0},{3,1},{4,6},{5,7},{6,4},{7,5},{8,10},{9,11},{10,... | collective-permute-start | bytes 196616 | tf_op jit(solution)/shard_map/ppermute | solution.py:508
  33.0 2.3 %shard_map.82 = (f32[1,3,16,2048]{3,2,1,0:T(8,128)}, f32[8,128]{1,0:T(8,128)S(1)}) custom-call(f32[6,8,512]{2,1,0:T(8,128)S(1)} %get-tuple-element.23.kept, f32[6,8,512]{2,1,0:T(8,128)S(1)} %collective-permute-done.6.got, f32[1,3,16,2048]{3,2,1,0:T(8,128)} %initial_in.1), custom_call_target="tpu_custom_call" | custom-call | flops 4000000 | bytes 4000000 | tf_op jit(solution)/shard_map/pallas_call | solution.py:481
  35.3 0.7 %collective-permute-done.8.b = f32[2,8,1024]{2,1,0:T(8,128)S(1)} collective-permute-done((f32[2,8,1024]{2,1,0:T(8,128)S(1)}, f32[2,8,1024]{2,1,0:T(8,128)S(1)}, u32[]{:S(2)}, u32[]{:S(2)}) %collective-permute-start.8) | collective-permute-done | bytes 65568 | tf_op jit(solution)/shard_map/ppermute | solution.py:508
  36.0 2.5 %collective-permute-start.10 = (f32[2,8,1024]{2,1,0:T(8,128)S(1)}, f32[2,8,1024]{2,1,0:T(8,128)S(1)}, u32[]{:S(2)}, u32[]{:S(2)}) collective-permute-start(f32[2,8,1024]{2,1,0:T(8,128)S(1)} %shard_map.84), channel_id=1, source_target_pairs={{0,8},{1,9},{2,10},{3,11},{4,12},{5,13},{6,14},{7,15},{8,0},{9,1},... | collective-permute-start | bytes 196616 | tf_op jit(solution)/shard_map/ppermute | solution.py:508
  38.5 0.8 %collective-permute-start.11 = (f32[2,8,1024]{2,1,0:T(8,128)S(1)}, f32[2,8,1024]{2,1,0:T(8,128)S(1)}, u32[]{:S(2)}, u32[]{:S(2)}) collective-permute-start(f32[2,8,1024]{2,1,0:T(8,128)S(1)} %shard_map.84), channel_id=1, source_target_pairs={{0,12},{1,13},{2,14},{3,15},{4,8},{5,9},{6,10},{7,11},{8,4},{9,5},... | collective-permute-start | bytes 196616 | tf_op jit(solution)/shard_map/ppermute | solution.py:508
  39.4 0.2 collective-permute-start.9
  39.6 3.5 %collective-permute-done.10 = f32[2,8,1024]{2,1,0:T(8,128)S(1)} collective-permute-done((f32[2,8,1024]{2,1,0:T(8,128)S(1)}, f32[2,8,1024]{2,1,0:T(8,128)S(1)}, u32[]{:S(2)}, u32[]{:S(2)}) %collective-permute-start.10) | collective-permute-done | bytes 65568 | tf_op jit(solution)/shard_map/ppermute | solution.py:508
  43.1 1.5 %collective-permute-done.11 = f32[2,8,1024]{2,1,0:T(8,128)S(1)} collective-permute-done((f32[2,8,1024]{2,1,0:T(8,128)S(1)}, f32[2,8,1024]{2,1,0:T(8,128)S(1)}, u32[]{:S(2)}, u32[]{:S(2)}) %collective-permute-start.11) | collective-permute-done | bytes 65568 | tf_op jit(solution)/shard_map/ppermute | solution.py:508
  44.6 0.0 collective-permute-done.9
  44.6 0.1 collective-permute-start.12
  44.7 1.2 %collective-permute-done.12.other = f32[2,8,1024]{2,1,0:T(8,128)S(1)} collective-permute-done((f32[2,8,1024]{2,1,0:T(8,128)S(1)}, f32[2,8,1024]{2,1,0:T(8,128)S(1)}, u32[]{:S(2)}, u32[]{:S(2)}) %collective-permute-start.12) | collective-permute-done | bytes 65568 | tf_op jit(solution)/shard_map/ppermute | solution.py:508
  46.0 0.7 %shard_map.85 = f32[2,16,8,128]{3,2,1,0:T(8,128)} custom-call(f32[2,8,1024]{2,1,0:T(8,128)S(1)} %add_add_fusion.mine, f32[2,8,1024]{2,1,0:T(8,128)S(1)} %collective-permute-done.12.other), custom_call_target="tpu_custom_call" | custom-call | flops 1000 | bytes 1000 | tf_op jit(solution)/shard_map/pallas_call | solution.py:481
  (3 shorter events, 0.0 us)
Async XLA Ops:
  0.6 20.4 %collective-permute-start.5 = (f32[1,3,16,2048]{3,2,1,0:T(8,128)}, f32[1,3,16,2048]{3,2,1,0:T(8,128)S(1)}, u32[]{:S(2)}, u32[]{:S(2)}) collective-permute-start(f32[1,3,16,2048]{3,2,1,0:T(8,128)} %initial_in.1), channel_id=1, source_target_pairs={{1,0},{2,1},{3,2},{4,3},{5,4},{6,5},{7,6},{8,7},{9,8},{10,9},{11,1... | collective-permute-start | bytes 1179656 | tf_op jit(solution)/shard_map/ppermute | solution.py:519
  6.3 2.2 %collective-permute-start = (f32[6,8,640]{2,1,0:T(8,128)S(1)}, f32[6,8,640]{2,1,0:T(8,128)S(1)}, u32[]{:S(2)}, u32[]{:S(2)}) collective-permute-start(f32[6,8,640]{2,1,0:T(8,128)S(1)} %get-tuple-element.17), channel_id=1, source_target_pairs={{0,1},{1,0},{2,3},{3,2},{4,5},{5,4},{6,7},{7,6},{8,9},{9,8},{10,11... | collective-permute-start | bytes 368648 | tf_op jit(solution)/shard_map/ppermute | solution.py:508
  8.6 6.9 %collective-permute-start.1 = (f32[6,8,640]{2,1,0:T(8,128)S(1)}, f32[6,8,640]{2,1,0:T(8,128)S(1)}, u32[]{:S(2)}, u32[]{:S(2)}) collective-permute-start(f32[6,8,640]{2,1,0:T(8,128)S(1)} %shard_map.78.own.refs_5_), channel_id=1, source_target_pairs={{0,2},{1,3},{2,0},{3,1},{4,6},{5,7},{6,4},{7,5},{8,10},{9,11},{10,... | collective-permute-start | bytes 368648 | tf_op jit(solution)/shard_map/ppermute | solution.py:508
  15.7 10.6 %collective-permute-start.2 = (f32[6,8,640]{2,1,0:T(8,128)S(1)}, f32[6,8,640]{2,1,0:T(8,128)S(1)}, u32[]{:S(2)}, u32[]{:S(2)}) collective-permute-start(f32[6,8,640]{2,1,0:T(8,128)S(1)} %get-tuple-element.19), channel_id=1, source_target_pairs={{0,12},{1,13},{2,14},{3,15},{4,0},{5,1},{6,2},{7,3},{8,4},{9,5},{1... | collective-permute-start | bytes 368648 | tf_op jit(solution)/shard_map/ppermute | solution.py:511
  20.0 6.3 %collective-permute-start.3 = (f32[3,8,640]{2,1,0:T(8,128)S(1)}, f32[3,8,640]{2,1,0:T(8,128)S(1)}, u32[]{:S(2)}, u32[]{:S(2)}) collective-permute-start(f32[3,8,640]{2,1,0:T(8,128)S(1)} %get-tuple-element.20.order), channel_id=1, source_target_pairs={{0,8},{1,9},{2,10},{3,11},{4,12},{5,13},{6,14},{7,15},{8,0},{9,1},... | collective-permute-start | bytes 184328 | tf_op jit(solution)/shard_map/ppermute | solution.py:511
  20.0 6.3 %collective-permute-start.4 = (f32[3,8,640]{2,1,0:T(8,128)S(1)}, f32[3,8,640]{2,1,0:T(8,128)S(1)}, u32[]{:S(2)}, u32[]{:S(2)}) collective-permute-start(f32[3,8,640]{2,1,0:T(8,128)S(1)} %get-tuple-element.20.order), channel_id=1, source_target_pairs={{0,4},{1,5},{2,6},{3,7},{4,8},{5,9},{6,10},{7,11},{8,12},{9,13},{1... | collective-permute-start | bytes 184328 | tf_op jit(solution)/shard_map/ppermute | solution.py:511
  27.2 1.4 %collective-permute-start.6 = (f32[6,8,512]{2,1,0:T(8,128)S(1)}, f32[6,8,512]{2,1,0:T(8,128)S(1)}, u32[]{:S(2)}, u32[]{:S(2)}) collective-permute-start(f32[6,8,512]{2,1,0:T(8,128)S(1)} %get-tuple-element.24), channel_id=1, source_target_pairs={{0,1},{1,0},{2,3},{3,2},{4,5},{5,4},{6,7},{7,6},{8,9},{9,8},{10,11... | collective-permute-start | bytes 294920 | tf_op jit(solution)/shard_map/ppermute | solution.py:508
  30.3 1.3 %collective-permute-start.7 = (f32[2,8,1024]{2,1,0:T(8,128)S(1)}, f32[2,8,1024]{2,1,0:T(8,128)S(1)}, u32[]{:S(2)}, u32[]{:S(2)}) collective-permute-start(f32[2,8,1024]{2,1,0:T(8,128)S(1)} %get-tuple-element.28), channel_id=1, source_target_pairs={{0,1},{1,0},{2,3},{3,2},{4,5},{5,4},{6,7},{7,6},{8,9},{9,8},{10,11... | collective-permute-start | bytes 196616 | tf_op jit(solution)/shard_map/ppermute | solution.py:508
  31.7 4.3 %collective-permute-start.8 = (f32[2,8,1024]{2,1,0:T(8,128)S(1)}, f32[2,8,1024]{2,1,0:T(8,128)S(1)}, u32[]{:S(2)}, u32[]{:S(2)}) collective-permute-start(f32[2,8,1024]{2,1,0:T(8,128)S(1)} %add.12.a), channel_id=1, source_target_pairs={{0,2},{1,3},{2,0},{3,1},{4,6},{5,7},{6,4},{7,5},{8,10},{9,11},{10,... | collective-permute-start | bytes 196616 | tf_op jit(solution)/shard_map/ppermute | solution.py:508
  36.0 7.1 %collective-permute-start.10 = (f32[2,8,1024]{2,1,0:T(8,128)S(1)}, f32[2,8,1024]{2,1,0:T(8,128)S(1)}, u32[]{:S(2)}, u32[]{:S(2)}) collective-permute-start(f32[2,8,1024]{2,1,0:T(8,128)S(1)} %shard_map.84), channel_id=1, source_target_pairs={{0,8},{1,9},{2,10},{3,11},{4,12},{5,13},{6,14},{7,15},{8,0},{9,1},... | collective-permute-start | bytes 196616 | tf_op jit(solution)/shard_map/ppermute | solution.py:508
  38.5 6.1 %collective-permute-start.11 = (f32[2,8,1024]{2,1,0:T(8,128)S(1)}, f32[2,8,1024]{2,1,0:T(8,128)S(1)}, u32[]{:S(2)}, u32[]{:S(2)}) collective-permute-start(f32[2,8,1024]{2,1,0:T(8,128)S(1)} %shard_map.84), channel_id=1, source_target_pairs={{0,12},{1,13},{2,14},{3,15},{4,8},{5,9},{6,10},{7,11},{8,4},{9,5},... | collective-permute-start | bytes 196616 | tf_op jit(solution)/shard_map/ppermute | solution.py:508
  39.4 5.3 %collective-permute-start.9 = (f32[2,8,1024]{2,1,0:T(8,128)S(1)}, f32[2,8,1024]{2,1,0:T(8,128)S(1)}, u32[]{:S(2)}, u32[]{:S(2)}) collective-permute-start(f32[2,8,1024]{2,1,0:T(8,128)S(1)} %shard_map.84), channel_id=1, source_target_pairs={{0,4},{1,5},{2,6},{3,7},{4,0},{5,1},{6,2},{7,3},{8,12},{9,13},{10,... | collective-permute-start | bytes 196616 | tf_op jit(solution)/shard_map/ppermute | solution.py:508
  44.6 1.3 %collective-permute-start.12 = (f32[2,8,1024]{2,1,0:T(8,128)S(1)}, f32[2,8,1024]{2,1,0:T(8,128)S(1)}, u32[]{:S(2)}, u32[]{:S(2)}) collective-permute-start(f32[2,8,1024]{2,1,0:T(8,128)S(1)} %add_add_fusion.mine), channel_id=1, source_target_pairs={{0,1},{1,0},{2,3},{3,2},{4,5},{5,4},{6,7},{7,6},{8,9},{9,8},{10,11... | collective-permute-start | bytes 196616 | tf_op jit(solution)/shard_map/ppermute | solution.py:508

commit v4 on v3

--- a/solution.py
+++ b/solution.py
@@ -16,6 +16,7 @@
 PREPARE_COST = 40_000_000
 BASE_COST = 8_000_000
 CORRECT_COST = 4_000_000
+SPLIT_COST = 1000
 EXACT = lax.Precision.HIGHEST
 
 
@@ -218,6 +219,7 @@
     own,
     sent,
     planes,
+    window_planes,
     coarse_faces,
     table,
     stage_l,
@@ -247,7 +249,8 @@
     half = 0.5 * COURANT * COURANT
     face_x = inside_x([half * (d + roll(d, -1, 1)) for d in depth])
     face_y = inside_y([half * (depth[0] + depth[1]), half * (depth[1] + roll(depth[0], -1, 0))])
-    for i, plane in enumerate(face_x + face_y + dry):
+    all_planes = face_x + face_y + dry
+    for i, plane in enumerate(all_planes):
         planes[i] = plane
 
     wait_all(stage_i, sems.at[2])
@@ -280,8 +283,11 @@
 
     core = lax.rem(lax.axis_index("tm"), 2)
     right = coarse_cols - width
-
-    def store(mine, other):
+    window = window_planes.shape[2]
+
+    def store(mine, other, start):
+        for i, plane in enumerate(all_planes):
+            window_planes[i] = plane[:, start : start + window]
         for ref, at in ((own, mine), (sent, other)):
             for i in range(3):
                 ref[i] = g[i][:, at : at + width]
@@ -291,14 +297,14 @@
 
     @pl.when(core == 0)
     def _():
-        store(0, right)
+        store(0, right, 0)
 
     @pl.when(core == 1)
     def _():
-        store(right, 0)
-
-
-def chip_pair(own, got, coarse_faces, out):
+        store(right, 0, 2 * coarse_cols - window)
+
+
+def chip_pair(own, got, coarse_faces, order, out):
     cx, cy = coarse_faces[0], coarse_faces[1]
     first = lax.rem(lax.axis_index("tm"), 2) == 0
     g_own, g_got = read(own), read(got)
@@ -308,7 +314,7 @@
     write(out, add(w_low, g_high), 3)
 
 
-def row_pair(own, got, coarse_faces, out, out_t):
+def row_pair(own, got, coarse_faces, order, through, out, out_t, passed):
     cx, cy = coarse_faces[0], coarse_faces[1]
     first = lax.rem(lax.axis_index("tm") // 2, 2) == 0
     t_own, t_got = read(own), read(got)
@@ -328,7 +334,7 @@
     write(out, add(read(own), moved))
 
 
-def finish(near, far, farther, own, got, chip, partner, coarse_faces, kept, sent, *, per_row, rows_in_all):
+def finish(near, far, farther, own, got, chip, partner, coarse_faces, starts, kept, sent, *, per_row, rows_in_all):
     cx, cy = coarse_faces[0], coarse_faces[1]
     width = coarse_faces.shape[2]
     half = kept.shape[2]
@@ -355,27 +361,26 @@
     c_low = add(q, coarse_step(end, cx, cy))
     c_high = add(w_high, end)
 
+    write(starts, pick(first, c_high, after))
+    write(starts, pick(first, after, c_high), 3)
+
     @pl.when(first)
     def _():
         for i in range(3):
             kept[i] = c_low[i][:, :half]
-            kept[3 + i] = c_high[i][:, :half]
             sent[i] = c_high[i][:, :half]
-            sent[3 + i] = after[i][:, :half]
 
     @pl.when(jnp.logical_not(first))
     def _():
         for i in range(3):
             kept[i] = c_high[i][:, width - half :]
-            kept[3 + i] = after[i][:, width - half :]
             sent[i] = c_low[i][:, width - half :]
-            sent[3 + i] = c_high[i][:, width - half :]
-
-
-def joined(kept, got, at):
+
+
+def joined(kept, got):
     first = lax.rem(lax.axis_index("tm"), 2) == 0
     fields = []
-    for i in range(at, at + 3):
+    for i in range(3):
         left = jnp.where(first, kept[i], got[i])
         right = jnp.where(first, got[i], kept[i])
         fields.append(jnp.concatenate([left, right], axis=1))
@@ -387,7 +392,7 @@
     load.start()
     done[...] = jnp.zeros_like(done)
     unscale = 1.0 / (COURANT * (steps / 2))
-    s, e, n = joined(kept, got, 0)
+    s, e, n = joined(kept, got)
     fields = prolong_all([s, e * unscale, n * unscale])
     load.wait()
     for i, field in enumerate(fields):
@@ -402,7 +407,7 @@
     ]
 
 
-def base(order, following, forcing, velocity, planes, flow, grad, stage_i, stage_f, sems):
+def base(order, following, forcing, velocity, planes, mine, other, stage_i, stage_f, flow, sems):
     sources = ((following.at[0], stage_i), (forcing, stage_f), (velocity, flow))
     for i, (source, stage) in enumerate(sources):
         for copy in spread_copies(source, stage, sems.at[i]):
@@ -424,25 +429,9 @@
             sums[k] = [a + d * v for a, d, v in zip(sums[k], slopes[k], rows_of(flow, step, k))]
         if step:
             s = [v + f for v, f in zip(s, rows_of(stage_f, step))]
-    for i, value in enumerate(pulled(sums, [planes[4], planes[5]])):
-        grad[i] = value
-
-
-def descend(kept, got, flow, planes, grad, mine, other):
-    steps = flow.shape[0]
+    total = pulled(sums, [planes[4], planes[5]])
+    first = lax.rem(device, 2) == 0
     half = mine.shape[2]
-    first = lax.rem(lax.axis_index("tm"), 2) == 0
-    inverse = 1.0 / (steps / 2)
-    s, e, n = prolong_columns(joined(kept, got, 3))
-    e, n = e * inverse, n * inverse
-    s, e, n = [s, s], inside_x([e, e]), inside_y([n, n])
-    face_x, face_y = [planes[0], planes[1]], [planes[2], planes[3]]
-    sums = [[jnp.zeros_like(v) for v in s] for _ in range(2)]
-    for step in reversed(range(steps)):
-        s, e, n, *slopes = fine_step(s, e, n, face_x, face_y)
-        for k in range(2):
-            sums[k] = [a + d * v for a, d, v in zip(sums[k], slopes[k], rows_of(flow, step, k))]
-    total = [grad[i] + v for i, v in enumerate(pulled(sums, [planes[4], planes[5]]))]
 
     @pl.when(first)
     def _():
@@ -455,6 +444,48 @@
         for i in range(2):
             mine[i] = total[i][:, half:]
             other[i] = total[i][:, :half]
+
+
+def split_flow(order, velocity, own, sent, sems):
+    core = lax.rem(lax.axis_index("tm"), 2)
+    blocks = own.shape[2]
+    right = velocity.shape[3] - blocks
+    for i, (out, start) in enumerate(((own, core * right), (sent, (1 - core) * right))):
+        source = velocity.at[:, :, :, pl.ds(start, blocks)]
+        for tile in range(velocity.shape[2]):
+            rows = pl.ds(tile * SUBLANES, SUBLANES)
+            pltpu.make_async_copy(source.at[:, :, tile], out.at[:, :, :, rows], sems.at[i]).start()
+    wait_all(own, sems.at[0])
+    wait_all(sent, sems.at[1])
+
+
+def descend(starts, flow, flow_got, planes, grad, grad_got, mine):
+    steps = flow.shape[0]
+    half = mine.shape[2]
+    width = starts.shape[2]
+    window = planes.shape[2]
+    first = lax.rem(lax.axis_index("tm"), 2) == 0
+    inverse = 1.0 / (steps / 2)
+    shift = width - window // 2
+    fields = [jnp.where(first, starts[i], roll(starts[i], -shift, 1)) for i in range(6)]
+    fields = [field[:, :window] for field in prolong_columns(fields)]
+    face_x, face_y = inside_x([planes[0], planes[1]]), [planes[2], planes[3]]
+    total = None
+    for k, velocity in enumerate((flow, flow_got)):
+        s, e, n = fields[3 * k : 3 * k + 3]
+        e, n = e * inverse, n * inverse
+        s, e, n = [s, s], inside_x([e, e]), inside_y([n, n])
+        for step in reversed(range(steps)):
+            s, e, n, *slopes = fine_step(s, e, n, face_x, face_y)
+            terms = [[d * v for d, v in zip(slopes[i], rows_of(velocity, step, i))] for i in range(2)]
+            if total is None:
+                total = terms
+            else:
+                total = [[a + b for a, b in zip(*pair)] for pair in zip(total, terms)]
+    total = pulled(total, [planes[4], planes[5]])
+    for i in range(2):
+        valid = jnp.where(first, total[i][:, :half], total[i][:, window - half :])
+        mine[i] = valid + (grad[i] + grad_got[i])
 
 
 def plus(a, b, order, out):
@@ -477,13 +508,14 @@
     wait_all(stage, sem)
 
 
-def call(body, shapes, operands, *, specs=None, outs=None, scratch=(), cost=1000):
+def call(body, shapes, operands, *, specs=None, outs=None, scratch=(), aliases={}, cost=1000):
     return pl.pallas_call(
         body,
         out_shape=[jax.ShapeDtypeStruct(shape, jnp.float32) for shape in shapes],
         in_specs=specs or [VMEM] * len(operands),
         out_specs=outs or [VMEM] * len(shapes),
         scratch_shapes=scratch,
+        input_output_aliases=aliases,
         cost_estimate=pl.CostEstimate(flops=cost, bytes_accessed=cost, transcendentals=0),
         compiler_params=pltpu.CompilerParams(vmem_limit_bytes=32 * 1024 * 1024),
     )(*operands)
@@ -502,6 +534,7 @@
     width = half + halo
     block = (half_rows, width)
     blocks = cols // LANES
+    window = cols // 2 - (-(steps + 1) // LANES) * LANES
     plane = (half_rows, cols)
 
     def paired(value, stride):
@@ -517,9 +550,9 @@
     tiled_in = {name: in_hbm(tiled(value)) for name, value in tiled_in.items()}
     pinned = in_hbm(initial)
     following = lax.ppermute(initial, "tm", [(s, s - 1) for s in range(1, count)])
-    own, sent, planes, coarse_faces = call(
+    own, sent, planes, window_planes, coarse_faces = call(
         prepare,
-        [(6, *block), (6, *block), (6, *plane), (2, *block)],
+        [(6, *block), (6, *block), (6, *plane), (6, half_rows, window), (2, *block)],
         [in_hbm(depth_table), *(tiled_in[name] for name in ("levels", "wet", "initial", "forcing"))],
         specs=[HBM] * 5,
         scratch=[
@@ -533,12 +566,37 @@
         cost=PREPARE_COST,
     )
     got = paired(sent, 1)
-    (chip,) = call(chip_pair, [(6, *block)], [own, got, coarse_faces])
+    flow, flow_other = call(
+        split_flow,
+        [(steps, 2, window // LANES, rows, LANES)] * 2,
+        [own, tiled_in["velocity"]],
+        specs=[ANY, HBM],
+        scratch=[pltpu.SemaphoreType.DMA((2,))],
+        cost=SPLIT_COST,
+    )
+    (chip,) = call(
+        chip_pair, [(6, *block)], [own, got, coarse_faces, flow], specs=[VMEM] * 3 + [ANY]
+    )
+    grad, grad_other = call(
+        base,
+        [(2, half_rows, cols // 2)] * 2,
+        [chip, tiled(following), tiled_in["forcing"], tiled_in["velocity"], planes],
+        specs=[ANY, VMEM, HBM, HBM, VMEM],
+        scratch=[stage(3), stage(steps), stage(steps, 2), pltpu.SemaphoreType.DMA((3,))],
+        cost=BASE_COST,
+    )
     per_row = 4 if count <= 16 else 2
     rows_in_all = count // per_row
     if per_row == 4:
         partner = paired(chip, 2)
-        row, row_t = call(row_pair, [(6, *block), (3, *block)], [chip, partner, coarse_faces])
+        row, row_t, flow_other = call(
+            row_pair,
+            [(6, *block), (3, *block), flow_other.shape],
+            [chip, partner, coarse_faces, grad, flow_other],
+            specs=[VMEM] * 3 + [ANY] * 2,
+            outs=[VMEM] * 2 + [ANY],
+            aliases={4: 2},
+        )
     else:
         partner = None
         row, row_t = chip, chip[:3]
@@ -556,14 +614,7 @@
             stride *= 2
         far, farther = back(row_t, 2 * per_row), None
 
-    flow, grad = call(
-        base,
-        [(steps, 2, blocks, rows, LANES), (2, *plane)],
-        [row_t, tiled(following), tiled_in["forcing"], tiled_in["velocity"], planes],
-        specs=[ANY, VMEM, HBM, HBM, VMEM],
-        scratch=[stage(3), stage(steps), pltpu.SemaphoreType.DMA((3,))],
-        cost=BASE_COST,
-    )
+    flow_got, grad_got = paired(flow_other, 1), paired(grad_other, 1)
 
     operands = {
         "near": near,
@@ -580,20 +631,21 @@
     def finish_body(*refs):
         given = dict.fromkeys(operands)
         given.update(zip(names, refs))
-        kept, sent = refs[len(names) + 1 :]
-        finish(**given, kept=kept, sent=sent, per_row=per_row, rows_in_all=rows_in_all)
-
-    kept, sent = call(
+        starts, kept, sent = refs[len(names) :]
+        finish(**given, starts=starts, kept=kept, sent=sent, per_row=per_row, rows_in_all=rows_in_all)
+
+    starts, kept, sent = call(
         finish_body,
-        [(6, half_rows, half)] * 2,
-        [operands[name] for name in names] + [grad],
-        specs=[VMEM] * len(names) + [ANY],
+        [(6, *block), (3, half_rows, half), (3, half_rows, half)],
+        [operands[name] for name in names],
+    )
+    (mine,) = call(
+        descend,
+        [(2, half_rows, cols // 2)],
+        [starts, flow, flow_got, window_planes, grad, grad_got],
+        cost=BASE_COST,
     )
     got = paired(sent, 1)
-    mine, other = call(
-        descend, [(2, half_rows, cols // 2)] * 2, [kept, got, flow, planes, grad], cost=BASE_COST
-    )
-    mine = mine + paired(other, 1)
     corrected, done = call(
         functools.partial(correct, steps=steps),
         [initial.shape, (8, LANES)],

time: 46.8 us -> 46.8 us (level)
  waiting for transfers between devices: 16.2 us -> 13.9 us
  Pallas kernels: 13.5 us -> 15.1 us
  starting transfers between devices: 16.2 us -> 16.8 us
    ppermute x9 -> x10, waiting for transfers between devices: 14.2 us -> 7.15 us  [paired(): return lax.ppermute(value, 'tm', [(s, s ^ stride) for s in range(count)])]
    ppermute x3, waiting for transfers between devices: 1.99 us -> 6.78 us  [back(): lax.ppermute(value, 'tm', [(s, (s - stride) % count) for s in range(count)])]
    pallas_call x9 -> x10, Pallas kernels: 13.5 us -> 15.1 us  [call(): pl.pallas_call(body, out_shape=[jax.ShapeDtypeStruct(shape, jnp.float32)...]
    ppermute x9 -> x10, starting transfers between devices: 9.5 us -> 9.81 us  [paired(): return lax.ppermute(value, 'tm', [(s, s ^ stride) for s in range(count)])]
  transfers between devices with their start and end apart: 13 -> 14, of which waited for: 9 -> 7; matrix products, arithmetic and copies ran while one was open for 0% -> 0% of each run, Pallas kernels for 22% -> 27%
where the time goes in v4:
time: 46.8 us; the launch traced here: 46.6 us
  starting transfers between devices  16.8 us (36%)
  Pallas kernels  15.1 us (32%)
  waiting for transfers between devices  13.9 us (30%)
  between operations  0.76 us (2%)
    pallas_call x10, Pallas kernels, call(): pl.pallas_call(body, out_shape=[jax.ShapeDtypeStruct(shape, jnp.float32)...  15.1 us
    ppermute x10, starting transfers between devices, paired(): return lax.ppermute(value, 'tm', [(s, s ^ stride) for s in range(count)])  9.81 us
    ppermute x10, waiting for transfers between devices, paired(): return lax.ppermute(value, 'tm', [(s, s ^ stride) for s in range(count)])  7.15 us
    ppermute x3, waiting for transfers between devices, back(): lax.ppermute(value, 'tm', [(s, (s - stride) % count) for s in range(count)])  6.78 us
    ppermute x3, starting transfers between devices, back(): lax.ppermute(value, 'tm', [(s, (s - stride) % count) for s in range(count)])  5.69 us
    ppermute x1, starting transfers between devices, shards(): lax.ppermute(initial, 'tm', [(s, s - 1) for s in range(1, count)])  1.29 us
  transfers between devices with their start and end apart: 14, of which 7 were waited for; matrix products, arithmetic and copies ran while one was open for 0% of the time, Pallas kernels for 27%

profile of v4, /device:TPU:0, one launch (start us, length us, event | category | flops | bytes accessed | tf_op | source)
XLA Modules:
  0.0 46.6 jit_solution(2561221920705230579)
XLA Ops:
  0.6 1.3 %collective-permute-start.2 = (f32[1,3,16,2048]{3,2,1,0:T(8,128)}, f32[1,3,16,2048]{3,2,1,0:T(8,128)S(1)}, u32[]{:S(2)}, u32[]{:S(2)}) collective-permute-start(f32[1,3,16,2048]{3,2,1,0:T(8,128)} %initial_in.1), channel_id=1, source_target_pairs={{1,0},{2,1},{3,2},{4,3},{5,4},{6,5},{7,6},{8,7},{9,8},{10,9},{11,1... | collective-permute-start | bytes 1179656 | tf_op jit(solution)/shard_map/ppermute | solution.py:552
  1.9 4.4 %shard_map.77 = (f32[6,8,640]{2,1,0:T(8,128)S(1)}, f32[6,8,640]{2,1,0:T(8,128)S(1)}, f32[6,8,2048]{2,1,0:T(8,128)S(1)}, f32[6,8,1152]{2,1,0:T(8,128)S(1)}, f32[2,8,640]{2,1,0:T(8,128)S(1)}) custom-call(f32[16]{0:T(128)} %table_in.1, s32[2,16,8,128]{3,2,1,0:T(8,128)} %bitcast.27, s32[2,16,8,128]{3,2,1,0:T(8,128)} %bitcast.28, ...), custom_call_target="tpu_custom_call" | custom-call | flops 40000000 | bytes 40000000 | tf_op jit(solution)/shard_map/pallas_call | solution.py:512
  6.3 1.2 %collective-permute-start = (f32[6,8,640]{2,1,0:T(8,128)S(1)}, f32[6,8,640]{2,1,0:T(8,128)S(1)}, u32[]{:S(2)}, u32[]{:S(2)}) collective-permute-start(f32[6,8,640]{2,1,0:T(8,128)S(1)} %get-tuple-element.20), channel_id=1, source_target_pairs={{0,1},{1,0},{2,3},{3,2},{4,5},{5,4},{6,7},{7,6},{8,9},{9,8},{10,11... | collective-permute-start | bytes 368648 | tf_op jit(solution)/shard_map/ppermute | solution.py:541
  7.5 1.6 %shard_map.78 = (f32[8,2,9,16,128]{4,3,2,1,0:T(8,128)S(1)}, f32[8,2,9,16,128]{4,3,2,1,0:T(8,128)S(1)}) custom-call(f32[6,8,640]{2,1,0:T(8,128)S(1)} %get-tuple-element.19.order.own.refs_3_, f32[8,2,2,16,8,128]{5,4,3,2,1,0:T(8,128)} %bitcast.22), custom_call_target="tpu_custom_call" | custom-call | flops 1000 | bytes 1000 | tf_op jit(solution)/shard_map/pallas_call | solution.py:512
  9.1 0.0 collective-permute-done.got.refs_4_
  9.2 0.1 shard_map.79.order.own.refs_5_
  9.3 3.0 %collective-permute-start.1 = (f32[6,8,640]{2,1,0:T(8,128)S(1)}, f32[6,8,640]{2,1,0:T(8,128)S(1)}, u32[]{:S(2)}, u32[]{:S(2)}) collective-permute-start(f32[6,8,640]{2,1,0:T(8,128)S(1)} %shard_map.79.order.own.refs_5_), channel_id=1, source_target_pairs={{0,2},{1,3},{2,0},{3,1},{4,6},{5,7},{6,4},{7,5},{8,10},{9,11},{10,... | collective-permute-start | bytes 368648 | tf_op jit(solution)/shard_map/ppermute | solution.py:541
  12.3 0.0 collective-permute-done.2
  12.3 3.2 %shard_map.80 = (f32[2,8,1024]{2,1,0:T(8,128)S(1)}, f32[2,8,1024]{2,1,0:T(8,128)S(1)}) custom-call(f32[6,8,640]{2,1,0:T(8,128)S(1)} %shard_map.79.order.own.refs_5_, f32[1,3,2,16,8,128]{5,4,3,2,1,0:T(8,128)S(1)} %bitcast.21, f32[8,2,16,8,128]{4,3,2,1,0:T(8,128)} %bitcast.25, f32[8,2,2,16,8,128]{5,4,3,2,1,0:T(8,128)} %bitcast.23, ...), custom_call_target="tpu_custom_call" | custom-call | flops 8000000 | bytes 8000000 | tf_op jit(solution)/shard_map/pallas_call | solution.py:512
  15.5 0.3 collective-permute-done.1.got.refs_6_
  15.8 0.2 shard_map.81
  16.0 0.1 collective-permute-start.7
  16.1 4.7 %collective-permute-start.3 = (f32[6,8,640]{2,1,0:T(8,128)S(1)}, f32[6,8,640]{2,1,0:T(8,128)S(1)}, u32[]{:S(2)}, u32[]{:S(2)}) collective-permute-start(f32[6,8,640]{2,1,0:T(8,128)S(1)} %get-tuple-element.26), channel_id=1, source_target_pairs={{0,12},{1,13},{2,14},{3,15},{4,0},{5,1},{6,2},{7,3},{8,4},{9,5},{1... | collective-permute-start | bytes 368648 | tf_op jit(solution)/shard_map/ppermute | solution.py:544
  20.8 0.2 collective-permute-start.8
  20.9 0.0 collective-permute-start.5
  20.9 1.0 %collective-permute-start.4 = (f32[3,8,640]{2,1,0:T(8,128)S(1)}, f32[3,8,640]{2,1,0:T(8,128)S(1)}, u32[]{:S(2)}, u32[]{:S(2)}) collective-permute-start(f32[3,8,640]{2,1,0:T(8,128)S(1)} %get-tuple-element.27), channel_id=1, source_target_pairs={{0,8},{1,9},{2,10},{3,11},{4,12},{5,13},{6,14},{7,15},{8,0},{9,1},... | collective-permute-start | bytes 184328 | tf_op jit(solution)/shard_map/ppermute | solution.py:544
  21.9 5.7 %collective-permute-done.5.refs_2_ = f32[3,8,640]{2,1,0:T(8,128)S(1)} collective-permute-done((f32[3,8,640]{2,1,0:T(8,128)S(1)}, f32[3,8,640]{2,1,0:T(8,128)S(1)}, u32[]{:S(2)}, u32[]{:S(2)}) %collective-permute-start.5) | collective-permute-done | bytes 61472 | tf_op jit(solution)/shard_map/ppermute | solution.py:544
  27.7 1.1 %collective-permute-done.4.refs_1_ = f32[3,8,640]{2,1,0:T(8,128)S(1)} collective-permute-done((f32[3,8,640]{2,1,0:T(8,128)S(1)}, f32[3,8,640]{2,1,0:T(8,128)S(1)}, u32[]{:S(2)}, u32[]{:S(2)}) %collective-permute-start.4) | collective-permute-done | bytes 61472 | tf_op jit(solution)/shard_map/ppermute | solution.py:544
  28.7 0.0 collective-permute-done.3.refs_0_
  28.7 0.9 %shard_map.82 = (f32[6,8,640]{2,1,0:T(8,128)S(1)}, f32[3,8,512]{2,1,0:T(8,128)S(1)}, f32[3,8,512]{2,1,0:T(8,128)S(1)}) custom-call(f32[6,8,640]{2,1,0:T(8,128)S(1)} %collective-permute-done.3.refs_0_, f32[3,8,640]{2,1,0:T(8,128)S(1)} %collective-permute-done.4.refs_1_, f32[3,8,640]{2,1,0:T(8,128)S(1)} %collective-permute-done.5.refs_2_, ...), custom_call_target="tpu_custom_call" | custom-call | flops 1000 | bytes 1000 | tf_op jit(solution)/shard_map/pallas_call | solution.py:512
  29.7 0.0 collective-permute-done.8.grad_got
  29.7 0.0 collective-permute-done.7.flow_got
  29.7 1.7 %shard_map.84.a = f32[2,8,1024]{2,1,0:T(8,128)S(1)} custom-call(f32[6,8,640]{2,1,0:T(8,128)S(1)} %get-tuple-element.31.starts, f32[8,2,9,16,128]{4,3,2,1,0:T(8,128)S(1)} %get-tuple-element.22.order.flow, f32[8,2,9,16,128]{4,3,2,1,0:T(8,128)S(1)} %collective-permute-done.7.flow_got, f32[6,8,1152]{2,1,0:T(8,128)S(1)} %get-tuple-element.33.planes, ...), custom_call_target="tpu_custom_call" | custom-call | flops 8000000 | bytes 8000000 | tf_op jit(solution)/shard_map/pallas_call | solution.py:512
  31.4 0.8 %collective-permute-start.9 = (f32[2,8,1024]{2,1,0:T(8,128)S(1)}, f32[2,8,1024]{2,1,0:T(8,128)S(1)}, u32[]{:S(2)}, u32[]{:S(2)}) collective-permute-start(f32[2,8,1024]{2,1,0:T(8,128)S(1)} %shard_map.84.a), channel_id=1, source_target_pairs={{0,2},{1,3},{2,0},{3,1},{4,6},{5,7},{6,4},{7,5},{8,10},{9,11},{10,... | collective-permute-start | bytes 196616 | tf_op jit(solution)/shard_map/ppermute | solution.py:541
  32.2 0.0 collective-permute-start.6
  32.2 1.2 %collective-permute-done.6.got = f32[3,8,512]{2,1,0:T(8,128)S(1)} collective-permute-done((f32[3,8,512]{2,1,0:T(8,128)S(1)}, f32[3,8,512]{2,1,0:T(8,128)S(1)}, u32[]{:S(2)}, u32[]{:S(2)}) %collective-permute-start.6) | collective-permute-done | bytes 49184 | tf_op jit(solution)/shard_map/ppermute | solution.py:541
  33.4 2.3 %shard_map.83 = (f32[1,3,16,2048]{3,2,1,0:T(8,128)}, f32[8,128]{1,0:T(8,128)S(1)}) custom-call(f32[3,8,512]{2,1,0:T(8,128)S(1)} %get-tuple-element.28.kept, f32[3,8,512]{2,1,0:T(8,128)S(1)} %collective-permute-done.6.got, f32[1,3,16,2048]{3,2,1,0:T(8,128)} %initial_in.1), custom_call_target="tpu_custom_call" | custom-call | flops 4000000 | bytes 4000000 | tf_op jit(solution)/shard_map/pallas_call | solution.py:512
  35.7 0.0 collective-permute-done.9.b
  35.7 2.5 %collective-permute-start.12 = (f32[2,8,1024]{2,1,0:T(8,128)S(1)}, f32[2,8,1024]{2,1,0:T(8,128)S(1)}, u32[]{:S(2)}, u32[]{:S(2)}) collective-permute-start(f32[2,8,1024]{2,1,0:T(8,128)S(1)} %shard_map.85), channel_id=1, source_target_pairs={{0,12},{1,13},{2,14},{3,15},{4,8},{5,9},{6,10},{7,11},{8,4},{9,5},... | collective-permute-start | bytes 196616 | tf_op jit(solution)/shard_map/ppermute | solution.py:541
  38.2 0.0 collective-permute-start.11
  38.2 2.0 %collective-permute-start.10 = (f32[2,8,1024]{2,1,0:T(8,128)S(1)}, f32[2,8,1024]{2,1,0:T(8,128)S(1)}, u32[]{:S(2)}, u32[]{:S(2)}) collective-permute-start(f32[2,8,1024]{2,1,0:T(8,128)S(1)} %shard_map.85), channel_id=1, source_target_pairs={{0,4},{1,5},{2,6},{3,7},{4,0},{5,1},{6,2},{7,3},{8,12},{9,13},{10,... | collective-permute-start | bytes 196616 | tf_op jit(solution)/shard_map/ppermute | solution.py:541
  40.2 2.4 %collective-permute-done.12 = f32[2,8,1024]{2,1,0:T(8,128)S(1)} collective-permute-done((f32[2,8,1024]{2,1,0:T(8,128)S(1)}, f32[2,8,1024]{2,1,0:T(8,128)S(1)}, u32[]{:S(2)}, u32[]{:S(2)}) %collective-permute-start.12) | collective-permute-done | bytes 65568 | tf_op jit(solution)/shard_map/ppermute | solution.py:541
  42.6 2.0 %collective-permute-done.11 = f32[2,8,1024]{2,1,0:T(8,128)S(1)} collective-permute-done((f32[2,8,1024]{2,1,0:T(8,128)S(1)}, f32[2,8,1024]{2,1,0:T(8,128)S(1)}, u32[]{:S(2)}, u32[]{:S(2)}) %collective-permute-start.11) | collective-permute-done | bytes 65568 | tf_op jit(solution)/shard_map/ppermute | solution.py:541
  44.6 0.0 collective-permute-done.10
  44.6 0.1 collective-permute-start.13
  44.7 1.2 %collective-permute-done.13.other = f32[2,8,1024]{2,1,0:T(8,128)S(1)} collective-permute-done((f32[2,8,1024]{2,1,0:T(8,128)S(1)}, f32[2,8,1024]{2,1,0:T(8,128)S(1)}, u32[]{:S(2)}, u32[]{:S(2)}) %collective-permute-start.13) | collective-permute-done | bytes 65568 | tf_op jit(solution)/shard_map/ppermute | solution.py:541
  45.9 0.7 %shard_map.86 = f32[2,16,8,128]{3,2,1,0:T(8,128)} custom-call(f32[2,8,1024]{2,1,0:T(8,128)S(1)} %add_add_fusion.mine, f32[2,8,1024]{2,1,0:T(8,128)S(1)} %collective-permute-done.13.other), custom_call_target="tpu_custom_call" | custom-call | flops 1000 | bytes 1000 | tf_op jit(solution)/shard_map/pallas_call | solution.py:512
  (2 shorter events, 0.0 us)
Async XLA Ops:
  0.6 11.7 %collective-permute-start.2 = (f32[1,3,16,2048]{3,2,1,0:T(8,128)}, f32[1,3,16,2048]{3,2,1,0:T(8,128)S(1)}, u32[]{:S(2)}, u32[]{:S(2)}) collective-permute-start(f32[1,3,16,2048]{3,2,1,0:T(8,128)} %initial_in.1), channel_id=1, source_target_pairs={{1,0},{2,1},{3,2},{4,3},{5,4},{6,5},{7,6},{8,7},{9,8},{10,9},{11,1... | collective-permute-start | bytes 1179656 | tf_op jit(solution)/shard_map/ppermute | solution.py:552
  6.3 2.8 %collective-permute-start = (f32[6,8,640]{2,1,0:T(8,128)S(1)}, f32[6,8,640]{2,1,0:T(8,128)S(1)}, u32[]{:S(2)}, u32[]{:S(2)}) collective-permute-start(f32[6,8,640]{2,1,0:T(8,128)S(1)} %get-tuple-element.20), channel_id=1, source_target_pairs={{0,1},{1,0},{2,3},{3,2},{4,5},{5,4},{6,7},{7,6},{8,9},{9,8},{10,11... | collective-permute-start | bytes 368648 | tf_op jit(solution)/shard_map/ppermute | solution.py:541
  9.3 6.5 %collective-permute-start.1 = (f32[6,8,640]{2,1,0:T(8,128)S(1)}, f32[6,8,640]{2,1,0:T(8,128)S(1)}, u32[]{:S(2)}, u32[]{:S(2)}) collective-permute-start(f32[6,8,640]{2,1,0:T(8,128)S(1)} %shard_map.79.order.own.refs_5_), channel_id=1, source_target_pairs={{0,2},{1,3},{2,0},{3,1},{4,6},{5,7},{6,4},{7,5},{8,10},{9,11},{10,... | collective-permute-start | bytes 368648 | tf_op jit(solution)/shard_map/ppermute | solution.py:541
  16.0 13.7 %collective-permute-start.7 = (f32[8,2,9,16,128]{4,3,2,1,0:T(8,128)S(1)}, f32[8,2,9,16,128]{4,3,2,1,0:T(8,128)S(1)}, u32[]{:S(2)}, u32[]{:S(2)}) collective-permute-start(f32[8,2,9,16,128]{4,3,2,1,0:T(8,128)S(1)} %get-tuple-element.32), channel_id=1, source_target_pairs={{0,1},{1,0},{2,3},{3,2},{4,5},{5,4},{6,7},{7,6},{8,9},{9,8},{10,11... | collective-permute-start | bytes 3538952 | tf_op jit(solution)/shard_map/ppermute | solution.py:541
  16.1 12.6 %collective-permute-start.3 = (f32[6,8,640]{2,1,0:T(8,128)S(1)}, f32[6,8,640]{2,1,0:T(8,128)S(1)}, u32[]{:S(2)}, u32[]{:S(2)}) collective-permute-start(f32[6,8,640]{2,1,0:T(8,128)S(1)} %get-tuple-element.26), channel_id=1, source_target_pairs={{0,12},{1,13},{2,14},{3,15},{4,0},{5,1},{6,2},{7,3},{8,4},{9,5},{1... | collective-permute-start | bytes 368648 | tf_op jit(solution)/shard_map/ppermute | solution.py:544
  20.8 8.9 %collective-permute-start.8 = (f32[2,8,1024]{2,1,0:T(8,128)S(1)}, f32[2,8,1024]{2,1,0:T(8,128)S(1)}, u32[]{:S(2)}, u32[]{:S(2)}) collective-permute-start(f32[2,8,1024]{2,1,0:T(8,128)S(1)} %get-tuple-element.34), channel_id=1, source_target_pairs={{0,1},{1,0},{2,3},{3,2},{4,5},{5,4},{6,7},{7,6},{8,9},{9,8},{10,11... | collective-permute-start | bytes 196616 | tf_op jit(solution)/shard_map/ppermute | solution.py:541
  20.9 6.7 %collective-permute-start.5 = (f32[3,8,640]{2,1,0:T(8,128)S(1)}, f32[3,8,640]{2,1,0:T(8,128)S(1)}, u32[]{:S(2)}, u32[]{:S(2)}) collective-permute-start(f32[3,8,640]{2,1,0:T(8,128)S(1)} %get-tuple-element.27), channel_id=1, source_target_pairs={{0,4},{1,5},{2,6},{3,7},{4,8},{5,9},{6,10},{7,11},{8,12},{9,13},{1... | collective-permute-start | bytes 184328 | tf_op jit(solution)/shard_map/ppermute | solution.py:544
  20.9 7.8 %collective-permute-start.4 = (f32[3,8,640]{2,1,0:T(8,128)S(1)}, f32[3,8,640]{2,1,0:T(8,128)S(1)}, u32[]{:S(2)}, u32[]{:S(2)}) collective-permute-start(f32[3,8,640]{2,1,0:T(8,128)S(1)} %get-tuple-element.27), channel_id=1, source_target_pairs={{0,8},{1,9},{2,10},{3,11},{4,12},{5,13},{6,14},{7,15},{8,0},{9,1},... | collective-permute-start | bytes 184328 | tf_op jit(solution)/shard_map/ppermute | solution.py:544
  31.4 4.3 %collective-permute-start.9 = (f32[2,8,1024]{2,1,0:T(8,128)S(1)}, f32[2,8,1024]{2,1,0:T(8,128)S(1)}, u32[]{:S(2)}, u32[]{:S(2)}) collective-permute-start(f32[2,8,1024]{2,1,0:T(8,128)S(1)} %shard_map.84.a), channel_id=1, source_target_pairs={{0,2},{1,3},{2,0},{3,1},{4,6},{5,7},{6,4},{7,5},{8,10},{9,11},{10,... | collective-permute-start | bytes 196616 | tf_op jit(solution)/shard_map/ppermute | solution.py:541
  32.2 1.2 %collective-permute-start.6 = (f32[3,8,512]{2,1,0:T(8,128)S(1)}, f32[3,8,512]{2,1,0:T(8,128)S(1)}, u32[]{:S(2)}, u32[]{:S(2)}) collective-permute-start(f32[3,8,512]{2,1,0:T(8,128)S(1)} %get-tuple-element.29), channel_id=1, source_target_pairs={{0,1},{1,0},{2,3},{3,2},{4,5},{5,4},{6,7},{7,6},{8,9},{9,8},{10,11... | collective-permute-start | bytes 147464 | tf_op jit(solution)/shard_map/ppermute | solution.py:541
  35.7 6.8 %collective-permute-start.12 = (f32[2,8,1024]{2,1,0:T(8,128)S(1)}, f32[2,8,1024]{2,1,0:T(8,128)S(1)}, u32[]{:S(2)}, u32[]{:S(2)}) collective-permute-start(f32[2,8,1024]{2,1,0:T(8,128)S(1)} %shard_map.85), channel_id=1, source_target_pairs={{0,12},{1,13},{2,14},{3,15},{4,8},{5,9},{6,10},{7,11},{8,4},{9,5},... | collective-permute-start | bytes 196616 | tf_op jit(solution)/shard_map/ppermute | solution.py:541
  38.2 6.4 %collective-permute-start.11 = (f32[2,8,1024]{2,1,0:T(8,128)S(1)}, f32[2,8,1024]{2,1,0:T(8,128)S(1)}, u32[]{:S(2)}, u32[]{:S(2)}) collective-permute-start(f32[2,8,1024]{2,1,0:T(8,128)S(1)} %shard_map.85), channel_id=1, source_target_pairs={{0,8},{1,9},{2,10},{3,11},{4,12},{5,13},{6,14},{7,15},{8,0},{9,1},... | collective-permute-start | bytes 196616 | tf_op jit(solution)/shard_map/ppermute | solution.py:541
  38.2 6.4 %collective-permute-start.10 = (f32[2,8,1024]{2,1,0:T(8,128)S(1)}, f32[2,8,1024]{2,1,0:T(8,128)S(1)}, u32[]{:S(2)}, u32[]{:S(2)}) collective-permute-start(f32[2,8,1024]{2,1,0:T(8,128)S(1)} %shard_map.85), channel_id=1, source_target_pairs={{0,4},{1,5},{2,6},{3,7},{4,0},{5,1},{6,2},{7,3},{8,12},{9,13},{10,... | collective-permute-start | bytes 196616 | tf_op jit(solution)/shard_map/ppermute | solution.py:541
  44.6 1.3 %collective-permute-start.13 = (f32[2,8,1024]{2,1,0:T(8,128)S(1)}, f32[2,8,1024]{2,1,0:T(8,128)S(1)}, u32[]{:S(2)}, u32[]{:S(2)}) collective-permute-start(f32[2,8,1024]{2,1,0:T(8,128)S(1)} %add_add_fusion.mine), channel_id=1, source_target_pairs={{0,1},{1,0},{2,3},{3,2},{4,5},{5,4},{6,7},{7,6},{8,9},{9,8},{10,11... | collective-permute-start | bytes 196616 | tf_op jit(solution)/shard_map/ppermute | solution.py:541

commit v5 on v4

--- a/solution.py
+++ b/solution.py
@@ -16,7 +16,7 @@
 PREPARE_COST = 40_000_000
 BASE_COST = 8_000_000
 CORRECT_COST = 4_000_000
-SPLIT_COST = 1000
+SPLIT_COST = 2_000_000
 EXACT = lax.Precision.HIGHEST
 
 
@@ -304,7 +304,7 @@
         store(right, 0, 2 * coarse_cols - window)
 
 
-def chip_pair(own, got, coarse_faces, order, out):
+def chip_pair(own, got, coarse_faces, out):
     cx, cy = coarse_faces[0], coarse_faces[1]
     first = lax.rem(lax.axis_index("tm"), 2) == 0
     g_own, g_got = read(own), read(got)
@@ -314,7 +314,7 @@
     write(out, add(w_low, g_high), 3)
 
 
-def row_pair(own, got, coarse_faces, order, through, out, out_t, passed):
+def row_pair(own, got, coarse_faces, order, out, out_t):
     cx, cy = coarse_faces[0], coarse_faces[1]
     first = lax.rem(lax.axis_index("tm") // 2, 2) == 0
     t_own, t_got = read(own), read(got)
@@ -387,7 +387,7 @@
     return fields
 
 
-def correct(kept, got, initial_in, corrected, done, initial, sem, *, steps):
+def correct(order, kept, got, initial_in, corrected, done, initial, sem, *, steps):
     load = pltpu.make_async_copy(initial_in, initial, sem)
     load.start()
     done[...] = jnp.zeros_like(done)
@@ -446,17 +446,16 @@
             other[i] = total[i][:, :half]
 
 
-def split_flow(order, velocity, own, sent, sems):
-    core = lax.rem(lax.axis_index("tm"), 2)
+def cut_flow(order, velocity, velocity_got, own, got, sems):
     blocks = own.shape[2]
-    right = velocity.shape[3] - blocks
-    for i, (out, start) in enumerate(((own, core * right), (sent, (1 - core) * right))):
-        source = velocity.at[:, :, :, pl.ds(start, blocks)]
+    start = lax.rem(lax.axis_index("tm"), 2) * (velocity.shape[3] - blocks)
+    for i, (source, out) in enumerate(((velocity, own), (velocity_got, got))):
+        source = source.at[:, :, :, pl.ds(start, blocks)]
         for tile in range(velocity.shape[2]):
             rows = pl.ds(tile * SUBLANES, SUBLANES)
             pltpu.make_async_copy(source.at[:, :, tile], out.at[:, :, :, rows], sems.at[i]).start()
     wait_all(own, sems.at[0])
-    wait_all(sent, sems.at[1])
+    wait_all(got, sems.at[1])
 
 
 def descend(starts, flow, flow_got, planes, grad, grad_got, mine):
@@ -492,6 +491,10 @@
     out[...] = a[...] + b[...]
 
 
+def plus_all(a, b, c, d, order, out):
+    out[...] = (a[...] + b[...]) + (c[...] + d[...])
+
+
 def weave(mine, other, out, stage, sem):
     first = lax.rem(lax.axis_index("tm"), 2) == 0
     half = stage.shape[1] // 2
@@ -508,14 +511,13 @@
     wait_all(stage, sem)
 
 
-def call(body, shapes, operands, *, specs=None, outs=None, scratch=(), aliases={}, cost=1000):
+def call(body, shapes, operands, *, specs=None, outs=None, scratch=(), cost=1000):
     return pl.pallas_call(
         body,
         out_shape=[jax.ShapeDtypeStruct(shape, jnp.float32) for shape in shapes],
         in_specs=specs or [VMEM] * len(operands),
         out_specs=outs or [VMEM] * len(shapes),
         scratch_shapes=scratch,
-        input_output_aliases=aliases,
         cost_estimate=pl.CostEstimate(flops=cost, bytes_accessed=cost, transcendentals=0),
         compiler_params=pltpu.CompilerParams(vmem_limit_bytes=32 * 1024 * 1024),
     )(*operands)
@@ -549,6 +551,7 @@
     tiled_in = dict(levels=levels, wet=wet_mask, initial=initial, forcing=forcing, velocity=velocity)
     tiled_in = {name: in_hbm(tiled(value)) for name, value in tiled_in.items()}
     pinned = in_hbm(initial)
+    velocity_got = paired(velocity, 1)
     following = lax.ppermute(initial, "tm", [(s, s - 1) for s in range(1, count)])
     own, sent, planes, window_planes, coarse_faces = call(
         prepare,
@@ -566,16 +569,8 @@
         cost=PREPARE_COST,
     )
     got = paired(sent, 1)
-    flow, flow_other = call(
-        split_flow,
-        [(steps, 2, window // LANES, rows, LANES)] * 2,
-        [own, tiled_in["velocity"]],
-        specs=[ANY, HBM],
-        scratch=[pltpu.SemaphoreType.DMA((2,))],
-        cost=SPLIT_COST,
-    )
     (chip,) = call(
-        chip_pair, [(6, *block)], [own, got, coarse_faces, flow], specs=[VMEM] * 3 + [ANY]
+        chip_pair, [(6, *block)], [own, got, coarse_faces]
     )
     grad, grad_other = call(
         base,
@@ -589,13 +584,11 @@
     rows_in_all = count // per_row
     if per_row == 4:
         partner = paired(chip, 2)
-        row, row_t, flow_other = call(
+        row, row_t = call(
             row_pair,
-            [(6, *block), (3, *block), flow_other.shape],
-            [chip, partner, coarse_faces, grad, flow_other],
-            specs=[VMEM] * 3 + [ANY] * 2,
-            outs=[VMEM] * 2 + [ANY],
-            aliases={4: 2},
+            [(6, *block), (3, *block)],
+            [chip, partner, coarse_faces, grad],
+            specs=[VMEM] * 3 + [ANY],
         )
     else:
         partner = None
@@ -614,7 +607,15 @@
             stride *= 2
         far, farther = back(row_t, 2 * per_row), None
 
-    flow_got, grad_got = paired(flow_other, 1), paired(grad_other, 1)
+    grad_got = paired(grad_other, 1)
+    flow, flow_got = call(
+        cut_flow,
+        [(steps, 2, window // LANES, rows, LANES)] * 2,
+        [row_t, tiled_in["velocity"], tiled(velocity_got)],
+        specs=[ANY, HBM, ANY],
+        scratch=[pltpu.SemaphoreType.DMA((2,))],
+        cost=SPLIT_COST,
+    )
 
     operands = {
         "near": near,
@@ -631,13 +632,14 @@
     def finish_body(*refs):
         given = dict.fromkeys(operands)
         given.update(zip(names, refs))
-        starts, kept, sent = refs[len(names) :]
+        starts, kept, sent = refs[len(names) + 1 :]
         finish(**given, starts=starts, kept=kept, sent=sent, per_row=per_row, rows_in_all=rows_in_all)
 
     starts, kept, sent = call(
         finish_body,
         [(6, *block), (3, half_rows, half), (3, half_rows, half)],
-        [operands[name] for name in names],
+        [operands[name] for name in names] + [flow],
+        specs=[VMEM] * len(names) + [ANY],
     )
     (mine,) = call(
         descend,
@@ -646,18 +648,19 @@
         cost=BASE_COST,
     )
     got = paired(sent, 1)
+    if per_row == 4:
+        (mine,) = call(plus, [mine.shape], [mine, paired(mine, 2), got], specs=[VMEM, VMEM, ANY])
     corrected, done = call(
         functools.partial(correct, steps=steps),
         [initial.shape, (8, LANES)],
-        [kept, got, pinned],
-        specs=[VMEM, VMEM, HBM],
+        [mine, kept, got, pinned],
+        specs=[ANY, VMEM, VMEM, HBM],
         scratch=[pltpu.VMEM(initial.shape, jnp.float32), pltpu.SemaphoreType.DMA],
         cost=CORRECT_COST,
     )
-    if per_row == 4:
-        (mine,) = call(plus, [mine.shape], [mine, paired(mine, 2), done], specs=[VMEM, VMEM, ANY])
     if rows_in_all == 4:
-        mine = mine + paired(mine, 4) + paired(mine, 8) + paired(mine, 12)
+        parts = [mine] + [paired(mine, stride) for stride in (4, 8, 12)]
+        (mine,) = call(plus_all, [mine.shape], parts + [done], specs=[VMEM] * 4 + [ANY])
     else:
         stride = per_row
         while stride < count:

time: 46.8 us -> 46 us (0.983)
  waiting for transfers between devices: 13.9 us -> 13.1 us
    ppermute x3, waiting for transfers between devices: 6.78 us -> 4.79 us  [back(): lax.ppermute(value, 'tm', [(s, (s - stride) % count) for s in range(count)])]
    ppermute x10, waiting for transfers between devices: 7.15 us -> 8.35 us  [paired(): return lax.ppermute(value, 'tm', [(s, s ^ stride) for s in range(count)])]
    pallas_call x10 -> x11, Pallas kernels: 15.1 us -> 14.7 us  [call(): pl.pallas_call(body, out_shape=[jax.ShapeDtypeStruct(shape, jnp.float32)...]
  transfers between devices with their start and end apart: 14 -> 14, of which waited for: 7 -> 8; matrix products, arithmetic and copies ran while one was open for 0% -> 0% of each run, Pallas kernels for 27% -> 27%
where the time goes in v5:
time: 46 us; the launch traced here: 45.8 us
  starting transfers between devices  17.1 us (37%)
  Pallas kernels  14.7 us (32%)
  waiting for transfers between devices  13.1 us (28%)
  between operations  0.74 us (2%)
    pallas_call x11, Pallas kernels, call(): pl.pallas_call(body, out_shape=[jax.ShapeDtypeStruct(shape, jnp.float32)...  14.7 us
    ppermute x10, starting transfers between devices, paired(): return lax.ppermute(value, 'tm', [(s, s ^ stride) for s in range(count)])  9.86 us
    ppermute x10, waiting for transfers between devices, paired(): return lax.ppermute(value, 'tm', [(s, s ^ stride) for s in range(count)])  8.35 us
    ppermute x3, starting transfers between devices, back(): lax.ppermute(value, 'tm', [(s, (s - stride) % count) for s in range(count)])  6.01 us
    ppermute x3, waiting for transfers between devices, back(): lax.ppermute(value, 'tm', [(s, (s - stride) % count) for s in range(count)])  4.79 us
    ppermute x1, starting transfers between devices, shards(): lax.ppermute(initial, 'tm', [(s, s - 1) for s in range(1, count)])  1.28 us
  transfers between devices with their start and end apart: 14, of which 8 were waited for; matrix products, arithmetic and copies ran while one was open for 0% of the time, Pallas kernels for 27%

profile of v5, /device:TPU:0, one launch (start us, length us, event | category | flops | bytes accessed | tf_op | source)
XLA Modules:
  0.0 45.8 jit_solution(16210825640668389759)
XLA Ops:
  0.6 0.5 %collective-permute-start.6 = (f32[8,2,16,2048]{3,2,1,0:T(8,128)}, f32[8,2,16,2048]{3,2,1,0:T(8,128)S(1)}, u32[]{:S(2)}, u32[]{:S(2)}) collective-permute-start(f32[8,2,16,2048]{3,2,1,0:T(8,128)} %param.7), channel_id=1, source_target_pairs={{0,1},{1,0},{2,3},{3,2},{4,5},{5,4},{6,7},{7,6},{8,9},{9,8},{10,11... | collective-permute-start | bytes 6291464 | tf_op jit(solution)/shard_map/ppermute | solution.py:543
  1.1 1.3 %collective-permute-start.2 = (f32[1,3,16,2048]{3,2,1,0:T(8,128)}, f32[1,3,16,2048]{3,2,1,0:T(8,128)S(1)}, u32[]{:S(2)}, u32[]{:S(2)}) collective-permute-start(f32[1,3,16,2048]{3,2,1,0:T(8,128)} %initial_in.1), channel_id=1, source_target_pairs={{1,0},{2,1},{3,2},{4,3},{5,4},{6,5},{7,6},{8,7},{9,8},{10,9},{11,1... | collective-permute-start | bytes 1179656 | tf_op jit(solution)/shard_map/ppermute | solution.py:555
  2.4 4.4 %shard_map.77 = (f32[6,8,640]{2,1,0:T(8,128)S(1)}, f32[6,8,640]{2,1,0:T(8,128)S(1)}, f32[6,8,2048]{2,1,0:T(8,128)S(1)}, f32[6,8,1152]{2,1,0:T(8,128)S(1)}, f32[2,8,640]{2,1,0:T(8,128)S(1)}) custom-call(f32[16]{0:T(128)} %table_in.1, s32[2,16,8,128]{3,2,1,0:T(8,128)} %bitcast.31, s32[2,16,8,128]{3,2,1,0:T(8,128)} %bitcast.32, ...), custom_call_target="tpu_custom_call" | custom-call | flops 40000000 | bytes 40000000 | tf_op jit(solution)/shard_map/pallas_call | solution.py:515
  6.8 1.2 %collective-permute-start = (f32[6,8,640]{2,1,0:T(8,128)S(1)}, f32[6,8,640]{2,1,0:T(8,128)S(1)}, u32[]{:S(2)}, u32[]{:S(2)}) collective-permute-start(f32[6,8,640]{2,1,0:T(8,128)S(1)} %get-tuple-element.19), channel_id=1, source_target_pairs={{0,1},{1,0},{2,3},{3,2},{4,5},{5,4},{6,7},{7,6},{8,9},{9,8},{10,11... | collective-permute-start | bytes 368648 | tf_op jit(solution)/shard_map/ppermute | solution.py:543
  8.0 1.0 %collective-permute-done.got.refs_4_ = f32[6,8,640]{2,1,0:T(8,128)S(1)} collective-permute-done((f32[6,8,640]{2,1,0:T(8,128)S(1)}, f32[6,8,640]{2,1,0:T(8,128)S(1)}, u32[]{:S(2)}, u32[]{:S(2)}) %collective-permute-start) | collective-permute-done | bytes 122912 | tf_op jit(solution)/shard_map/ppermute | solution.py:543
  9.0 0.1 shard_map.78.order.own.refs_5_
  9.1 2.6 %collective-permute-start.1 = (f32[6,8,640]{2,1,0:T(8,128)S(1)}, f32[6,8,640]{2,1,0:T(8,128)S(1)}, u32[]{:S(2)}, u32[]{:S(2)}) collective-permute-start(f32[6,8,640]{2,1,0:T(8,128)S(1)} %shard_map.78.order.own.refs_5_), channel_id=1, source_target_pairs={{0,2},{1,3},{2,0},{3,1},{4,6},{5,7},{6,4},{7,5},{8,10},{9,11},{10,... | collective-permute-start | bytes 368648 | tf_op jit(solution)/shard_map/ppermute | solution.py:543
  11.7 0.0 collective-permute-done.2
  11.7 3.2 %shard_map.79 = (f32[2,8,1024]{2,1,0:T(8,128)S(1)}, f32[2,8,1024]{2,1,0:T(8,128)S(1)}) custom-call(f32[6,8,640]{2,1,0:T(8,128)S(1)} %shard_map.78.order.own.refs_5_, f32[1,3,2,16,8,128]{5,4,3,2,1,0:T(8,128)S(1)} %bitcast.25, f32[8,2,16,8,128]{4,3,2,1,0:T(8,128)} %bitcast.29, f32[8,2,2,16,8,128]{5,4,3,2,1,0:T(8,128)} %bitcast.26, ...), custom_call_target="tpu_custom_call" | custom-call | flops 8000000 | bytes 8000000 | tf_op jit(solution)/shard_map/pallas_call | solution.py:515
  14.9 0.6 %collective-permute-done.1.got.refs_6_ = f32[6,8,640]{2,1,0:T(8,128)S(1)} collective-permute-done((f32[6,8,640]{2,1,0:T(8,128)S(1)}, f32[6,8,640]{2,1,0:T(8,128)S(1)}, u32[]{:S(2)}, u32[]{:S(2)}) %collective-permute-start.1) | collective-permute-done | bytes 122912 | tf_op jit(solution)/shard_map/ppermute | solution.py:543
  15.6 0.2 shard_map.80
  15.8 5.0 %collective-permute-start.3 = (f32[6,8,640]{2,1,0:T(8,128)S(1)}, f32[6,8,640]{2,1,0:T(8,128)S(1)}, u32[]{:S(2)}, u32[]{:S(2)}) collective-permute-start(f32[6,8,640]{2,1,0:T(8,128)S(1)} %get-tuple-element.23), channel_id=1, source_target_pairs={{0,12},{1,13},{2,14},{3,15},{4,0},{5,1},{6,2},{7,3},{8,4},{9,5},{1... | collective-permute-start | bytes 368648 | tf_op jit(solution)/shard_map/ppermute | solution.py:546
  20.8 0.0 collective-permute-start.7
  20.8 0.0 collective-permute-start.4
  20.8 1.0 %collective-permute-start.5 = (f32[3,8,640]{2,1,0:T(8,128)S(1)}, f32[3,8,640]{2,1,0:T(8,128)S(1)}, u32[]{:S(2)}, u32[]{:S(2)}) collective-permute-start(f32[3,8,640]{2,1,0:T(8,128)S(1)} %get-tuple-element.24.order), channel_id=1, source_target_pairs={{0,4},{1,5},{2,6},{3,7},{4,8},{5,9},{6,10},{7,11},{8,12},{9,13},{1... | collective-permute-start | bytes 184328 | tf_op jit(solution)/shard_map/ppermute | solution.py:546
  21.8 0.0 collective-permute-done.6
  21.8 1.3 %shard_map.81 = (f32[8,2,9,16,128]{4,3,2,1,0:T(8,128)S(1)}, f32[8,2,9,16,128]{4,3,2,1,0:T(8,128)S(1)}) custom-call(f32[3,8,640]{2,1,0:T(8,128)S(1)} %get-tuple-element.24.order, f32[8,2,2,16,8,128]{5,4,3,2,1,0:T(8,128)} %bitcast.27, f32[8,2,2,16,8,128]{5,4,3,2,1,0:T(8,128)S(1)} %bitcast.24), custom_call_target="tpu_custom_call" | custom-call | flops 2000000 | bytes 2000000 | tf_op jit(solution)/shard_map/pallas_call | solution.py:515
  23.0 4.8 %collective-permute-done.4.refs_1_ = f32[3,8,640]{2,1,0:T(8,128)S(1)} collective-permute-done((f32[3,8,640]{2,1,0:T(8,128)S(1)}, f32[3,8,640]{2,1,0:T(8,128)S(1)}, u32[]{:S(2)}, u32[]{:S(2)}) %collective-permute-start.4) | collective-permute-done | bytes 61472 | tf_op jit(solution)/shard_map/ppermute | solution.py:546
  27.8 0.0 collective-permute-done.5.refs_2_
  27.8 0.0 collective-permute-done.3.refs_0_
  27.8 0.9 %shard_map.82 = (f32[6,8,640]{2,1,0:T(8,128)S(1)}, f32[3,8,512]{2,1,0:T(8,128)S(1)}, f32[3,8,512]{2,1,0:T(8,128)S(1)}) custom-call(f32[6,8,640]{2,1,0:T(8,128)S(1)} %collective-permute-done.3.refs_0_, f32[3,8,640]{2,1,0:T(8,128)S(1)} %collective-permute-done.4.refs_1_, f32[3,8,640]{2,1,0:T(8,128)S(1)} %collective-permute-done.5.refs_2_, ...), custom_call_target="tpu_custom_call" | custom-call | flops 1000 | bytes 1000 | tf_op jit(solution)/shard_map/pallas_call | solution.py:515
  28.8 0.0 collective-permute-done.7.grad_got
  28.8 1.7 %shard_map.83.a = f32[2,8,1024]{2,1,0:T(8,128)S(1)} custom-call(f32[6,8,640]{2,1,0:T(8,128)S(1)} %get-tuple-element.26.starts, f32[8,2,9,16,128]{4,3,2,1,0:T(8,128)S(1)} %get-tuple-element.25.refs_8_.flow, f32[8,2,9,16,128]{4,3,2,1,0:T(8,128)S(1)} %get-tuple-element.27.flow_got, f32[6,8,1152]{2,1,0:T(8,128)S(1)} %get-tuple-element.28.planes, ...), custom_call_target="tpu_custom_call" | custom-call | flops 8000000 | bytes 8000000 | tf_op jit(solution)/shard_map/pallas_call | solution.py:515
  30.5 1.0 %collective-permute-start.8 = (f32[2,8,1024]{2,1,0:T(8,128)S(1)}, f32[2,8,1024]{2,1,0:T(8,128)S(1)}, u32[]{:S(2)}, u32[]{:S(2)}) collective-permute-start(f32[2,8,1024]{2,1,0:T(8,128)S(1)} %shard_map.83.a), channel_id=1, source_target_pairs={{0,2},{1,3},{2,0},{3,1},{4,6},{5,7},{6,4},{7,5},{8,10},{9,11},{10,... | collective-permute-start | bytes 196616 | tf_op jit(solution)/shard_map/ppermute | solution.py:543
  31.5 0.0 collective-permute-start.9
  31.5 1.2 %collective-permute-done.9.order.got = f32[3,8,512]{2,1,0:T(8,128)S(1)} collective-permute-done((f32[3,8,512]{2,1,0:T(8,128)S(1)}, f32[3,8,512]{2,1,0:T(8,128)S(1)}, u32[]{:S(2)}, u32[]{:S(2)}) %collective-permute-start.9) | collective-permute-done | bytes 49184 | tf_op jit(solution)/shard_map/ppermute | solution.py:543
  32.7 2.1 %collective-permute-done.8.b = f32[2,8,1024]{2,1,0:T(8,128)S(1)} collective-permute-done((f32[2,8,1024]{2,1,0:T(8,128)S(1)}, f32[2,8,1024]{2,1,0:T(8,128)S(1)}, u32[]{:S(2)}, u32[]{:S(2)}) %collective-permute-start.8) | collective-permute-done | bytes 65568 | tf_op jit(solution)/shard_map/ppermute | solution.py:543
  34.8 0.5 %collective-permute-start.10 = (f32[2,8,1024]{2,1,0:T(8,128)S(1)}, f32[2,8,1024]{2,1,0:T(8,128)S(1)}, u32[]{:S(2)}, u32[]{:S(2)}) collective-permute-start(f32[2,8,1024]{2,1,0:T(8,128)S(1)} %shard_map.84.order.a), channel_id=1, source_target_pairs={{0,4},{1,5},{2,6},{3,7},{4,0},{5,1},{6,2},{7,3},{8,12},{9,13},{10,... | collective-permute-start | bytes 196616 | tf_op jit(solution)/shard_map/ppermute | solution.py:543
  35.4 2.2 %collective-permute-start.11 = (f32[2,8,1024]{2,1,0:T(8,128)S(1)}, f32[2,8,1024]{2,1,0:T(8,128)S(1)}, u32[]{:S(2)}, u32[]{:S(2)}) collective-permute-start(f32[2,8,1024]{2,1,0:T(8,128)S(1)} %shard_map.84.order.a), channel_id=1, source_target_pairs={{0,8},{1,9},{2,10},{3,11},{4,12},{5,13},{6,14},{7,15},{8,0},{9,1},... | collective-permute-start | bytes 196616 | tf_op jit(solution)/shard_map/ppermute | solution.py:543
  37.6 1.7 %collective-permute-start.12 = (f32[2,8,1024]{2,1,0:T(8,128)S(1)}, f32[2,8,1024]{2,1,0:T(8,128)S(1)}, u32[]{:S(2)}, u32[]{:S(2)}) collective-permute-start(f32[2,8,1024]{2,1,0:T(8,128)S(1)} %shard_map.84.order.a), channel_id=1, source_target_pairs={{0,12},{1,13},{2,14},{3,15},{4,8},{5,9},{6,10},{7,11},{8,4},{9,5},... | collective-permute-start | bytes 196616 | tf_op jit(solution)/shard_map/ppermute | solution.py:543
  39.3 2.3 %shard_map.85 = (f32[1,3,16,2048]{3,2,1,0:T(8,128)}, f32[8,128]{1,0:T(8,128)S(1)}) custom-call(f32[2,8,1024]{2,1,0:T(8,128)S(1)} %shard_map.84.order.a, f32[3,8,512]{2,1,0:T(8,128)S(1)} %get-tuple-element.31.kept, f32[3,8,512]{2,1,0:T(8,128)S(1)} %collective-permute-done.9.order.got, f32[1,3,16,2048]{3,2,1,0:T(8,128)} %initial_in.1), custom_call_target="tpu_custom_call" | custom-call | flops 4000000 | bytes 4000000 | tf_op jit(solution)/shard_map/pallas_call | solution.py:515
  41.6 0.0 collective-permute-done.10.b
  41.6 0.9 %collective-permute-done.11.c = f32[2,8,1024]{2,1,0:T(8,128)S(1)} collective-permute-done((f32[2,8,1024]{2,1,0:T(8,128)S(1)}, f32[2,8,1024]{2,1,0:T(8,128)S(1)}, u32[]{:S(2)}, u32[]{:S(2)}) %collective-permute-start.11) | collective-permute-done | bytes 65568 | tf_op jit(solution)/shard_map/ppermute | solution.py:543
  42.5 1.3 %collective-permute-done.12.d = f32[2,8,1024]{2,1,0:T(8,128)S(1)} collective-permute-done((f32[2,8,1024]{2,1,0:T(8,128)S(1)}, f32[2,8,1024]{2,1,0:T(8,128)S(1)}, u32[]{:S(2)}, u32[]{:S(2)}) %collective-permute-start.12) | collective-permute-done | bytes 65568 | tf_op jit(solution)/shard_map/ppermute | solution.py:543
  43.8 0.1 collective-permute-start.13
  43.9 1.2 %collective-permute-done.13.other = f32[2,8,1024]{2,1,0:T(8,128)S(1)} collective-permute-done((f32[2,8,1024]{2,1,0:T(8,128)S(1)}, f32[2,8,1024]{2,1,0:T(8,128)S(1)}, u32[]{:S(2)}, u32[]{:S(2)}) %collective-permute-start.13) | collective-permute-done | bytes 65568 | tf_op jit(solution)/shard_map/ppermute | solution.py:543
  45.1 0.7 %shard_map.87 = f32[2,16,8,128]{3,2,1,0:T(8,128)} custom-call(f32[2,8,1024]{2,1,0:T(8,128)S(1)} %shard_map.86.mine, f32[2,8,1024]{2,1,0:T(8,128)S(1)} %collective-permute-done.13.other), custom_call_target="tpu_custom_call" | custom-call | flops 1000 | bytes 1000 | tf_op jit(solution)/shard_map/pallas_call | solution.py:515
  (2 shorter events, 0.0 us)
Async XLA Ops:
  0.6 21.1 %collective-permute-start.6 = (f32[8,2,16,2048]{3,2,1,0:T(8,128)}, f32[8,2,16,2048]{3,2,1,0:T(8,128)S(1)}, u32[]{:S(2)}, u32[]{:S(2)}) collective-permute-start(f32[8,2,16,2048]{3,2,1,0:T(8,128)} %param.7), channel_id=1, source_target_pairs={{0,1},{1,0},{2,3},{3,2},{4,5},{5,4},{6,7},{7,6},{8,9},{9,8},{10,11... | collective-permute-start | bytes 6291464 | tf_op jit(solution)/shard_map/ppermute | solution.py:543
  1.1 10.6 %collective-permute-start.2 = (f32[1,3,16,2048]{3,2,1,0:T(8,128)}, f32[1,3,16,2048]{3,2,1,0:T(8,128)S(1)}, u32[]{:S(2)}, u32[]{:S(2)}) collective-permute-start(f32[1,3,16,2048]{3,2,1,0:T(8,128)} %initial_in.1), channel_id=1, source_target_pairs={{1,0},{2,1},{3,2},{4,3},{5,4},{6,5},{7,6},{8,7},{9,8},{10,9},{11,1... | collective-permute-start | bytes 1179656 | tf_op jit(solution)/shard_map/ppermute | solution.py:555
  6.8 2.2 %collective-permute-start = (f32[6,8,640]{2,1,0:T(8,128)S(1)}, f32[6,8,640]{2,1,0:T(8,128)S(1)}, u32[]{:S(2)}, u32[]{:S(2)}) collective-permute-start(f32[6,8,640]{2,1,0:T(8,128)S(1)} %get-tuple-element.19), channel_id=1, source_target_pairs={{0,1},{1,0},{2,3},{3,2},{4,5},{5,4},{6,7},{7,6},{8,9},{9,8},{10,11... | collective-permute-start | bytes 368648 | tf_op jit(solution)/shard_map/ppermute | solution.py:543
  9.1 6.5 %collective-permute-start.1 = (f32[6,8,640]{2,1,0:T(8,128)S(1)}, f32[6,8,640]{2,1,0:T(8,128)S(1)}, u32[]{:S(2)}, u32[]{:S(2)}) collective-permute-start(f32[6,8,640]{2,1,0:T(8,128)S(1)} %shard_map.78.order.own.refs_5_), channel_id=1, source_target_pairs={{0,2},{1,3},{2,0},{3,1},{4,6},{5,7},{6,4},{7,5},{8,10},{9,11},{10,... | collective-permute-start | bytes 368648 | tf_op jit(solution)/shard_map/ppermute | solution.py:543
  15.8 12.1 %collective-permute-start.3 = (f32[6,8,640]{2,1,0:T(8,128)S(1)}, f32[6,8,640]{2,1,0:T(8,128)S(1)}, u32[]{:S(2)}, u32[]{:S(2)}) collective-permute-start(f32[6,8,640]{2,1,0:T(8,128)S(1)} %get-tuple-element.23), channel_id=1, source_target_pairs={{0,12},{1,13},{2,14},{3,15},{4,0},{5,1},{6,2},{7,3},{8,4},{9,5},{1... | collective-permute-start | bytes 368648 | tf_op jit(solution)/shard_map/ppermute | solution.py:546
  20.8 8.0 %collective-permute-start.7 = (f32[2,8,1024]{2,1,0:T(8,128)S(1)}, f32[2,8,1024]{2,1,0:T(8,128)S(1)}, u32[]{:S(2)}, u32[]{:S(2)}) collective-permute-start(f32[2,8,1024]{2,1,0:T(8,128)S(1)} %get-tuple-element.29), channel_id=1, source_target_pairs={{0,1},{1,0},{2,3},{3,2},{4,5},{5,4},{6,7},{7,6},{8,9},{9,8},{10,11... | collective-permute-start | bytes 196616 | tf_op jit(solution)/shard_map/ppermute | solution.py:543
  20.8 7.1 %collective-permute-start.4 = (f32[3,8,640]{2,1,0:T(8,128)S(1)}, f32[3,8,640]{2,1,0:T(8,128)S(1)}, u32[]{:S(2)}, u32[]{:S(2)}) collective-permute-start(f32[3,8,640]{2,1,0:T(8,128)S(1)} %get-tuple-element.24.order), channel_id=1, source_target_pairs={{0,8},{1,9},{2,10},{3,11},{4,12},{5,13},{6,14},{7,15},{8,0},{9,1},... | collective-permute-start | bytes 184328 | tf_op jit(solution)/shard_map/ppermute | solution.py:546
  20.8 7.1 %collective-permute-start.5 = (f32[3,8,640]{2,1,0:T(8,128)S(1)}, f32[3,8,640]{2,1,0:T(8,128)S(1)}, u32[]{:S(2)}, u32[]{:S(2)}) collective-permute-start(f32[3,8,640]{2,1,0:T(8,128)S(1)} %get-tuple-element.24.order), channel_id=1, source_target_pairs={{0,4},{1,5},{2,6},{3,7},{4,8},{5,9},{6,10},{7,11},{8,12},{9,13},{1... | collective-permute-start | bytes 184328 | tf_op jit(solution)/shard_map/ppermute | solution.py:546
  30.5 4.3 %collective-permute-start.8 = (f32[2,8,1024]{2,1,0:T(8,128)S(1)}, f32[2,8,1024]{2,1,0:T(8,128)S(1)}, u32[]{:S(2)}, u32[]{:S(2)}) collective-permute-start(f32[2,8,1024]{2,1,0:T(8,128)S(1)} %shard_map.83.a), channel_id=1, source_target_pairs={{0,2},{1,3},{2,0},{3,1},{4,6},{5,7},{6,4},{7,5},{8,10},{9,11},{10,... | collective-permute-start | bytes 196616 | tf_op jit(solution)/shard_map/ppermute | solution.py:543
  31.5 1.2 %collective-permute-start.9 = (f32[3,8,512]{2,1,0:T(8,128)S(1)}, f32[3,8,512]{2,1,0:T(8,128)S(1)}, u32[]{:S(2)}, u32[]{:S(2)}) collective-permute-start(f32[3,8,512]{2,1,0:T(8,128)S(1)} %get-tuple-element.30), channel_id=1, source_target_pairs={{0,1},{1,0},{2,3},{3,2},{4,5},{5,4},{6,7},{7,6},{8,9},{9,8},{10,11... | collective-permute-start | bytes 147464 | tf_op jit(solution)/shard_map/ppermute | solution.py:543
  34.8 6.7 %collective-permute-start.10 = (f32[2,8,1024]{2,1,0:T(8,128)S(1)}, f32[2,8,1024]{2,1,0:T(8,128)S(1)}, u32[]{:S(2)}, u32[]{:S(2)}) collective-permute-start(f32[2,8,1024]{2,1,0:T(8,128)S(1)} %shard_map.84.order.a), channel_id=1, source_target_pairs={{0,4},{1,5},{2,6},{3,7},{4,0},{5,1},{6,2},{7,3},{8,12},{9,13},{10,... | collective-permute-start | bytes 196616 | tf_op jit(solution)/shard_map/ppermute | solution.py:543
  35.4 7.1 %collective-permute-start.11 = (f32[2,8,1024]{2,1,0:T(8,128)S(1)}, f32[2,8,1024]{2,1,0:T(8,128)S(1)}, u32[]{:S(2)}, u32[]{:S(2)}) collective-permute-start(f32[2,8,1024]{2,1,0:T(8,128)S(1)} %shard_map.84.order.a), channel_id=1, source_target_pairs={{0,8},{1,9},{2,10},{3,11},{4,12},{5,13},{6,14},{7,15},{8,0},{9,1},... | collective-permute-start | bytes 196616 | tf_op jit(solution)/shard_map/ppermute | solution.py:543
  37.6 6.2 %collective-permute-start.12 = (f32[2,8,1024]{2,1,0:T(8,128)S(1)}, f32[2,8,1024]{2,1,0:T(8,128)S(1)}, u32[]{:S(2)}, u32[]{:S(2)}) collective-permute-start(f32[2,8,1024]{2,1,0:T(8,128)S(1)} %shard_map.84.order.a), channel_id=1, source_target_pairs={{0,12},{1,13},{2,14},{3,15},{4,8},{5,9},{6,10},{7,11},{8,4},{9,5},... | collective-permute-start | bytes 196616 | tf_op jit(solution)/shard_map/ppermute | solution.py:543
  43.8 1.3 %collective-permute-start.13 = (f32[2,8,1024]{2,1,0:T(8,128)S(1)}, f32[2,8,1024]{2,1,0:T(8,128)S(1)}, u32[]{:S(2)}, u32[]{:S(2)}) collective-permute-start(f32[2,8,1024]{2,1,0:T(8,128)S(1)} %shard_map.86.mine), channel_id=1, source_target_pairs={{0,1},{1,0},{2,3},{3,2},{4,5},{5,4},{6,7},{7,6},{8,9},{9,8},{10,11... | collective-permute-start | bytes 196616 | tf_op jit(solution)/shard_map/ppermute | solution.py:543

commit v6 on v5

--- a/solution.py
+++ b/solution.py
@@ -59,11 +59,15 @@
     return [pair[0], jnp.where(index_of(pair[1].shape, 0) < rows - 1, pair[1], 0.0)]
 
 
-def rows_of(ref, *at):
+def rows_of(ref, *at, first=0, blocks=None):
     half = ref.shape[-2] // 2
     return [
         jnp.concatenate(
-            [ref[(*at, v, pl.ds(parity, half, stride=2), slice(None))] for v in range(ref.shape[-3])], axis=1
+            [
+                ref[(*at, first + v, pl.ds(parity, half, stride=2), slice(None))]
+                for v in range(blocks or ref.shape[-3])
+            ],
+            axis=1,
         )
         for parity in range(2)
     ]
@@ -216,21 +220,23 @@
     wet,
     initial,
     forcing,
+    velocity,
     own,
     sent,
     planes,
     window_planes,
     coarse_faces,
+    stage_f,
+    flow,
     table,
     stage_l,
     stage_w,
     stage_i,
-    stage_f,
     sems,
 ):
-    load_table = pltpu.make_async_copy(table_in, table, sems.at[4])
+    load_table = pltpu.make_async_copy(table_in, table, sems.at[5])
     load_table.start()
-    sources = ((levels, stage_l), (wet, stage_w), (initial.at[0], stage_i), (forcing, stage_f))
+    sources = ((levels, stage_l), (wet, stage_w), (initial.at[0], stage_i), (forcing, stage_f), (velocity, flow))
     for i, (source, stage) in enumerate(sources):
         for copy in spread_copies(source, stage, sems.at[i]):
             copy.start()
@@ -303,6 +309,8 @@
     def _():
         store(right, 0, 2 * coarse_cols - window)
 
+    wait_all(flow, sems.at[4])
+
 
 def chip_pair(own, got, coarse_faces, out):
     cx, cy = coarse_faces[0], coarse_faces[1]
@@ -407,21 +415,17 @@
     ]
 
 
-def base(order, following, forcing, velocity, planes, mine, other, stage_i, stage_f, flow, sems):
-    sources = ((following.at[0], stage_i), (forcing, stage_f), (velocity, flow))
-    for i, (source, stage) in enumerate(sources):
-        for copy in spread_copies(source, stage, sems.at[i]):
-            copy.start()
-    steps = forcing.shape[0]
+def base(order, following, stage_f, flow, planes, mine, other, stage_i, sem):
+    for copy in spread_copies(following.at[0], stage_i, sem):
+        copy.start()
+    steps = flow.shape[0]
     device = lax.axis_index("tm")
     there = jnp.where(device + 1 < lax.axis_size("tm"), 1.0, 0.0)
     face_x, face_y = [planes[0], planes[1]], [planes[2], planes[3]]
-    wait_all(stage_i, sems.at[0])
+    wait_all(stage_i, sem)
     s = [v * there for v in rows_of(stage_i, 0)]
     e = inside_x([v * (there * COURANT) for v in rows_of(stage_i, 1)])
     n = inside_y([v * (there * COURANT) for v in rows_of(stage_i, 2)])
-    wait_all(stage_f, sems.at[1])
-    wait_all(flow, sems.at[2])
     sums = [[jnp.zeros_like(v) for v in s] for _ in range(2)]
     for step in reversed(range(steps)):
         s, e, n, *slopes = fine_step(s, e, n, face_x, face_y)
@@ -446,16 +450,12 @@
             other[i] = total[i][:, :half]
 
 
-def cut_flow(order, velocity, velocity_got, own, got, sems):
-    blocks = own.shape[2]
+def cut_flow(order, velocity, out, sem):
+    blocks = out.shape[2]
     start = lax.rem(lax.axis_index("tm"), 2) * (velocity.shape[3] - blocks)
-    for i, (source, out) in enumerate(((velocity, own), (velocity_got, got))):
-        source = source.at[:, :, :, pl.ds(start, blocks)]
-        for tile in range(velocity.shape[2]):
-            rows = pl.ds(tile * SUBLANES, SUBLANES)
-            pltpu.make_async_copy(source.at[:, :, tile], out.at[:, :, :, rows], sems.at[i]).start()
-    wait_all(own, sems.at[0])
-    wait_all(got, sems.at[1])
+    for copy in spread_copies(velocity.at[:, :, :, pl.ds(start, blocks)], out, sem):
+        copy.start()
+    wait_all(out, sem)
 
 
 def descend(starts, flow, flow_got, planes, grad, grad_got, mine):
@@ -470,13 +470,15 @@
     fields = [field[:, :window] for field in prolong_columns(fields)]
     face_x, face_y = inside_x([planes[0], planes[1]]), [planes[2], planes[3]]
     total = None
-    for k, velocity in enumerate((flow, flow_got)):
+    blocks = flow_got.shape[2]
+    start = jnp.where(first, 0, flow.shape[2] - blocks)
+    for k, (velocity, at) in enumerate(((flow, start), (flow_got, 0))):
         s, e, n = fields[3 * k : 3 * k + 3]
         e, n = e * inverse, n * inverse
         s, e, n = [s, s], inside_x([e, e]), inside_y([n, n])
         for step in reversed(range(steps)):
             s, e, n, *slopes = fine_step(s, e, n, face_x, face_y)
-            terms = [[d * v for d, v in zip(slopes[i], rows_of(velocity, step, i))] for i in range(2)]
+            terms = [[d * v for d, v in zip(slopes[i], rows_of(velocity, step, i, first=at, blocks=blocks))] for i in range(2)]
             if total is None:
                 total = terms
             else:
@@ -553,18 +555,25 @@
     pinned = in_hbm(initial)
     velocity_got = paired(velocity, 1)
     following = lax.ppermute(initial, "tm", [(s, s - 1) for s in range(1, count)])
-    own, sent, planes, window_planes, coarse_faces = call(
+    own, sent, planes, window_planes, coarse_faces, staged_forcing, flow = call(
         prepare,
-        [(6, *block), (6, *block), (6, *plane), (6, half_rows, window), (2, *block)],
-        [in_hbm(depth_table), *(tiled_in[name] for name in ("levels", "wet", "initial", "forcing"))],
-        specs=[HBM] * 5,
+        [
+            (6, *block),
+            (6, *block),
+            (6, *plane),
+            (6, half_rows, window),
+            (2, *block),
+            (steps, blocks, rows, LANES),
+            (steps, 2, blocks, rows, LANES),
+        ],
+        [in_hbm(depth_table), *(tiled_in[name] for name in ("levels", "wet", "initial", "forcing", "velocity"))],
+        specs=[HBM] * 6,
         scratch=[
             pltpu.SMEM(depth_table.shape, jnp.float32),
             stage(kind=jnp.int32),
             stage(kind=jnp.int32),
             stage(3),
-            stage(steps),
-            pltpu.SemaphoreType.DMA((5,)),
+            pltpu.SemaphoreType.DMA((6,)),
         ],
         cost=PREPARE_COST,
     )
@@ -575,11 +584,12 @@
     grad, grad_other = call(
         base,
         [(2, half_rows, cols // 2)] * 2,
-        [chip, tiled(following), tiled_in["forcing"], tiled_in["velocity"], planes],
-        specs=[ANY, VMEM, HBM, HBM, VMEM],
-        scratch=[stage(3), stage(steps), stage(steps, 2), pltpu.SemaphoreType.DMA((3,))],
+        [chip, tiled(following), staged_forcing, flow, planes],
+        specs=[ANY] + [VMEM] * 4,
+        scratch=[stage(3), pltpu.SemaphoreType.DMA],
         cost=BASE_COST,
     )
+    grad_got = paired(grad_other, 1)
     per_row = 4 if count <= 16 else 2
     rows_in_all = count // per_row
     if per_row == 4:
@@ -587,7 +597,7 @@
         row, row_t = call(
             row_pair,
             [(6, *block), (3, *block)],
-            [chip, partner, coarse_faces, grad],
+            [chip, partner, coarse_faces, grad_got],
             specs=[VMEM] * 3 + [ANY],
         )
     else:
@@ -607,13 +617,12 @@
             stride *= 2
         far, farther = back(row_t, 2 * per_row), None
 
-    grad_got = paired(grad_other, 1)
-    flow, flow_got = call(
+    (flow_got,) = call(
         cut_flow,
-        [(steps, 2, window // LANES, rows, LANES)] * 2,
-        [row_t, tiled_in["velocity"], tiled(velocity_got)],
-        specs=[ANY, HBM, ANY],
-        scratch=[pltpu.SemaphoreType.DMA((2,))],
+        [(steps, 2, window // LANES, rows, LANES)],
+        [row_t, tiled(velocity_got)],
+        specs=[ANY, ANY],
+        scratch=[pltpu.SemaphoreType.DMA],
         cost=SPLIT_COST,
     )
 
@@ -638,7 +647,7 @@
     starts, kept, sent = call(
         finish_body,
         [(6, *block), (3, half_rows, half), (3, half_rows, half)],
-        [operands[name] for name in names] + [flow],
+        [operands[name] for name in names] + [flow_got],
         specs=[VMEM] * len(names) + [ANY],
     )
     (mine,) = call(

time: 46 us -> 45.6 us (level)
  Pallas kernels: 14.7 us -> 11.8 us
  waiting for transfers between devices: 13.1 us -> 15.7 us
    pallas_call x11, Pallas kernels: 14.7 us -> 11.8 us  [call(): pl.pallas_call(body, out_shape=[jax.ShapeDtypeStruct(shape, jnp.float32)...]
    ppermute x10, waiting for transfers between devices: 8.35 us -> 10.6 us  [paired(): return lax.ppermute(value, 'tm', [(s, s ^ stride) for s in range(count)])]
  transfers between devices with their start and end apart: 14 -> 14, of which waited for: 8 -> 8; matrix products, arithmetic and copies ran while one was open for 0% -> 0% of each run, Pallas kernels for 27% -> 19%
where the time goes in v6:
time: 45.6 us; the launch traced here: 45.5 us
  starting transfers between devices  17.2 us (38%)
  waiting for transfers between devices  15.7 us (34%)
  Pallas kernels  11.8 us (26%)
  between operations  0.74 us (2%)
    pallas_call x11, Pallas kernels, call(): pl.pallas_call(body, out_shape=[jax.ShapeDtypeStruct(shape, jnp.float32)...  11.8 us
    ppermute x10, waiting for transfers between devices, paired(): return lax.ppermute(value, 'tm', [(s, s ^ stride) for s in range(count)])  10.6 us
    ppermute x10, starting transfers between devices, paired(): return lax.ppermute(value, 'tm', [(s, s ^ stride) for s in range(count)])  9.88 us
    ppermute x3, starting transfers between devices, back(): lax.ppermute(value, 'tm', [(s, (s - stride) % count) for s in range(count)])  6.01 us
    ppermute x3, waiting for transfers between devices, back(): lax.ppermute(value, 'tm', [(s, (s - stride) % count) for s in range(count)])  5.14 us
    ppermute x1, starting transfers between devices, shards(): lax.ppermute(initial, 'tm', [(s, s - 1) for s in range(1, count)])  1.28 us
  transfers between devices with their start and end apart: 14, of which 8 were waited for; matrix products, arithmetic and copies ran while one was open for 0% of the time, Pallas kernels for 19%

profile of v6, /device:TPU:0, one launch (start us, length us, event | category | flops | bytes accessed | tf_op | source)
XLA Modules:
  0.0 45.5 jit_solution(8034185378582601625)
XLA Ops:
  0.6 0.5 %collective-permute-start.7 = (f32[8,2,16,2048]{3,2,1,0:T(8,128)}, f32[8,2,16,2048]{3,2,1,0:T(8,128)S(1)}, u32[]{:S(2)}, u32[]{:S(2)}) collective-permute-start(f32[8,2,16,2048]{3,2,1,0:T(8,128)} %param.7), channel_id=1, source_target_pairs={{0,1},{1,0},{2,3},{3,2},{4,5},{5,4},{6,7},{7,6},{8,9},{9,8},{10,11... | collective-permute-start | bytes 6291464 | tf_op jit(solution)/shard_map/ppermute | solution.py:545
  1.1 1.3 %collective-permute-start.2 = (f32[1,3,16,2048]{3,2,1,0:T(8,128)}, f32[1,3,16,2048]{3,2,1,0:T(8,128)S(1)}, u32[]{:S(2)}, u32[]{:S(2)}) collective-permute-start(f32[1,3,16,2048]{3,2,1,0:T(8,128)} %initial_in.1), channel_id=1, source_target_pairs={{1,0},{2,1},{3,2},{4,3},{5,4},{6,5},{7,6},{8,7},{9,8},{10,9},{11,1... | collective-permute-start | bytes 1179656 | tf_op jit(solution)/shard_map/ppermute | solution.py:557
  2.4 4.4 %shard_map.77 = (f32[6,8,640]{2,1,0:T(8,128)S(1)}, f32[6,8,640]{2,1,0:T(8,128)S(1)}, f32[6,8,2048]{2,1,0:T(8,128)S(1)}, f32[6,8,1152]{2,1,0:T(8,128)S(1)}, f32[2...) custom-call(f32[16]{0:T(128)} %table_in.1, s32[2,16,8,128]{3,2,1,0:T(8,128)} %bitcast.29, ...), custom_call_target="tpu_custom_call" | custom-call | flops 40000000 | bytes 40000000 | tf_op jit(solution)/shard_map/pallas_call | solution.py:517
  6.9 1.2 %collective-permute-start = (f32[6,8,640]{2,1,0:T(8,128)S(1)}, f32[6,8,640]{2,1,0:T(8,128)S(1)}, u32[]{:S(2)}, u32[]{:S(2)}) collective-permute-start(f32[6,8,640]{2,1,0:T(8,128)S(1)} %get-tuple-element.19), channel_id=1, source_target_pairs={{0,1},{1,0},{2,3},{3,2},{4,5},{5,4},{6,7},{7,6},{8,9},{9,8},{10,11... | collective-permute-start | bytes 368648 | tf_op jit(solution)/shard_map/ppermute | solution.py:545
  8.1 1.0 %collective-permute-done.got.refs_4_ = f32[6,8,640]{2,1,0:T(8,128)S(1)} collective-permute-done((f32[6,8,640]{2,1,0:T(8,128)S(1)}, f32[6,8,640]{2,1,0:T(8,128)S(1)}, u32[]{:S(2)}, u32[]{:S(2)}) %collective-permute-start) | collective-permute-done | bytes 122912 | tf_op jit(solution)/shard_map/ppermute | solution.py:545
  9.0 0.1 shard_map.78.order.own.refs_5_
  9.2 2.6 %collective-permute-start.1 = (f32[6,8,640]{2,1,0:T(8,128)S(1)}, f32[6,8,640]{2,1,0:T(8,128)S(1)}, u32[]{:S(2)}, u32[]{:S(2)}) collective-permute-start(f32[6,8,640]{2,1,0:T(8,128)S(1)} %shard_map.78.order.own.refs_5_), channel_id=1, source_target_pairs={{0,2},{1,3},{2,0},{3,1},{4,6},{5,7},{6,4},{7,5},{8,10},{9,11},{10,... | collective-permute-start | bytes 368648 | tf_op jit(solution)/shard_map/ppermute | solution.py:545
  11.8 0.0 collective-permute-done.2
  11.8 1.4 %shard_map.79 = (f32[2,8,1024]{2,1,0:T(8,128)S(1)}, f32[2,8,1024]{2,1,0:T(8,128)S(1)}) custom-call(f32[6,8,640]{2,1,0:T(8,128)S(1)} %shard_map.78.order.own.refs_5_, f32[1,3,2,16,8,128]{5,4,3,2,1,0:T(8,128)S(1)} %bitcast.25, f32[8,16,16,128]{3,2,1,0:T(8,128)S(1)} %get-tuple-element.21.stage_f, f32[8,2,16,16,128]{4,3,2,1,0:T(8,128)S(1)} %get-tuple-element.22.flow, ...), custom_call_target="tpu_custom_call" | custom-call | flops 8000000 | bytes 8000000 | tf_op jit(solution)/shard_map/pallas_call | solution.py:517
  13.2 0.1 collective-permute-start.3
  13.3 2.3 %collective-permute-done.1.got.refs_6_ = f32[6,8,640]{2,1,0:T(8,128)S(1)} collective-permute-done((f32[6,8,640]{2,1,0:T(8,128)S(1)}, f32[6,8,640]{2,1,0:T(8,128)S(1)}, u32[]{:S(2)}, u32[]{:S(2)}) %collective-permute-start.1) | collective-permute-done | bytes 122912 | tf_op jit(solution)/shard_map/ppermute | solution.py:545
  15.6 0.0 collective-permute-done.3.order.grad_got
  15.6 0.2 shard_map.80
  15.8 5.0 %collective-permute-start.4 = (f32[6,8,640]{2,1,0:T(8,128)S(1)}, f32[6,8,640]{2,1,0:T(8,128)S(1)}, u32[]{:S(2)}, u32[]{:S(2)}) collective-permute-start(f32[6,8,640]{2,1,0:T(8,128)S(1)} %get-tuple-element.25), channel_id=1, source_target_pairs={{0,12},{1,13},{2,14},{3,15},{4,0},{5,1},{6,2},{7,3},{8,4},{9,5},{1... | collective-permute-start | bytes 368648 | tf_op jit(solution)/shard_map/ppermute | solution.py:548
  20.8 0.0 collective-permute-start.5
  20.8 1.0 %collective-permute-start.6 = (f32[3,8,640]{2,1,0:T(8,128)S(1)}, f32[3,8,640]{2,1,0:T(8,128)S(1)}, u32[]{:S(2)}, u32[]{:S(2)}) collective-permute-start(f32[3,8,640]{2,1,0:T(8,128)S(1)} %get-tuple-element.26.order), channel_id=1, source_target_pairs={{0,4},{1,5},{2,6},{3,7},{4,8},{5,9},{6,10},{7,11},{8,12},{9,13},{1... | collective-permute-start | bytes 184328 | tf_op jit(solution)/shard_map/ppermute | solution.py:548
  21.8 0.0 collective-permute-done.7
  21.8 0.1 shard_map.81.refs_8_.flow_got
  21.9 5.1 %collective-permute-done.5.refs_1_ = f32[3,8,640]{2,1,0:T(8,128)S(1)} collective-permute-done((f32[3,8,640]{2,1,0:T(8,128)S(1)}, f32[3,8,640]{2,1,0:T(8,128)S(1)}, u32[]{:S(2)}, u32[]{:S(2)}) %collective-permute-start.5) | collective-permute-done | bytes 61472 | tf_op jit(solution)/shard_map/ppermute | solution.py:548
  27.1 0.0 collective-permute-done.6.refs_2_
  27.1 0.0 collective-permute-done.4.refs_0_
  27.1 0.9 %shard_map.82 = (f32[6,8,640]{2,1,0:T(8,128)S(1)}, f32[3,8,512]{2,1,0:T(8,128)S(1)}, f32[3,8,512]{2,1,0:T(8,128)S(1)}) custom-call(f32[6,8,640]{2,1,0:T(8,128)S(1)} %collective-permute-done.4.refs_0_, f32[3,8,640]{2,1,0:T(8,128)S(1)} %collective-permute-done.5.refs_1_, f32[3,8,640]{2,1,0:T(8,128)S(1)} %collective-permute-done.6.refs_2_, ...), custom_call_target="tpu_custom_call" | custom-call | flops 1000 | bytes 1000 | tf_op jit(solution)/shard_map/pallas_call | solution.py:517
  28.0 1.7 %shard_map.83.a = f32[2,8,1024]{2,1,0:T(8,128)S(1)} custom-call(f32[6,8,640]{2,1,0:T(8,128)S(1)} %get-tuple-element.27.starts, f32[8,2,16,16,128]{4,3,2,1,0:T(8,128)S(1)} %get-tuple-element.22.flow, f32[8,2,9,16,128]{4,3,2,1,0:T(8,128)S(1)} %shard_map.81.refs_8_.flow_got, f32[6,8,1152]{2,1,0:T(8,128)S(1)} %get-tuple-element.28.planes, ...), custom_call_target="tpu_custom_call" | custom-call | flops 8000000 | bytes 8000000 | tf_op jit(solution)/shard_map/pallas_call | solution.py:517
  29.7 0.9 %collective-permute-start.8 = (f32[2,8,1024]{2,1,0:T(8,128)S(1)}, f32[2,8,1024]{2,1,0:T(8,128)S(1)}, u32[]{:S(2)}, u32[]{:S(2)}) collective-permute-start(f32[2,8,1024]{2,1,0:T(8,128)S(1)} %shard_map.83.a), channel_id=1, source_target_pairs={{0,2},{1,3},{2,0},{3,1},{4,6},{5,7},{6,4},{7,5},{8,10},{9,11},{10,... | collective-permute-start | bytes 196616 | tf_op jit(solution)/shard_map/ppermute | solution.py:545
  30.6 0.0 collective-permute-start.9
  30.6 1.2 %collective-permute-done.9.order.got = f32[3,8,512]{2,1,0:T(8,128)S(1)} collective-permute-done((f32[3,8,512]{2,1,0:T(8,128)S(1)}, f32[3,8,512]{2,1,0:T(8,128)S(1)}, u32[]{:S(2)}, u32[]{:S(2)}) %collective-permute-start.9) | collective-permute-done | bytes 49184 | tf_op jit(solution)/shard_map/ppermute | solution.py:545
  31.8 2.2 %collective-permute-done.8.b = f32[2,8,1024]{2,1,0:T(8,128)S(1)} collective-permute-done((f32[2,8,1024]{2,1,0:T(8,128)S(1)}, f32[2,8,1024]{2,1,0:T(8,128)S(1)}, u32[]{:S(2)}, u32[]{:S(2)}) %collective-permute-start.8) | collective-permute-done | bytes 65568 | tf_op jit(solution)/shard_map/ppermute | solution.py:545
  34.1 1.0 %collective-permute-start.10 = (f32[2,8,1024]{2,1,0:T(8,128)S(1)}, f32[2,8,1024]{2,1,0:T(8,128)S(1)}, u32[]{:S(2)}, u32[]{:S(2)}) collective-permute-start(f32[2,8,1024]{2,1,0:T(8,128)S(1)} %shard_map.84.order.a), channel_id=1, source_target_pairs={{0,4},{1,5},{2,6},{3,7},{4,0},{5,1},{6,2},{7,3},{8,12},{9,13},{10,... | collective-permute-start | bytes 196616 | tf_op jit(solution)/shard_map/ppermute | solution.py:545
  35.0 2.3 %collective-permute-start.11 = (f32[2,8,1024]{2,1,0:T(8,128)S(1)}, f32[2,8,1024]{2,1,0:T(8,128)S(1)}, u32[]{:S(2)}, u32[]{:S(2)}) collective-permute-start(f32[2,8,1024]{2,1,0:T(8,128)S(1)} %shard_map.84.order.a), channel_id=1, source_target_pairs={{0,8},{1,9},{2,10},{3,11},{4,12},{5,13},{6,14},{7,15},{8,0},{9,1},... | collective-permute-start | bytes 196616 | tf_op jit(solution)/shard_map/ppermute | solution.py:545
  37.4 1.1 %collective-permute-start.12 = (f32[2,8,1024]{2,1,0:T(8,128)S(1)}, f32[2,8,1024]{2,1,0:T(8,128)S(1)}, u32[]{:S(2)}, u32[]{:S(2)}) collective-permute-start(f32[2,8,1024]{2,1,0:T(8,128)S(1)} %shard_map.84.order.a), channel_id=1, source_target_pairs={{0,12},{1,13},{2,14},{3,15},{4,8},{5,9},{6,10},{7,11},{8,4},{9,5},... | collective-permute-start | bytes 196616 | tf_op jit(solution)/shard_map/ppermute | solution.py:545
  38.5 2.3 %shard_map.85 = (f32[1,3,16,2048]{3,2,1,0:T(8,128)}, f32[8,128]{1,0:T(8,128)S(1)}) custom-call(f32[2,8,1024]{2,1,0:T(8,128)S(1)} %shard_map.84.order.a, f32[3,8,512]{2,1,0:T(8,128)S(1)} %get-tuple-element.31.kept, f32[3,8,512]{2,1,0:T(8,128)S(1)} %collective-permute-done.9.order.got, f32[1,3,16,2048]{3,2,1,0:T(8,128)} %initial_in.1), custom_call_target="tpu_custom_call" | custom-call | flops 4000000 | bytes 4000000 | tf_op jit(solution)/shard_map/pallas_call | solution.py:517
  40.8 0.0 collective-permute-done.10.b
  40.8 0.4 collective-permute-done.11.c
  41.2 2.2 %collective-permute-done.12.d = f32[2,8,1024]{2,1,0:T(8,128)S(1)} collective-permute-done((f32[2,8,1024]{2,1,0:T(8,128)S(1)}, f32[2,8,1024]{2,1,0:T(8,128)S(1)}, u32[]{:S(2)}, u32[]{:S(2)}) %collective-permute-start.12) | collective-permute-done | bytes 65568 | tf_op jit(solution)/shard_map/ppermute | solution.py:545
  43.5 0.1 collective-permute-start.13
  43.5 1.2 %collective-permute-done.13.other = f32[2,8,1024]{2,1,0:T(8,128)S(1)} collective-permute-done((f32[2,8,1024]{2,1,0:T(8,128)S(1)}, f32[2,8,1024]{2,1,0:T(8,128)S(1)}, u32[]{:S(2)}, u32[]{:S(2)}) %collective-permute-start.13) | collective-permute-done | bytes 65568 | tf_op jit(solution)/shard_map/ppermute | solution.py:545
  44.8 0.7 %shard_map.87 = f32[2,16,8,128]{3,2,1,0:T(8,128)} custom-call(f32[2,8,1024]{2,1,0:T(8,128)S(1)} %shard_map.86.mine, f32[2,8,1024]{2,1,0:T(8,128)S(1)} %collective-permute-done.13.other), custom_call_target="tpu_custom_call" | custom-call | flops 1000 | bytes 1000 | tf_op jit(solution)/shard_map/pallas_call | solution.py:517
  (2 shorter events, 0.0 us)
Async XLA Ops:
  0.6 21.2 %collective-permute-start.7 = (f32[8,2,16,2048]{3,2,1,0:T(8,128)}, f32[8,2,16,2048]{3,2,1,0:T(8,128)S(1)}, u32[]{:S(2)}, u32[]{:S(2)}) collective-permute-start(f32[8,2,16,2048]{3,2,1,0:T(8,128)} %param.7), channel_id=1, source_target_pairs={{0,1},{1,0},{2,3},{3,2},{4,5},{5,4},{6,7},{7,6},{8,9},{9,8},{10,11... | collective-permute-start | bytes 6291464 | tf_op jit(solution)/shard_map/ppermute | solution.py:545
  1.1 10.6 %collective-permute-start.2 = (f32[1,3,16,2048]{3,2,1,0:T(8,128)}, f32[1,3,16,2048]{3,2,1,0:T(8,128)S(1)}, u32[]{:S(2)}, u32[]{:S(2)}) collective-permute-start(f32[1,3,16,2048]{3,2,1,0:T(8,128)} %initial_in.1), channel_id=1, source_target_pairs={{1,0},{2,1},{3,2},{4,3},{5,4},{6,5},{7,6},{8,7},{9,8},{10,9},{11,1... | collective-permute-start | bytes 1179656 | tf_op jit(solution)/shard_map/ppermute | solution.py:557
  6.9 2.2 %collective-permute-start = (f32[6,8,640]{2,1,0:T(8,128)S(1)}, f32[6,8,640]{2,1,0:T(8,128)S(1)}, u32[]{:S(2)}, u32[]{:S(2)}) collective-permute-start(f32[6,8,640]{2,1,0:T(8,128)S(1)} %get-tuple-element.19), channel_id=1, source_target_pairs={{0,1},{1,0},{2,3},{3,2},{4,5},{5,4},{6,7},{7,6},{8,9},{9,8},{10,11... | collective-permute-start | bytes 368648 | tf_op jit(solution)/shard_map/ppermute | solution.py:545
  9.2 6.5 %collective-permute-start.1 = (f32[6,8,640]{2,1,0:T(8,128)S(1)}, f32[6,8,640]{2,1,0:T(8,128)S(1)}, u32[]{:S(2)}, u32[]{:S(2)}) collective-permute-start(f32[6,8,640]{2,1,0:T(8,128)S(1)} %shard_map.78.order.own.refs_5_), channel_id=1, source_target_pairs={{0,2},{1,3},{2,0},{3,1},{4,6},{5,7},{6,4},{7,5},{8,10},{9,11},{10,... | collective-permute-start | bytes 368648 | tf_op jit(solution)/shard_map/ppermute | solution.py:545
  13.2 2.4 %collective-permute-start.3 = (f32[2,8,1024]{2,1,0:T(8,128)S(1)}, f32[2,8,1024]{2,1,0:T(8,128)S(1)}, u32[]{:S(2)}, u32[]{:S(2)}) collective-permute-start(f32[2,8,1024]{2,1,0:T(8,128)S(1)} %get-tuple-element.24), channel_id=1, source_target_pairs={{0,1},{1,0},{2,3},{3,2},{4,5},{5,4},{6,7},{7,6},{8,9},{9,8},{10,11... | collective-permute-start | bytes 196616 | tf_op jit(solution)/shard_map/ppermute | solution.py:545
  15.8 11.3 %collective-permute-start.4 = (f32[6,8,640]{2,1,0:T(8,128)S(1)}, f32[6,8,640]{2,1,0:T(8,128)S(1)}, u32[]{:S(2)}, u32[]{:S(2)}) collective-permute-start(f32[6,8,640]{2,1,0:T(8,128)S(1)} %get-tuple-element.25), channel_id=1, source_target_pairs={{0,12},{1,13},{2,14},{3,15},{4,0},{5,1},{6,2},{7,3},{8,4},{9,5},{1... | collective-permute-start | bytes 368648 | tf_op jit(solution)/shard_map/ppermute | solution.py:548
  20.8 6.3 %collective-permute-start.5 = (f32[3,8,640]{2,1,0:T(8,128)S(1)}, f32[3,8,640]{2,1,0:T(8,128)S(1)}, u32[]{:S(2)}, u32[]{:S(2)}) collective-permute-start(f32[3,8,640]{2,1,0:T(8,128)S(1)} %get-tuple-element.26.order), channel_id=1, source_target_pairs={{0,8},{1,9},{2,10},{3,11},{4,12},{5,13},{6,14},{7,15},{8,0},{9,1},... | collective-permute-start | bytes 184328 | tf_op jit(solution)/shard_map/ppermute | solution.py:548
  20.8 6.3 %collective-permute-start.6 = (f32[3,8,640]{2,1,0:T(8,128)S(1)}, f32[3,8,640]{2,1,0:T(8,128)S(1)}, u32[]{:S(2)}, u32[]{:S(2)}) collective-permute-start(f32[3,8,640]{2,1,0:T(8,128)S(1)} %get-tuple-element.26.order), channel_id=1, source_target_pairs={{0,4},{1,5},{2,6},{3,7},{4,8},{5,9},{6,10},{7,11},{8,12},{9,13},{1... | collective-permute-start | bytes 184328 | tf_op jit(solution)/shard_map/ppermute | solution.py:548
  29.7 4.3 %collective-permute-start.8 = (f32[2,8,1024]{2,1,0:T(8,128)S(1)}, f32[2,8,1024]{2,1,0:T(8,128)S(1)}, u32[]{:S(2)}, u32[]{:S(2)}) collective-permute-start(f32[2,8,1024]{2,1,0:T(8,128)S(1)} %shard_map.83.a), channel_id=1, source_target_pairs={{0,2},{1,3},{2,0},{3,1},{4,6},{5,7},{6,4},{7,5},{8,10},{9,11},{10,... | collective-permute-start | bytes 196616 | tf_op jit(solution)/shard_map/ppermute | solution.py:545
  30.6 1.2 %collective-permute-start.9 = (f32[3,8,512]{2,1,0:T(8,128)S(1)}, f32[3,8,512]{2,1,0:T(8,128)S(1)}, u32[]{:S(2)}, u32[]{:S(2)}) collective-permute-start(f32[3,8,512]{2,1,0:T(8,128)S(1)} %get-tuple-element.30), channel_id=1, source_target_pairs={{0,1},{1,0},{2,3},{3,2},{4,5},{5,4},{6,7},{7,6},{8,9},{9,8},{10,11... | collective-permute-start | bytes 147464 | tf_op jit(solution)/shard_map/ppermute | solution.py:545
  34.1 6.7 %collective-permute-start.10 = (f32[2,8,1024]{2,1,0:T(8,128)S(1)}, f32[2,8,1024]{2,1,0:T(8,128)S(1)}, u32[]{:S(2)}, u32[]{:S(2)}) collective-permute-start(f32[2,8,1024]{2,1,0:T(8,128)S(1)} %shard_map.84.order.a), channel_id=1, source_target_pairs={{0,4},{1,5},{2,6},{3,7},{4,0},{5,1},{6,2},{7,3},{8,12},{9,13},{10,... | collective-permute-start | bytes 196616 | tf_op jit(solution)/shard_map/ppermute | solution.py:545
  35.0 6.2 %collective-permute-start.11 = (f32[2,8,1024]{2,1,0:T(8,128)S(1)}, f32[2,8,1024]{2,1,0:T(8,128)S(1)}, u32[]{:S(2)}, u32[]{:S(2)}) collective-permute-start(f32[2,8,1024]{2,1,0:T(8,128)S(1)} %shard_map.84.order.a), channel_id=1, source_target_pairs={{0,8},{1,9},{2,10},{3,11},{4,12},{5,13},{6,14},{7,15},{8,0},{9,1},... | collective-permute-start | bytes 196616 | tf_op jit(solution)/shard_map/ppermute | solution.py:545
  37.4 6.1 %collective-permute-start.12 = (f32[2,8,1024]{2,1,0:T(8,128)S(1)}, f32[2,8,1024]{2,1,0:T(8,128)S(1)}, u32[]{:S(2)}, u32[]{:S(2)}) collective-permute-start(f32[2,8,1024]{2,1,0:T(8,128)S(1)} %shard_map.84.order.a), channel_id=1, source_target_pairs={{0,12},{1,13},{2,14},{3,15},{4,8},{5,9},{6,10},{7,11},{8,4},{9,5},... | collective-permute-start | bytes 196616 | tf_op jit(solution)/shard_map/ppermute | solution.py:545
  43.5 1.3 %collective-permute-start.13 = (f32[2,8,1024]{2,1,0:T(8,128)S(1)}, f32[2,8,1024]{2,1,0:T(8,128)S(1)}, u32[]{:S(2)}, u32[]{:S(2)}) collective-permute-start(f32[2,8,1024]{2,1,0:T(8,128)S(1)} %shard_map.86.mine), channel_id=1, source_target_pairs={{0,1},{1,0},{2,3},{3,2},{4,5},{5,4},{6,7},{7,6},{8,9},{9,8},{10,11... | collective-permute-start | bytes 196616 | tf_op jit(solution)/shard_map/ppermute | solution.py:545

commit v7 on v6

--- a/solution.py
+++ b/solution.py
@@ -38,14 +38,50 @@
     return east, north
 
 
-def fine_step(s, e, n, face_x, face_y):
-    slope_x = [roll(v, -1, 1) - v for v in s]
-    slope_y = [s[1] - s[0], roll(s[0], -1, 0) - s[1]]
-    e = [v + f * d for v, f, d in zip(e, face_x, slope_x)]
-    n = [v + f * d for v, f, d in zip(n, face_y, slope_y)]
-    flow_y = [n[0] - roll(n[1], 1, 0), n[1] - n[0]]
-    s = [v + ((x - roll(x, 1, 1)) + y) for v, x, y in zip(s, e, flow_y)]
-    return s, e, n, slope_x, slope_y
+def fine_step(s, e, n, face_x, face_y, forcing=None, flow=None, sums=None):
+    lane = index_of(s[0][0].shape, 1)
+    count = len(s[0])
+    new_s, new_e, new_n = ([[], []] for _ in range(3))
+    turned = [roll(p[0], -1, 1) for p in s]
+    west = [0.0, 0.0]
+    for v in range(count):
+        here = [p[v] for p in s]
+        ahead = [roll(p[min(v + 1, count - 1)], -1, 1) for p in s]
+        slope_x = [jnp.where(lane < LANES - 1, t, a) - h for t, a, h in zip(turned, ahead, here)]
+        slope_y = [here[1] - here[0], roll(here[0], -1, 0) - here[1]]
+        turned = ahead
+        east = [e[p][v] + face_x[p][v] * slope_x[p] for p in range(2)]
+        north = [n[p][v] + face_y[p][v] * slope_y[p] for p in range(2)]
+        flow_y = [north[0] - roll(north[1], 1, 0), north[1] - north[0]]
+        back = [roll(x, 1, 1) for x in east]
+        for p in range(2):
+            value = here[p] + ((east[p] - jnp.where(lane > 0, back[p], west[p])) + flow_y[p])
+            if forcing is not None:
+                value = value + forcing(p, v)
+            new_s[p].append(value)
+            new_e[p].append(east[p])
+            new_n[p].append(north[p])
+            if flow is not None:
+                for k, slope in enumerate((slope_x, slope_y)):
+                    term = slope[p] * flow(k, p, v)
+                    if len(sums[k][p]) > v:
+                        sums[k][p][v] = sums[k][p][v] + term
+                    else:
+                        sums[k][p].append(term)
+        west = back
+    return new_s, new_e, new_n
+
+
+def cut(*pairs):
+    return [[[v[:, c : c + LANES] for c in range(0, v.shape[1], LANES)] for v in pair] for pair in pairs]
+
+
+def glued(*pairs):
+    return [[jnp.concatenate(blocks, axis=1) for blocks in pair] for pair in pairs]
+
+
+def block_of(ref, *at, parity):
+    return ref[(*at, pl.ds(parity, ref.shape[-2] // 2, stride=2), slice(None))]
 
 
 def inside_x(pair):
@@ -59,13 +95,13 @@
     return [pair[0], jnp.where(index_of(pair[1].shape, 0) < rows - 1, pair[1], 0.0)]
 
 
-def rows_of(ref, *at, first=0, blocks=None):
+def rows_of(ref, *at):
     half = ref.shape[-2] // 2
     return [
         jnp.concatenate(
             [
-                ref[(*at, first + v, pl.ds(parity, half, stride=2), slice(None))]
-                for v in range(blocks or ref.shape[-3])
+                ref[(*at, v, pl.ds(parity, half, stride=2), slice(None))]
+                for v in range(ref.shape[-3])
             ],
             axis=1,
         )
@@ -264,20 +300,24 @@
     e0 = [v * COURANT for v in rows_of(stage_i, 1)]
     n0 = [v * COURANT for v in rows_of(stage_i, 2)]
     e_in, n_in = inside_x(e0), inside_y(n0)
-    s, e, n = s0, e_in, n_in
+    faces_x, faces_y = cut(face_x, face_y)
+    s, e, n = cut(s0, e_in, n_in)
     for _ in range(steps):
-        s, e, n, _, _ = fine_step(s, e, n, face_x, face_y)
+        s, e, n = fine_step(s, e, n, faces_x, faces_y)
+    s, e, n = glued(s, e, n)
     e = [v + (x - y) for v, x, y in zip(e, e0, e_in)]
     n = [v + (x - y) for v, x, y in zip(n, n0, n_in)]
     relaxed = [s, e, n]
 
     wait_all(stage_f, sems.at[3])
     s = rows_of(stage_f, steps - 1)
-    e = [jnp.zeros_like(v) for v in s]
-    n = e
+    zero = [jnp.zeros_like(v) for v in s]
+    s, e, n = cut(s, zero, zero)
     for step in reversed(range(steps - 1)):
-        s, e, n, _, _ = fine_step(s, e, n, face_x, face_y)
-        s = [v + f for v, f in zip(s, rows_of(stage_f, step))]
+        s, e, n = fine_step(
+            s, e, n, faces_x, faces_y, forcing=lambda p, v: block_of(stage_f, step, v, parity=p)
+        )
+    s, e, n = glued(s, e, n)
     for pair, start in zip((s, e, n), (s0, e0, n0)):
         relaxed.append([v - x for v, x in zip(pair, start)])
     su, eu, nu, sw, ew, nw, coarse_depth = restrict_pairs(relaxed + [depth])
@@ -426,13 +466,20 @@
     s = [v * there for v in rows_of(stage_i, 0)]
     e = inside_x([v * (there * COURANT) for v in rows_of(stage_i, 1)])
     n = inside_y([v * (there * COURANT) for v in rows_of(stage_i, 2)])
-    sums = [[jnp.zeros_like(v) for v in s] for _ in range(2)]
+    s, e, n, faces_x, faces_y = cut(s, e, n, face_x, face_y)
+    sums = [[[], []], [[], []]]
     for step in reversed(range(steps)):
-        s, e, n, *slopes = fine_step(s, e, n, face_x, face_y)
-        for k in range(2):
-            sums[k] = [a + d * v for a, d, v in zip(sums[k], slopes[k], rows_of(flow, step, k))]
-        if step:
-            s = [v + f for v, f in zip(s, rows_of(stage_f, step))]
+        s, e, n = fine_step(
+            s,
+            e,
+            n,
+            faces_x,
+            faces_y,
+            forcing=lambda p, v: block_of(stage_f, step, v, parity=p),
+            flow=lambda k, p, v: block_of(flow, step, k, v, parity=p),
+            sums=sums,
+        )
+    sums = glued(*sums)
     total = pulled(sums, [planes[4], planes[5]])
     first = lax.rem(device, 2) == 0
     half = mine.shape[2]
@@ -469,20 +516,24 @@
     fields = [jnp.where(first, starts[i], roll(starts[i], -shift, 1)) for i in range(6)]
     fields = [field[:, :window] for field in prolong_columns(fields)]
     face_x, face_y = inside_x([planes[0], planes[1]]), [planes[2], planes[3]]
-    total = None
-    blocks = flow_got.shape[2]
-    start = jnp.where(first, 0, flow.shape[2] - blocks)
-    for k, (velocity, at) in enumerate(((flow, start), (flow_got, 0))):
-        s, e, n = fields[3 * k : 3 * k + 3]
+    sums = [[[], []], [[], []]]
+    start = jnp.where(first, 0, flow.shape[2] - flow_got.shape[2])
+    faces_x, faces_y = cut(face_x, face_y)
+    for i, (velocity, at) in enumerate(((flow, start), (flow_got, 0))):
+        s, e, n = fields[3 * i : 3 * i + 3]
         e, n = e * inverse, n * inverse
-        s, e, n = [s, s], inside_x([e, e]), inside_y([n, n])
+        s, e, n = cut([s, s], inside_x([e, e]), inside_y([n, n]))
         for step in reversed(range(steps)):
-            s, e, n, *slopes = fine_step(s, e, n, face_x, face_y)
-            terms = [[d * v for d, v in zip(slopes[i], rows_of(velocity, step, i, first=at, blocks=blocks))] for i in range(2)]
-            if total is None:
-                total = terms
-            else:
-                total = [[a + b for a, b in zip(*pair)] for pair in zip(total, terms)]
+            s, e, n = fine_step(
+                s,
+                e,
+                n,
+                faces_x,
+                faces_y,
+                flow=lambda k, p, v: block_of(velocity, step, k, at + v, parity=p),
+                sums=sums,
+            )
+    total = glued(*sums)
     total = pulled(total, [planes[4], planes[5]])
     for i in range(2):
         valid = jnp.where(first, total[i][:, :half], total[i][:, window - half :])

time: 45.6 us -> 45.5 us (level)
  transfers between devices with their start and end apart: 14 -> 14, of which waited for: 8 -> 7; matrix products, arithmetic and copies ran while one was open for 0% -> 0% of each run, Pallas kernels for 19% -> 18%
where the time goes in v7:
time: 45.5 us; the launch traced here: 45.3 us
  starting transfers between devices  17.3 us (38%)
  waiting for transfers between devices  15.7 us (35%)
  Pallas kernels  11.6 us (25%)
  between operations  0.74 us (2%)
    pallas_call x11, Pallas kernels, call(): pl.pallas_call(body, out_shape=[jax.ShapeDtypeStruct(shape, jnp.float32)...  11.6 us
    ppermute x10, waiting for transfers between devices, paired(): return lax.ppermute(value, 'tm', [(s, s ^ stride) for s in range(count)])  10.6 us
    ppermute x10, starting transfers between devices, paired(): return lax.ppermute(value, 'tm', [(s, s ^ stride) for s in range(count)])  9.99 us
    ppermute x3, starting transfers between devices, back(): lax.ppermute(value, 'tm', [(s, (s - stride) % count) for s in range(count)])  6 us
    ppermute x3, waiting for transfers between devices, back(): lax.ppermute(value, 'tm', [(s, (s - stride) % count) for s in range(count)])  5.14 us
    ppermute x1, starting transfers between devices, shards(): lax.ppermute(initial, 'tm', [(s, s - 1) for s in range(1, count)])  1.28 us
  transfers between devices with their start and end apart: 14, of which 7 were waited for; matrix products, arithmetic and copies ran while one was open for 0% of the time, Pallas kernels for 18%

profile of v7, /device:TPU:0, one launch (start us, length us, event | category | flops | bytes accessed | tf_op | source)
XLA Modules:
  0.0 45.3 jit_solution(15933181435497370637)
XLA Ops:
  0.6 0.5 %collective-permute-start.7 = (f32[8,2,16,2048]{3,2,1,0:T(8,128)}, f32[8,2,16,2048]{3,2,1,0:T(8,128)S(1)}, u32[]{:S(2)}, u32[]{:S(2)}) collective-permute-start(f32[8,2,16,2048]{3,2,1,0:T(8,128)} %param.7), channel_id=1, source_target_pairs={{0,1},{1,0},{2,3},{3,2},{4,5},{5,4},{6,7},{7,6},{8,9},{9,8},{10,11... | collective-permute-start | bytes 6291464 | tf_op jit(solution)/shard_map/ppermute | solution.py:596
  1.1 1.3 %collective-permute-start.2 = (f32[1,3,16,2048]{3,2,1,0:T(8,128)}, f32[1,3,16,2048]{3,2,1,0:T(8,128)S(1)}, u32[]{:S(2)}, u32[]{:S(2)}) collective-permute-start(f32[1,3,16,2048]{3,2,1,0:T(8,128)} %initial_in.1), channel_id=1, source_target_pairs={{1,0},{2,1},{3,2},{4,3},{5,4},{6,5},{7,6},{8,7},{9,8},{10,9},{11,1... | collective-permute-start | bytes 1179656 | tf_op jit(solution)/shard_map/ppermute | solution.py:608
  2.4 4.3 %shard_map.77 = (f32[6,8,640]{2,1,0:T(8,128)S(1)}, f32[6,8,640]{2,1,0:T(8,128)S(1)}, f32[6,8,2048]{2,1,0:T(8,128)S(1)}, f32[6,8,1152]{2,1,0:T(8,128)S(1)}, f32[2...) custom-call(f32[16]{0:T(128)} %table_in.1, s32[2,16,8,128]{3,2,1,0:T(8,128)} %bitcast.29, ...), custom_call_target="tpu_custom_call" | custom-call | flops 40000000 | bytes 40000000 | tf_op jit(solution)/shard_map/pallas_call | solution.py:568
  6.7 1.2 %collective-permute-start = (f32[6,8,640]{2,1,0:T(8,128)S(1)}, f32[6,8,640]{2,1,0:T(8,128)S(1)}, u32[]{:S(2)}, u32[]{:S(2)}) collective-permute-start(f32[6,8,640]{2,1,0:T(8,128)S(1)} %get-tuple-element.19), channel_id=1, source_target_pairs={{0,1},{1,0},{2,3},{3,2},{4,5},{5,4},{6,7},{7,6},{8,9},{9,8},{10,11... | collective-permute-start | bytes 368648 | tf_op jit(solution)/shard_map/ppermute | solution.py:596
  7.9 1.0 %collective-permute-done.got.refs_4_ = f32[6,8,640]{2,1,0:T(8,128)S(1)} collective-permute-done((f32[6,8,640]{2,1,0:T(8,128)S(1)}, f32[6,8,640]{2,1,0:T(8,128)S(1)}, u32[]{:S(2)}, u32[]{:S(2)}) %collective-permute-start) | collective-permute-done | bytes 122912 | tf_op jit(solution)/shard_map/ppermute | solution.py:596
  8.9 0.1 shard_map.78.order.own.refs_5_
  9.0 2.6 %collective-permute-start.1 = (f32[6,8,640]{2,1,0:T(8,128)S(1)}, f32[6,8,640]{2,1,0:T(8,128)S(1)}, u32[]{:S(2)}, u32[]{:S(2)}) collective-permute-start(f32[6,8,640]{2,1,0:T(8,128)S(1)} %shard_map.78.order.own.refs_5_), channel_id=1, source_target_pairs={{0,2},{1,3},{2,0},{3,1},{4,6},{5,7},{6,4},{7,5},{8,10},{9,11},{10,... | collective-permute-start | bytes 368648 | tf_op jit(solution)/shard_map/ppermute | solution.py:596
  11.6 0.0 collective-permute-done.2
  11.6 1.3 %shard_map.79 = (f32[2,8,1024]{2,1,0:T(8,128)S(1)}, f32[2,8,1024]{2,1,0:T(8,128)S(1)}) custom-call(f32[6,8,640]{2,1,0:T(8,128)S(1)} %shard_map.78.order.own.refs_5_, f32[1,3,2,16,8,128]{5,4,3,2,1,0:T(8,128)S(1)} %bitcast.25, f32[8,16,16,128]{3,2,1,0:T(8,128)S(1)} %get-tuple-element.21.stage_f, f32[8,2,16,16,128]{4,3,2,1,0:T(8,128)S(1)} %get-tuple-element.22.flow, ...), custom_call_target="tpu_custom_call" | custom-call | flops 8000000 | bytes 8000000 | tf_op jit(solution)/shard_map/pallas_call | solution.py:568
  13.0 0.1 collective-permute-start.3
  13.1 2.4 %collective-permute-done.1.got.refs_6_ = f32[6,8,640]{2,1,0:T(8,128)S(1)} collective-permute-done((f32[6,8,640]{2,1,0:T(8,128)S(1)}, f32[6,8,640]{2,1,0:T(8,128)S(1)}, u32[]{:S(2)}, u32[]{:S(2)}) %collective-permute-start.1) | collective-permute-done | bytes 122912 | tf_op jit(solution)/shard_map/ppermute | solution.py:596
  15.5 0.0 collective-permute-done.3.order.grad_got
  15.5 0.2 shard_map.80
  15.7 5.0 %collective-permute-start.4 = (f32[6,8,640]{2,1,0:T(8,128)S(1)}, f32[6,8,640]{2,1,0:T(8,128)S(1)}, u32[]{:S(2)}, u32[]{:S(2)}) collective-permute-start(f32[6,8,640]{2,1,0:T(8,128)S(1)} %get-tuple-element.25), channel_id=1, source_target_pairs={{0,12},{1,13},{2,14},{3,15},{4,0},{5,1},{6,2},{7,3},{8,4},{9,5},{1... | collective-permute-start | bytes 368648 | tf_op jit(solution)/shard_map/ppermute | solution.py:599
  20.7 0.0 collective-permute-start.5
  20.7 1.0 %collective-permute-start.6 = (f32[3,8,640]{2,1,0:T(8,128)S(1)}, f32[3,8,640]{2,1,0:T(8,128)S(1)}, u32[]{:S(2)}, u32[]{:S(2)}) collective-permute-start(f32[3,8,640]{2,1,0:T(8,128)S(1)} %get-tuple-element.26.order), channel_id=1, source_target_pairs={{0,4},{1,5},{2,6},{3,7},{4,8},{5,9},{6,10},{7,11},{8,12},{9,13},{1... | collective-permute-start | bytes 184328 | tf_op jit(solution)/shard_map/ppermute | solution.py:599
  21.7 0.0 collective-permute-done.7
  21.7 0.1 shard_map.81.refs_8_.flow_got
  21.8 5.1 %collective-permute-done.5.refs_1_ = f32[3,8,640]{2,1,0:T(8,128)S(1)} collective-permute-done((f32[3,8,640]{2,1,0:T(8,128)S(1)}, f32[3,8,640]{2,1,0:T(8,128)S(1)}, u32[]{:S(2)}, u32[]{:S(2)}) %collective-permute-start.5) | collective-permute-done | bytes 61472 | tf_op jit(solution)/shard_map/ppermute | solution.py:599
  26.9 0.0 collective-permute-done.6.refs_2_
  26.9 0.0 collective-permute-done.4.refs_0_
  26.9 0.9 %shard_map.82 = (f32[6,8,640]{2,1,0:T(8,128)S(1)}, f32[3,8,512]{2,1,0:T(8,128)S(1)}, f32[3,8,512]{2,1,0:T(8,128)S(1)}) custom-call(f32[6,8,640]{2,1,0:T(8,128)S(1)} %collective-permute-done.4.refs_0_, f32[3,8,640]{2,1,0:T(8,128)S(1)} %collective-permute-done.5.refs_1_, f32[3,8,640]{2,1,0:T(8,128)S(1)} %collective-permute-done.6.refs_2_, ...), custom_call_target="tpu_custom_call" | custom-call | flops 1000 | bytes 1000 | tf_op jit(solution)/shard_map/pallas_call | solution.py:568
  27.9 1.7 %shard_map.83.a = f32[2,8,1024]{2,1,0:T(8,128)S(1)} custom-call(f32[6,8,640]{2,1,0:T(8,128)S(1)} %get-tuple-element.27.starts, f32[8,2,16,16,128]{4,3,2,1,0:T(8,128)S(1)} %get-tuple-element.22.flow, f32[8,2,9,16,128]{4,3,2,1,0:T(8,128)S(1)} %shard_map.81.refs_8_.flow_got, f32[6,8,1152]{2,1,0:T(8,128)S(1)} %get-tuple-element.28.planes, ...), custom_call_target="tpu_custom_call" | custom-call | flops 8000000 | bytes 8000000 | tf_op jit(solution)/shard_map/pallas_call | solution.py:568
  29.5 1.0 %collective-permute-start.8 = (f32[2,8,1024]{2,1,0:T(8,128)S(1)}, f32[2,8,1024]{2,1,0:T(8,128)S(1)}, u32[]{:S(2)}, u32[]{:S(2)}) collective-permute-start(f32[2,8,1024]{2,1,0:T(8,128)S(1)} %shard_map.83.a), channel_id=1, source_target_pairs={{0,2},{1,3},{2,0},{3,1},{4,6},{5,7},{6,4},{7,5},{8,10},{9,11},{10,... | collective-permute-start | bytes 196616 | tf_op jit(solution)/shard_map/ppermute | solution.py:596
  30.5 0.0 collective-permute-start.9
  30.5 1.2 %collective-permute-done.9.order.got = f32[3,8,512]{2,1,0:T(8,128)S(1)} collective-permute-done((f32[3,8,512]{2,1,0:T(8,128)S(1)}, f32[3,8,512]{2,1,0:T(8,128)S(1)}, u32[]{:S(2)}, u32[]{:S(2)}) %collective-permute-start.9) | collective-permute-done | bytes 49184 | tf_op jit(solution)/shard_map/ppermute | solution.py:596
  31.7 2.1 %collective-permute-done.8.b = f32[2,8,1024]{2,1,0:T(8,128)S(1)} collective-permute-done((f32[2,8,1024]{2,1,0:T(8,128)S(1)}, f32[2,8,1024]{2,1,0:T(8,128)S(1)}, u32[]{:S(2)}, u32[]{:S(2)}) %collective-permute-start.8) | collective-permute-done | bytes 65568 | tf_op jit(solution)/shard_map/ppermute | solution.py:596
  33.9 1.0 %collective-permute-start.10 = (f32[2,8,1024]{2,1,0:T(8,128)S(1)}, f32[2,8,1024]{2,1,0:T(8,128)S(1)}, u32[]{:S(2)}, u32[]{:S(2)}) collective-permute-start(f32[2,8,1024]{2,1,0:T(8,128)S(1)} %shard_map.84.order.a), channel_id=1, source_target_pairs={{0,4},{1,5},{2,6},{3,7},{4,0},{5,1},{6,2},{7,3},{8,12},{9,13},{10,... | collective-permute-start | bytes 196616 | tf_op jit(solution)/shard_map/ppermute | solution.py:596
  34.9 2.3 %collective-permute-start.11 = (f32[2,8,1024]{2,1,0:T(8,128)S(1)}, f32[2,8,1024]{2,1,0:T(8,128)S(1)}, u32[]{:S(2)}, u32[]{:S(2)}) collective-permute-start(f32[2,8,1024]{2,1,0:T(8,128)S(1)} %shard_map.84.order.a), channel_id=1, source_target_pairs={{0,8},{1,9},{2,10},{3,11},{4,12},{5,13},{6,14},{7,15},{8,0},{9,1},... | collective-permute-start | bytes 196616 | tf_op jit(solution)/shard_map/ppermute | solution.py:596
  37.2 1.1 %collective-permute-start.12 = (f32[2,8,1024]{2,1,0:T(8,128)S(1)}, f32[2,8,1024]{2,1,0:T(8,128)S(1)}, u32[]{:S(2)}, u32[]{:S(2)}) collective-permute-start(f32[2,8,1024]{2,1,0:T(8,128)S(1)} %shard_map.84.order.a), channel_id=1, source_target_pairs={{0,12},{1,13},{2,14},{3,15},{4,8},{5,9},{6,10},{7,11},{8,4},{9,5},... | collective-permute-start | bytes 196616 | tf_op jit(solution)/shard_map/ppermute | solution.py:596
  38.3 2.3 %shard_map.85 = (f32[1,3,16,2048]{3,2,1,0:T(8,128)}, f32[8,128]{1,0:T(8,128)S(1)}) custom-call(f32[2,8,1024]{2,1,0:T(8,128)S(1)} %shard_map.84.order.a, f32[3,8,512]{2,1,0:T(8,128)S(1)} %get-tuple-element.31.kept, f32[3,8,512]{2,1,0:T(8,128)S(1)} %collective-permute-done.9.order.got, f32[1,3,16,2048]{3,2,1,0:T(8,128)} %initial_in.1), custom_call_target="tpu_custom_call" | custom-call | flops 4000000 | bytes 4000000 | tf_op jit(solution)/shard_map/pallas_call | solution.py:568
  40.6 0.0 collective-permute-done.10.b
  40.6 0.0 collective-permute-done.11.c
  40.7 2.6 %collective-permute-done.12.d = f32[2,8,1024]{2,1,0:T(8,128)S(1)} collective-permute-done((f32[2,8,1024]{2,1,0:T(8,128)S(1)}, f32[2,8,1024]{2,1,0:T(8,128)S(1)}, u32[]{:S(2)}, u32[]{:S(2)}) %collective-permute-start.12) | collective-permute-done | bytes 65568 | tf_op jit(solution)/shard_map/ppermute | solution.py:596
  43.3 0.1 collective-permute-start.13
  43.4 1.2 %collective-permute-done.13.other = f32[2,8,1024]{2,1,0:T(8,128)S(1)} collective-permute-done((f32[2,8,1024]{2,1,0:T(8,128)S(1)}, f32[2,8,1024]{2,1,0:T(8,128)S(1)}, u32[]{:S(2)}, u32[]{:S(2)}) %collective-permute-start.13) | collective-permute-done | bytes 65568 | tf_op jit(solution)/shard_map/ppermute | solution.py:596
  44.6 0.7 %shard_map.87 = f32[2,16,8,128]{3,2,1,0:T(8,128)} custom-call(f32[2,8,1024]{2,1,0:T(8,128)S(1)} %shard_map.86.mine, f32[2,8,1024]{2,1,0:T(8,128)S(1)} %collective-permute-done.13.other), custom_call_target="tpu_custom_call" | custom-call | flops 1000 | bytes 1000 | tf_op jit(solution)/shard_map/pallas_call | solution.py:568
  (2 shorter events, 0.0 us)
Async XLA Ops:
  0.6 21.0 %collective-permute-start.7 = (f32[8,2,16,2048]{3,2,1,0:T(8,128)}, f32[8,2,16,2048]{3,2,1,0:T(8,128)S(1)}, u32[]{:S(2)}, u32[]{:S(2)}) collective-permute-start(f32[8,2,16,2048]{3,2,1,0:T(8,128)} %param.7), channel_id=1, source_target_pairs={{0,1},{1,0},{2,3},{3,2},{4,5},{5,4},{6,7},{7,6},{8,9},{9,8},{10,11... | collective-permute-start | bytes 6291464 | tf_op jit(solution)/shard_map/ppermute | solution.py:596
  1.1 10.5 %collective-permute-start.2 = (f32[1,3,16,2048]{3,2,1,0:T(8,128)}, f32[1,3,16,2048]{3,2,1,0:T(8,128)S(1)}, u32[]{:S(2)}, u32[]{:S(2)}) collective-permute-start(f32[1,3,16,2048]{3,2,1,0:T(8,128)} %initial_in.1), channel_id=1, source_target_pairs={{1,0},{2,1},{3,2},{4,3},{5,4},{6,5},{7,6},{8,7},{9,8},{10,9},{11,1... | collective-permute-start | bytes 1179656 | tf_op jit(solution)/shard_map/ppermute | solution.py:608
  6.7 2.2 %collective-permute-start = (f32[6,8,640]{2,1,0:T(8,128)S(1)}, f32[6,8,640]{2,1,0:T(8,128)S(1)}, u32[]{:S(2)}, u32[]{:S(2)}) collective-permute-start(f32[6,8,640]{2,1,0:T(8,128)S(1)} %get-tuple-element.19), channel_id=1, source_target_pairs={{0,1},{1,0},{2,3},{3,2},{4,5},{5,4},{6,7},{7,6},{8,9},{9,8},{10,11... | collective-permute-start | bytes 368648 | tf_op jit(solution)/shard_map/ppermute | solution.py:596
  9.0 6.5 %collective-permute-start.1 = (f32[6,8,640]{2,1,0:T(8,128)S(1)}, f32[6,8,640]{2,1,0:T(8,128)S(1)}, u32[]{:S(2)}, u32[]{:S(2)}) collective-permute-start(f32[6,8,640]{2,1,0:T(8,128)S(1)} %shard_map.78.order.own.refs_5_), channel_id=1, source_target_pairs={{0,2},{1,3},{2,0},{3,1},{4,6},{5,7},{6,4},{7,5},{8,10},{9,11},{10,... | collective-permute-start | bytes 368648 | tf_op jit(solution)/shard_map/ppermute | solution.py:596
  13.0 2.5 %collective-permute-start.3 = (f32[2,8,1024]{2,1,0:T(8,128)S(1)}, f32[2,8,1024]{2,1,0:T(8,128)S(1)}, u32[]{:S(2)}, u32[]{:S(2)}) collective-permute-start(f32[2,8,1024]{2,1,0:T(8,128)S(1)} %get-tuple-element.24), channel_id=1, source_target_pairs={{0,1},{1,0},{2,3},{3,2},{4,5},{5,4},{6,7},{7,6},{8,9},{9,8},{10,11... | collective-permute-start | bytes 196616 | tf_op jit(solution)/shard_map/ppermute | solution.py:596
  15.7 11.3 %collective-permute-start.4 = (f32[6,8,640]{2,1,0:T(8,128)S(1)}, f32[6,8,640]{2,1,0:T(8,128)S(1)}, u32[]{:S(2)}, u32[]{:S(2)}) collective-permute-start(f32[6,8,640]{2,1,0:T(8,128)S(1)} %get-tuple-element.25), channel_id=1, source_target_pairs={{0,12},{1,13},{2,14},{3,15},{4,0},{5,1},{6,2},{7,3},{8,4},{9,5},{1... | collective-permute-start | bytes 368648 | tf_op jit(solution)/shard_map/ppermute | solution.py:599
  20.7 6.3 %collective-permute-start.5 = (f32[3,8,640]{2,1,0:T(8,128)S(1)}, f32[3,8,640]{2,1,0:T(8,128)S(1)}, u32[]{:S(2)}, u32[]{:S(2)}) collective-permute-start(f32[3,8,640]{2,1,0:T(8,128)S(1)} %get-tuple-element.26.order), channel_id=1, source_target_pairs={{0,8},{1,9},{2,10},{3,11},{4,12},{5,13},{6,14},{7,15},{8,0},{9,1},... | collective-permute-start | bytes 184328 | tf_op jit(solution)/shard_map/ppermute | solution.py:599
  20.7 6.3 %collective-permute-start.6 = (f32[3,8,640]{2,1,0:T(8,128)S(1)}, f32[3,8,640]{2,1,0:T(8,128)S(1)}, u32[]{:S(2)}, u32[]{:S(2)}) collective-permute-start(f32[3,8,640]{2,1,0:T(8,128)S(1)} %get-tuple-element.26.order), channel_id=1, source_target_pairs={{0,4},{1,5},{2,6},{3,7},{4,8},{5,9},{6,10},{7,11},{8,12},{9,13},{1... | collective-permute-start | bytes 184328 | tf_op jit(solution)/shard_map/ppermute | solution.py:599
  29.5 4.3 %collective-permute-start.8 = (f32[2,8,1024]{2,1,0:T(8,128)S(1)}, f32[2,8,1024]{2,1,0:T(8,128)S(1)}, u32[]{:S(2)}, u32[]{:S(2)}) collective-permute-start(f32[2,8,1024]{2,1,0:T(8,128)S(1)} %shard_map.83.a), channel_id=1, source_target_pairs={{0,2},{1,3},{2,0},{3,1},{4,6},{5,7},{6,4},{7,5},{8,10},{9,11},{10,... | collective-permute-start | bytes 196616 | tf_op jit(solution)/shard_map/ppermute | solution.py:596
  30.5 1.2 %collective-permute-start.9 = (f32[3,8,512]{2,1,0:T(8,128)S(1)}, f32[3,8,512]{2,1,0:T(8,128)S(1)}, u32[]{:S(2)}, u32[]{:S(2)}) collective-permute-start(f32[3,8,512]{2,1,0:T(8,128)S(1)} %get-tuple-element.30), channel_id=1, source_target_pairs={{0,1},{1,0},{2,3},{3,2},{4,5},{5,4},{6,7},{7,6},{8,9},{9,8},{10,11... | collective-permute-start | bytes 147464 | tf_op jit(solution)/shard_map/ppermute | solution.py:596
  33.9 6.7 %collective-permute-start.10 = (f32[2,8,1024]{2,1,0:T(8,128)S(1)}, f32[2,8,1024]{2,1,0:T(8,128)S(1)}, u32[]{:S(2)}, u32[]{:S(2)}) collective-permute-start(f32[2,8,1024]{2,1,0:T(8,128)S(1)} %shard_map.84.order.a), channel_id=1, source_target_pairs={{0,4},{1,5},{2,6},{3,7},{4,0},{5,1},{6,2},{7,3},{8,12},{9,13},{10,... | collective-permute-start | bytes 196616 | tf_op jit(solution)/shard_map/ppermute | solution.py:596
  34.9 5.8 %collective-permute-start.11 = (f32[2,8,1024]{2,1,0:T(8,128)S(1)}, f32[2,8,1024]{2,1,0:T(8,128)S(1)}, u32[]{:S(2)}, u32[]{:S(2)}) collective-permute-start(f32[2,8,1024]{2,1,0:T(8,128)S(1)} %shard_map.84.order.a), channel_id=1, source_target_pairs={{0,8},{1,9},{2,10},{3,11},{4,12},{5,13},{6,14},{7,15},{8,0},{9,1},... | collective-permute-start | bytes 196616 | tf_op jit(solution)/shard_map/ppermute | solution.py:596
  37.2 6.1 %collective-permute-start.12 = (f32[2,8,1024]{2,1,0:T(8,128)S(1)}, f32[2,8,1024]{2,1,0:T(8,128)S(1)}, u32[]{:S(2)}, u32[]{:S(2)}) collective-permute-start(f32[2,8,1024]{2,1,0:T(8,128)S(1)} %shard_map.84.order.a), channel_id=1, source_target_pairs={{0,12},{1,13},{2,14},{3,15},{4,8},{5,9},{6,10},{7,11},{8,4},{9,5},... | collective-permute-start | bytes 196616 | tf_op jit(solution)/shard_map/ppermute | solution.py:596
  43.3 1.3 %collective-permute-start.13 = (f32[2,8,1024]{2,1,0:T(8,128)S(1)}, f32[2,8,1024]{2,1,0:T(8,128)S(1)}, u32[]{:S(2)}, u32[]{:S(2)}) collective-permute-start(f32[2,8,1024]{2,1,0:T(8,128)S(1)} %shard_map.86.mine), channel_id=1, source_target_pairs={{0,1},{1,0},{2,3},{3,2},{4,5},{5,4},{6,7},{7,6},{8,9},{9,8},{10,11... | collective-permute-start | bytes 196616 | tf_op jit(solution)/shard_map/ppermute | solution.py:596
